TPU v7x, 512 devices: a whole 4x4x16 slice. The times are simulated.
512 devices in a mesh: dp: 64 (over z, y), seq: 8 (over x, core).
Axes of the slice: x: 4, y: 4, z: 16, core: 2. Of those that a mesh axis runs over, the one named last changes fastest.
Arguments:
- token_rows: bfloat16 [65536, 4096], P(('dp', 'seq')), may hold values from -16 to 16
- extra_len: int32 [64, 16], P('dp'), may hold values from 1 to 497, 784 in all within a row
- queries: bfloat16 [1024, 4096], P(('dp', 'seq')), may hold values from -8 to 8
- positive: int32 [1024], replicated, may hold values from 0 to 1023
Outputs:
- grad_rows: bfloat16 [65536, 4096], P(('dp', 'seq'))
Inputs may be any that keep to these rules, and one draw needn't show every extreme that they name: `extra_len`: each group's entries sum to 784, and in every group one passage has 512 tokens.
All inputs are finite; a program needn't handle non-finite values.
Results may differ from a plain program's by a relative error of at most 0.0053.
Values may be sent and summed in bfloat16 or wider, within the bound.
No kernel may reach another device: no remote copies, remote signals or barrier semaphores. Data moves between devices by JAX's collectives and lax.ppermute only.
A program may use at most 64 MiB of HBM per device.

v0:
```python
import jax
import jax.numpy as jnp
from jax import lax
from jax.sharding import PartitionSpec as P

loss_scale = 1048576.0
inv_temp = 20.0


def per_device(token_rows, extra_len, queries, positive):
    row_count = token_rows.shape[0]
    pass_count = extra_len.shape[1]
    seq_count = lax.axis_size("seq")
    seq_index = lax.axis_index("seq")
    dp_index = lax.axis_index("dp")
    lengths = extra_len[0] + 15
    end_rows = jnp.cumsum(lengths)
    first_rows = end_rows - lengths
    shard_low = seq_index * row_count
    row_pos = shard_low + jnp.arange(row_count, dtype=jnp.int32)
    slot_count = pass_count // seq_count
    member = (
        (row_pos[None, :] >= first_rows[:, None]) & (row_pos[None, :] < end_rows[:, None])
    ).astype(jnp.bfloat16)
    member_block = member
    owned_sums = lax.psum_scatter(
        jnp.dot(member_block, token_rows, preferred_element_type=jnp.float32),
        "seq",
        scatter_dimension=0,
        tiled=True,
    )
    slot_len = lax.dynamic_slice_in_dim(lengths, seq_index * slot_count, slot_count, 0).astype(
        jnp.float32
    )
    slot_ids = (
        dp_index * pass_count + seq_index * slot_count + jnp.arange(slot_count, dtype=jnp.int32)
    )
    slot_live = jnp.ones((slot_count,), jnp.bool_)
    pooled = owned_sums / slot_len[:, None]
    inv_norm = lax.rsqrt(jnp.sum(pooled * pooled, axis=-1, keepdims=True) + 1e-06)
    embedding = pooled * inv_norm
    embed_half = embedding.astype(jnp.bfloat16)
    query_float = queries.astype(jnp.float32)
    query_norm = (
        query_float * lax.rsqrt(jnp.sum(query_float * query_float, axis=-1, keepdims=True) + 1e-06)
    ).astype(jnp.bfloat16)
    factor = loss_scale * inv_temp / positive.shape[0]
    every_query = lax.all_gather(query_norm, ("dp", "seq"), axis=0, tiled=True)
    scores = jnp.dot(every_query, embed_half.T, preferred_element_type=jnp.float32) * inv_temp
    exp_scores = jnp.exp(scores) * slot_live.astype(jnp.float32)[None, :]
    totals = lax.psum(jnp.sum(exp_scores, axis=-1), ("dp", "seq"))
    target = (positive[:, None] == slot_ids[None, :]).astype(jnp.float32)
    coefficients = ((exp_scores / totals[:, None] - target) * factor).astype(jnp.bfloat16)
    d_embed = jnp.dot(coefficients.T, every_query, preferred_element_type=jnp.float32)
    d_pooled = inv_norm * (
        d_embed - embedding * jnp.sum(embedding * d_embed, axis=-1, keepdims=True)
    )
    d_sum = (d_pooled / slot_len[:, None]).astype(jnp.bfloat16)
    member_block = member
    grads = lax.dot_general(
        member_block,
        lax.all_gather(d_sum, "seq", axis=0, tiled=True),
        (((0,), (0,)), ((), ())),
        preferred_element_type=jnp.float32,
    )
    return grads.astype(jnp.bfloat16)


def solution(mesh):
    return jax.shard_map(
        per_device,
        mesh=mesh,
        in_specs=(P(("dp", "seq"), None), P("dp", None), P(("dp", "seq"), None), P()),
        out_specs=P(("dp", "seq"), None),
        check_vma=False,
    )
```

profile of v0, /device:TPU:1, one launch (start us, length us, event | category | flops | bytes accessed | tf_op | source)
XLA Modules:
  0.0 380.8 jit_solution(16040950349150287580)
XLA Ops:
  7.4 0.7 fusion.22
  8.1 0.1 copy.7
  8.2 0.1 reduce
  8.4 0.7 bitcast_subtract_fusion
  9.0 1.0 fusion.8
  10.0 0.0 all-reduce.3.cloned.1.call-update
  10.1 0.0 all-gather.4.cloned.1.call-start
  10.1 0.9 fusion.1
  11.0 1.4 fusion.4
  12.4 0.0 all-gather.4.cloned.1.call-update
  12.4 1.3 dynamic-slice.1
  14.3 0.1 convert_bitcast_fusion
  14.3 76.0 %all-reduce.3.cloned.1.call-done = f32[16,4096]{1,0:T(8,128)} async-done(((f32[16,4096]{1,0:T(8,128)}), f32[16,4096]{1,0:T(8,128)}) %all-reduce.3.cloned.1.call-update) | async-done | bytes 262160
  90.3 1.1 multiply_reduce_fusion.1
  91.4 142.6 %all-gather.4.cloned.1.call-done = bf16[512,2,4096]{2,1,0:T(2,128)(2,1)} async-done(((bf16[1,2,4096]{2,1,0:T(2,128)(2,1)}), bf16[512,2,4096]{2,1,0:T(2,128)(2,1)}) %all-gather.4.cloned.1.call-update) | async-done | bytes 8388624 | tf_op jit(solution)/shard_map/all_gather | solution.py:48
  234.1 13.1 %reshape.61 = bf16[1024,4096]{1,0:T(8,128)(2,1)} reshape(bf16[512,2,4096]{2,1,0:T(2,128)(2,1)} %all-gather.4.cloned.1.call-done) | data formatting | bytes 16777216
  247.2 5.7 %fusion.23 = (f32[1024]{0:T(1024)S(1)}, f32[1024,2]{0,1:T(2,128)S(1)}) fusion(bf16[1024,4096]{1,0:T(8,128)(2,1)} %reshape.61, f32[2,4096]{1,0:T(2,128)S(1)} %get-tuple-element.6, f32[2]{0:T(128)S(1)} %add_rsqrt_fusion.1), kind=kOutput, calls=%fused_computation.41 | convolution fusion | flops 16796672 | bytes 8433672 | tf_op jit(solution)/shard_map/dot_general | solution.py:49
  252.8 100.8 %psum.7 = f32[1024]{0:T(1024)S(1)} all-reduce(f32[1024]{0:T(1024)S(1)} %get-tuple-element.9), channel_id=1, replica_groups=mesh['dp'=64,'seq'=8] {'dp','seq'}, use_global_device_ids=true, to_apply=%region_5.6 | all-reduce | flops 1024 | bytes 8192 | tf_op jit(solution)/shard_map/psum | solution.py:51
  353.7 0.0 copy-done.1
  353.7 4.7 %multiply_reduce_fusion = (f32[2]{0:T(128)S(1)}, f32[2,4096]{1,0:T(2,128)S(1)}) fusion(f32[2,4096]{1,0:T(2,128)S(1)} %get-tuple-element.6, f32[2]{0:T(128)S(1)} %add_rsqrt_fusion.1, bf16[1024,4096]{1,0:T(8,128)(2,1)} %reshape.61, f32[1024,2]{0,1:T(2,128)S(1)} %get-tuple-element.10, s32[1024]{0:T(1024)S(1)} %copy-done.1, f32[1024]{0:T(1024)S(1)} %psum.7, ...), kind=kOutput, calls=%fused_computation.9 | convolution fusion | flops 16814078 | bytes 8470552 | tf_op jit(solution)/shard_map/dot_general | solution.py:54
  358.4 0.1 fusion.5
  358.5 13.3 %all-gather.1 = bf16[8,2,4096]{2,1,0:T(2,128)(2,1)S(1)} all-gather(bf16[1,2,4096]{2,1,0:T(2,128)(2,1)S(1)} %fusion.5), channel_id=1, replica_groups=mesh['dp'=64,'seq'=8] {'seq'}, dimensions={0}, use_global_device_ids=true | all-gather | bytes 147456 | tf_op jit(solution)/shard_map/all_gather | solution.py:62
  371.8 0.1 reshape.63
  371.9 1.5 convolution_convert_fusion
  (9 shorter events, 0.1 us)
Async XLA Ops:
  7.4 1.7 copy-start
  7.4 82.9 %all-reduce.3.cloned.1.call-start = ((), (), s32[]{:S(2)}) async-start(), calls=%async_computation.1 | async-start | bytes 524288
  10.1 224.0 %all-gather.4.cloned.1.call-start = ((), (), s32[]{:S(2)}) async-start(), calls=%async_computation | async-start | bytes 8404992 | tf_op jit(solution)/shard_map/all_gather | solution.py:48
  247.2 106.5 %copy-start.1 = (s32[1024]{0:T(1024)S(1)}, s32[1024]{0:T(1024)}, u32[]{:S(2)}) copy-start(s32[1024]{0:T(1024)} %param.7) | copy-start | bytes 12292
Sparse Core Ops, SparseCore 0:
  10.5 79.7 all-reduce.2
Sparse Core Ops, SparseCore 1:
  16.0 218.0 all-gather.3
where the time goes:
time: 382 us; the launch traced here: 381 us
  waiting for transfers between devices  219 us (57%)
  blocking collectives  114 us (30%)
  between operations  15.5 us (4%)
  local copies, waits for them, and re-layouts  14.5 us (4%)
  matrix products  12.9 us (3%)
  other arithmetic  5.15 us (1%)
    all_gather x1, waiting for transfers between devices, per_device(): every_query = lax.all_gather(query_norm, ('dp', 'seq'), axis=0, tiled=True)  143 us
    psum x1, blocking collectives, per_device(): totals = lax.psum(jnp.sum(exp_scores, axis=-1), ('dp', 'seq'))  101 us
    unnamed x3, waiting for transfers between devices  76 us
    unnamed x7, local copies, waits for them, and re-layouts  14.4 us
    all_gather x1, blocking collectives, per_device(): lax.all_gather(d_sum, 'seq', axis=0, tiled=True)  13.3 us
  transfers between devices with their start and end apart: 2, of which 2 were waited for; matrix products, arithmetic and copies ran while one was open for 1% of the time, Pallas kernels for 0%

commit v1 on v0

v1 whole, which is shorter than its diff:
```python
import jax
import jax.numpy as jnp
from jax import lax
from jax.sharding import PartitionSpec as P

loss_scale = 1048576.0
inv_temp = 20.0
Z, Y, S = 16, 4, 8
Y_GROUPS = [[z * Y + y for y in range(Y)] for z in range(Z)]
Z_GROUPS = [[z * Y + y for z in range(Z)] for y in range(Y)]


def share(block, axis, count, groups=None):
    copies = jnp.broadcast_to(block[None], (count,) + block.shape)
    return lax.all_to_all(copies, axis, 0, 0, axis_index_groups=groups)


def per_device(token_rows, extra_len, queries, positive):
    row_count, width = token_rows.shape
    pass_count = extra_len.shape[1]
    seq_index = lax.axis_index("seq")
    dp_index = lax.axis_index("dp")

    query_float = queries.astype(jnp.float32)
    query_norm = (
        query_float * lax.rsqrt(jnp.sum(query_float * query_float, axis=-1, keepdims=True) + 1e-06)
    ).astype(jnp.bfloat16)
    own = queries.shape[0]
    along_z = share(query_norm, "dp", Z, Z_GROUPS).reshape(Z * own, width)
    some_queries = share(along_z, "dp", Y, Y_GROUPS).reshape(Y * Z * own, width)
    some_positive = lax.dynamic_index_in_dim(
        positive.reshape(Z, Y, S, own), seq_index, 2, keepdims=False
    )
    some_positive = some_positive.transpose(1, 0, 2).reshape(-1)

    lengths = extra_len[0] + 15
    upto = jnp.tril(jnp.ones((pass_count, pass_count), jnp.int32))
    end_rows = jnp.sum(upto * lengths[None, :], axis=1)
    first_rows = end_rows - lengths
    row_pos = seq_index * row_count + jnp.arange(row_count, dtype=jnp.int32)
    member = (
        (row_pos[None, :] >= first_rows[:, None]) & (row_pos[None, :] < end_rows[:, None])
    ).astype(jnp.bfloat16)
    partial = jnp.dot(member, token_rows, preferred_element_type=jnp.float32).astype(jnp.bfloat16)
    sums = jnp.sum(share(partial, "seq", S).astype(jnp.float32), axis=0)
    float_len = lengths.astype(jnp.float32)[:, None]
    pooled = sums / float_len
    inv_norm = lax.rsqrt(jnp.sum(pooled * pooled, axis=-1, keepdims=True) + 1e-06)
    embedding = pooled * inv_norm
    embed_half = embedding.astype(jnp.bfloat16)

    scores = (
        lax.dot_general(
            embed_half, some_queries, (((1,), (1,)), ((), ())), preferred_element_type=jnp.float32
        )
        * inv_temp
    )
    exp_scores = jnp.exp(scores)
    part_totals = jnp.sum(exp_scores, axis=0, keepdims=True)
    part_totals = jnp.sum(share(part_totals, "dp", Y, Y_GROUPS), axis=0)
    totals = jnp.sum(share(part_totals, "dp", Z, Z_GROUPS), axis=0)
    pass_ids = dp_index * pass_count + jnp.arange(pass_count, dtype=jnp.int32)
    target = (pass_ids[:, None] == some_positive[None, :]).astype(jnp.float32)
    factor = loss_scale * inv_temp / positive.shape[0]
    coefficients = ((exp_scores / totals - target) * factor).astype(jnp.bfloat16)

    d_partial = jnp.dot(coefficients, some_queries, preferred_element_type=jnp.float32)
    d_embed = jnp.sum(share(d_partial.astype(jnp.bfloat16), "seq", S).astype(jnp.float32), axis=0)
    d_pooled = inv_norm * (
        d_embed - embedding * jnp.sum(embedding * d_embed, axis=-1, keepdims=True)
    )
    d_sum = (d_pooled / float_len).astype(jnp.bfloat16)
    grads = lax.dot_general(
        member, d_sum, (((0,), (0,)), ((), ())), preferred_element_type=jnp.float32
    )
    return grads.astype(jnp.bfloat16)


def solution(mesh):
    return jax.shard_map(
        per_device,
        mesh=mesh,
        in_specs=(P(("dp", "seq"), None), P("dp", None), P(("dp", "seq"), None), P()),
        out_specs=P(("dp", "seq"), None),
        check_vma=False,
    )
```

time: 382 us -> 128 us (0.34)
  waiting for transfers between devices: 219 us -> 53 us
  blocking collectives: 114 us -> 22.1 us
  starting transfers between devices: 0.05 us -> 39.3 us
  between operations: 15.5 us -> 0.09 us
  matrix products: 12.9 us -> 2.56 us
  local copies, waits for them, and re-layouts: 14.5 us -> 6.7 us
    all_gather x1 -> x0, waiting for transfers between devices: 143 us -> none  [per_device(): every_query = lax.all_gather(query_norm, ('dp', 'seq'), axis=0, tiled=True)]
    psum x1 -> x0, blocking collectives: 101 us -> none  [per_device(): totals = lax.psum(jnp.sum(exp_scores, axis=-1), ('dp', 'seq'))]
    unnamed x3 -> x0, waiting for transfers between devices: 76 us -> none
    all_to_all x0 -> x5, waiting for transfers between devices: none -> 53 us  [share(): return lax.all_to_all(copies, axis, 0, 0, axis_index_groups=groups)]
    all_to_all x0 -> x5, starting transfers between devices: none -> 39.3 us  [share(): return lax.all_to_all(copies, axis, 0, 0, axis_index_groups=groups)]
    all_to_all x0 -> x1, blocking collectives: none -> 22.1 us  [share(): return lax.all_to_all(copies, axis, 0, 0, axis_index_groups=groups)]
    unnamed x7 -> x4, local copies, waits for them, and re-layouts: 14.4 us -> 0.01 us
    all_gather x1 -> x0, blocking collectives: 13.3 us -> none  [per_device(): lax.all_gather(d_sum, 'seq', axis=0, tiled=True)]
  transfers between devices with their start and end apart: 2 -> 5, of which waited for: 2 -> 5; matrix products, arithmetic and copies ran while one was open for 1% -> 3% of each run, Pallas kernels for 0% -> 0%
where the time goes in v1:
time: 128 us
  waiting for transfers between devices  53 us (41%)
  starting transfers between devices  39.3 us (31%)
  blocking collectives  22.1 us (17%)
  local copies, waits for them, and re-layouts  6.7 us (5%)
  other arithmetic  3.98 us (3%)
  matrix products  2.56 us (2%)
    all_to_all x5, waiting for transfers between devices, share(): return lax.all_to_all(copies, axis, 0, 0, axis_index_groups=groups)  53 us
    all_to_all x5, starting transfers between devices, share(): return lax.all_to_all(copies, axis, 0, 0, axis_index_groups=groups)  39.3 us
    all_to_all x1, blocking collectives, share(): return lax.all_to_all(copies, axis, 0, 0, axis_index_groups=groups)  22.1 us
    broadcast_in_dim x7, local copies, waits for them, and re-layouts, share(): copies = jnp.broadcast_to(block[None], (count,) + block.shape)  4.46 us
  transfers between devices with their start and end apart: 5, of which 5 were waited for; matrix products, arithmetic and copies ran while one was open for 3% of the time, Pallas kernels for 0%

profile of v1, /device:TPU:1, one launch (start us, length us, event | category | flops | bytes accessed | tf_op | source)
XLA Modules:
  0.0 127.7 jit_solution(12694303642448705035)
XLA Ops:
  0.0 1.0 fusion.5
  1.0 0.8 fusion.6
  1.8 0.9 broadcast_in_dim.23
  2.7 15.7 %all-to-all-start.1 = ((bf16[16,2,4096]{2,1,0:T(2,128)(2,1)}), bf16[16,2,4096]{2,1,0:T(2,128)(2,1)S(1)}, u32[]{:S(2)}, u32[]{:S(2)}) async-start(bf16[16,2,4096]{2,1,0:T(2,128)(2,1)} %broadcast_in_dim.23), calls=%async_computation.1 | async-start | bytes 524288 | tf_op jit(solution)/shard_map/all_to_all | solution.py:15
  18.4 0.7 fusion.18
  19.2 0.7 fusion.19
  20.2 11.4 %all-to-all-done.1 = bf16[16,2,4096]{2,1,0:T(2,128)(2,1)S(1)} async-done(((bf16[16,2,4096]{2,1,0:T(2,128)(2,1)}), bf16[16,2,4096]{2,1,0:T(2,128)(2,1)S(1)}, u32[]{:S(2)}, u32[]{:S(2)}) %all-to-all-start.1) | async-done | bytes 262176 | tf_op jit(solution)/shard_map/all_to_all | solution.py:15
  31.6 1.1 broadcast_in_dim.22
  32.6 10.5 %all-to-all-start = ((bf16[8,16,4096]{2,1,0:T(8,128)(2,1)}), bf16[8,16,4096]{2,1,0:T(8,128)(2,1)S(1)}, u32[]{:S(2)}, u32[]{:S(2)}) async-start(bf16[8,16,4096]{2,1,0:T(8,128)(2,1)} %broadcast_in_dim.22), calls=%async_computation | async-start | bytes 2097152 | tf_op jit(solution)/shard_map/all_to_all | solution.py:15
  43.2 15.0 %all-to-all-done = bf16[8,16,4096]{2,1,0:T(8,128)(2,1)S(1)} async-done(((bf16[8,16,4096]{2,1,0:T(8,128)(2,1)}), bf16[8,16,4096]{2,1,0:T(8,128)(2,1)S(1)}, u32[]{:S(2)}, u32[]{:S(2)}) %all-to-all-start) | async-done | bytes 1048608 | tf_op jit(solution)/shard_map/all_to_all | solution.py:15
  58.2 1.1 broadcast_in_dim.25
  59.3 4.3 %all-to-all-start.2 = ((bf16[4,32,4096]{2,1,0:T(8,128)(2,1)}), bf16[4,32,4096]{2,1,0:T(8,128)(2,1)S(1)}, u32[]{:S(2)}, u32[]{:S(2)}) async-start(bf16[4,32,4096]{2,1,0:T(8,128)(2,1)} %broadcast_in_dim.25), calls=%async_computation.2 | async-start | bytes 2097152 | tf_op jit(solution)/shard_map/all_to_all | solution.py:15
  63.6 0.9 reshape.58
  64.9 12.7 %all-to-all-done.2 = bf16[4,32,4096]{2,1,0:T(8,128)(2,1)S(1)} async-done(((bf16[4,32,4096]{2,1,0:T(8,128)(2,1)}), bf16[4,32,4096]{2,1,0:T(8,128)(2,1)S(1)}, u32[]{:S(2)}, u32[]{:S(2)}) %all-to-all-start.2) | async-done | bytes 1048608 | tf_op jit(solution)/shard_map/all_to_all | solution.py:15
  77.6 0.4 fusion.20
  78.0 0.6 broadcast_in_dim.26
  78.6 3.2 %all-to-all-start.3 = ((f32[4,1,128]{2,1,0:T(1,128)}), f32[4,1,128]{2,1,0:T(1,128)S(1)}, u32[]{:S(2)}, u32[]{:S(2)}) async-start(f32[4,1,128]{2,1,0:T(1,128)} %broadcast_in_dim.26), calls=%async_computation.3 | async-start | bytes 4096 | tf_op jit(solution)/shard_map/all_to_all | solution.py:15
  81.9 1.0 constant_dynamic-slice_fusion
  82.8 3.0 %all-to-all-done.3 = f32[4,1,128]{2,1,0:T(1,128)S(1)} async-done(((f32[4,1,128]{2,1,0:T(1,128)}), f32[4,1,128]{2,1,0:T(1,128)S(1)}, u32[]{:S(2)}, u32[]{:S(2)}) %all-to-all-start.3) | async-done | bytes 2080 | tf_op jit(solution)/shard_map/all_to_all | solution.py:15
  85.9 0.6 broadcast_in_dim.27
  86.5 5.5 %all-to-all-start.4 = ((f32[16,1,128]{2,1,0:T(1,128)}), f32[16,1,128]{2,1,0:T(1,128)S(1)}, u32[]{:S(2)}, u32[]{:S(2)}) async-start(f32[16,1,128]{2,1,0:T(1,128)} %broadcast_in_dim.27), calls=%async_computation.4 | async-start | bytes 16384 | tf_op jit(solution)/shard_map/all_to_all | solution.py:15
  92.4 10.9 %all-to-all-done.4 = f32[16,1,128]{2,1,0:T(1,128)S(1)} async-done(((f32[16,1,128]{2,1,0:T(1,128)}), f32[16,1,128]{2,1,0:T(1,128)S(1)}, u32[]{:S(2)}, u32[]{:S(2)}) %all-to-all-start.4) | async-done | bytes 8224 | tf_op jit(solution)/shard_map/all_to_all | solution.py:15
  103.7 22.1 %all_to_all.30 = bf16[8,16,4096]{2,1,0:T(8,128)(2,1)S(1)} all-to-all(bf16[8,16,4096]{2,1,0:T(8,128)(2,1)S(1)} %broadcast_in_dim.28), channel_id=1, replica_groups=mesh['dp'=64,'seq'=8] {'seq'}, dimensions={0} | all-to-all | bytes 2097152 | tf_op jit(solution)/shard_map/all_to_all | solution.py:15
  126.2 1.5 %convolution_convert_fusion = bf16[128,4096]{1,0:T(8,128)(2,1)} fusion(f32[16,4096]{1,0:T(8,128)S(1)} %convert_reduce_fusion, f32[16]{0:T(128)S(1)} %multiply_reduce_fusion, f32[16]{0:T(128)S(1)} %add_rsqrt_fusion.1, f32[16]{0:T(128)S(1)} %get-tuple-element.5, s32[128]{0:T(128)S(1)} %iota_add_fusion.1, s32[16]{0:T(128)S(1)} %multiply_reduce_fusion.2, ...), kind=kOutput, calls=%fused_computation | convolution fusion | flops 17766400 | bytes 1573696 | tf_op jit(solution)/shard_map/dot_general | solution.py:73
  (22 shorter events, 2.1 us)
Async XLA Ops:
  0.0 19.9 %copy-start = (bf16[128,4096]{1,0:T(8,128)(2,1)S(1)}, bf16[128,4096]{1,0:T(8,128)(2,1)}, u32[]{:S(2)}) copy-start(bf16[128,4096]{1,0:T(8,128)(2,1)} %param.4) | copy-start | bytes 3145732
  2.7 28.9 %all-to-all-start.1 = ((bf16[16,2,4096]{2,1,0:T(2,128)(2,1)}), bf16[16,2,4096]{2,1,0:T(2,128)(2,1)S(1)}, u32[]{:S(2)}, u32[]{:S(2)}) async-start(bf16[16,2,4096]{2,1,0:T(2,128)(2,1)} %broadcast_in_dim.23), calls=%async_computation.1 | async-start | bytes 524288 | tf_op jit(solution)/shard_map/all_to_all | solution.py:15
  32.6 25.6 %all-to-all-start = ((bf16[8,16,4096]{2,1,0:T(8,128)(2,1)}), bf16[8,16,4096]{2,1,0:T(8,128)(2,1)S(1)}, u32[]{:S(2)}, u32[]{:S(2)}) async-start(bf16[8,16,4096]{2,1,0:T(8,128)(2,1)} %broadcast_in_dim.22), calls=%async_computation | async-start | bytes 2097152 | tf_op jit(solution)/shard_map/all_to_all | solution.py:15
  59.3 4.3 %copy-start.1 = (s32[1024]{0:T(1024)S(1)}, s32[1024]{0:T(1024)}, u32[]{:S(2)}) copy-start(s32[1024]{0:T(1024)} %param.7) | copy-start | bytes 12292
  59.3 18.3 %all-to-all-start.2 = ((bf16[4,32,4096]{2,1,0:T(8,128)(2,1)}), bf16[4,32,4096]{2,1,0:T(8,128)(2,1)S(1)}, u32[]{:S(2)}, u32[]{:S(2)}) async-start(bf16[4,32,4096]{2,1,0:T(8,128)(2,1)} %broadcast_in_dim.25), calls=%async_computation.2 | async-start | bytes 2097152 | tf_op jit(solution)/shard_map/all_to_all | solution.py:15
  78.6 7.2 %all-to-all-start.3 = ((f32[4,1,128]{2,1,0:T(1,128)}), f32[4,1,128]{2,1,0:T(1,128)S(1)}, u32[]{:S(2)}, u32[]{:S(2)}) async-start(f32[4,1,128]{2,1,0:T(1,128)} %broadcast_in_dim.26), calls=%async_computation.3 | async-start | bytes 4096 | tf_op jit(solution)/shard_map/all_to_all | solution.py:15
  86.5 16.7 %all-to-all-start.4 = ((f32[16,1,128]{2,1,0:T(1,128)}), f32[16,1,128]{2,1,0:T(1,128)S(1)}, u32[]{:S(2)}, u32[]{:S(2)}) async-start(f32[16,1,128]{2,1,0:T(1,128)} %broadcast_in_dim.27), calls=%async_computation.4 | async-start | bytes 16384 | tf_op jit(solution)/shard_map/all_to_all | solution.py:15

commit v2 on v1

v2 whole, which is shorter than its diff:
```python
import jax
import jax.numpy as jnp
from jax import lax
from jax.sharding import PartitionSpec as P

loss_scale = 1048576.0
inv_temp = 20.0
Z, Y, S = 16, 4, 8
Z_GROUPS = [[z * Y + y for z in range(Z)] for y in range(Y)]
PLANES = [[z * Y * S + i for i in range(Y * S)] for z in range(Z)]


def share(block, axis, count, groups=None):
    copies = jnp.broadcast_to(block[None], (count,) + block.shape)
    return lax.all_to_all(copies, axis, 0, 0, axis_index_groups=groups)


def swap_seq(block, mask):
    return lax.ppermute(block, "seq", [(i, i ^ mask) for i in range(S)])


def swap_y(block, mask):
    return lax.ppermute(block, "dp", [(i, i ^ mask) for i in range(Z * Y)])


def per_device(token_rows, extra_len, queries, positive):
    row_count, width = token_rows.shape
    pass_count = extra_len.shape[1]
    own = queries.shape[0]
    seq_index = lax.axis_index("seq")
    dp_index = lax.axis_index("dp")
    z_index, y_index = dp_index // Y, dp_index % Y

    query_float = queries.astype(jnp.float32)
    query_norm = (
        query_float * lax.rsqrt(jnp.sum(query_float * query_float, axis=-1, keepdims=True) + 1e-06)
    ).astype(jnp.bfloat16)
    some_queries = share(query_norm, "dp", Z, Z_GROUPS).reshape(Z * own, width)
    some_positive = lax.dynamic_slice(
        positive.reshape(Z, Y, S, own), (0, y_index, seq_index, 0), (Z, 1, 1, own)
    ).reshape(-1)

    lengths = extra_len[0] + 15
    upto = jnp.tril(jnp.ones((pass_count, pass_count), jnp.int32))
    end_rows = jnp.sum(upto * lengths[None, :], axis=1)
    first_rows = end_rows - lengths
    row_pos = seq_index * row_count + jnp.arange(row_count, dtype=jnp.int32)
    member = (
        (row_pos[None, :] >= first_rows[:, None]) & (row_pos[None, :] < end_rows[:, None])
    ).astype(jnp.bfloat16)
    sums = jnp.dot(member, token_rows, preferred_element_type=jnp.float32)
    for mask in (1, 2, 6):
        sums = sums + swap_seq(sums.astype(jnp.bfloat16), mask).astype(jnp.float32)
    float_len = lengths.astype(jnp.float32)[:, None]
    pooled = sums / float_len
    inv_norm = lax.rsqrt(jnp.sum(pooled * pooled, axis=-1, keepdims=True) + 1e-06)
    embedding = pooled * inv_norm

    near = embedding.astype(jnp.bfloat16)[None]
    near = jnp.concatenate([near, swap_y(near, 1)], axis=0)
    far = swap_y(near, 3)

    def score(blocks):
        return lax.dot_general(
            blocks, some_queries, (((2,), (1,)), ((), ())), preferred_element_type=jnp.float32
        )

    near_scores, far_scores = score(near), score(far)
    by_mask = [near_scores[0], near_scores[1], far_scores[1], far_scores[0]]
    ordered = []
    for y in range(Y):
        mask = y_index ^ y
        picked = by_mask[0]
        for other in range(1, Y):
            picked = jnp.where(mask == other, by_mask[other], picked)
        ordered.append(picked)
    scores = jnp.concatenate(ordered, axis=0) * inv_temp
    exp_scores = jnp.exp(scores)
    part_totals = jnp.sum(exp_scores, axis=0, keepdims=True)
    totals = jnp.sum(share(part_totals, "dp", Z, Z_GROUPS), axis=0)
    pass_ids = z_index * Y * pass_count + jnp.arange(Y * pass_count, dtype=jnp.int32)
    target = (pass_ids[:, None] == some_positive[None, :]).astype(jnp.float32)
    factor = loss_scale * inv_temp / positive.shape[0]
    coefficients = ((exp_scores / totals - target) * factor).astype(jnp.bfloat16)

    slots = pass_count // S
    d_partial = jnp.dot(coefficients, some_queries, preferred_element_type=jnp.float32)
    d_partial = d_partial.astype(jnp.bfloat16).reshape(Y * S, slots, width)
    d_parts = lax.all_to_all(d_partial, ("dp", "seq"), 0, 0, axis_index_groups=PLANES)
    d_embed = jnp.sum(d_parts.astype(jnp.float32), axis=0)
    first = seq_index * slots
    own_embedding = lax.dynamic_slice_in_dim(embedding, first, slots, 0)
    own_norm = lax.dynamic_slice_in_dim(inv_norm, first, slots, 0)
    own_len = lax.dynamic_slice_in_dim(float_len, first, slots, 0)
    d_pooled = own_norm * (
        d_embed - own_embedding * jnp.sum(own_embedding * d_embed, axis=-1, keepdims=True)
    )
    d_sum = (d_pooled / own_len).astype(jnp.bfloat16)
    every_d_sum = share(d_sum, "seq", S).reshape(pass_count, width)
    grads = lax.dot_general(
        member, every_d_sum, (((0,), (0,)), ((), ())), preferred_element_type=jnp.float32
    )
    return grads.astype(jnp.bfloat16)


def solution(mesh):
    return jax.shard_map(
        per_device,
        mesh=mesh,
        in_specs=(P(("dp", "seq"), None), P("dp", None), P(("dp", "seq"), None), P()),
        out_specs=P(("dp", "seq"), None),
        check_vma=False,
    )
```

time: 128 us -> 106 us (0.83)
  waiting for transfers between devices: 53 us -> 34.1 us
  starting transfers between devices: 39.3 us -> 53.7 us
  blocking collectives: 22.1 us -> 8.1 us
  local copies, waits for them, and re-layouts: 6.7 us -> 3.45 us
    all_to_all x5 -> x2, waiting for transfers between devices: 53 us -> 12.4 us  [share(): return lax.all_to_all(copies, axis, 0, 0, axis_index_groups=groups)]
    ppermute x0 -> x5, starting transfers between devices: none -> 20.5 us  [the longest x3 12.6 us: swap_seq(): return lax.ppermute(block, 'seq', [(i, i ^ mask) for i in range(S)])]
    all_to_all x5 -> x2, starting transfers between devices: 39.3 us -> 23.2 us  [share(): return lax.all_to_all(copies, axis, 0, 0, axis_index_groups=groups)]
    all_to_all x1, blocking collectives: 22.1 us -> 8.1 us  [share(): return lax.all_to_all(copies, axis, 0, 0, axis_index_groups=groups)]
    all_to_all x0 -> x1, waiting for transfers between devices: none -> 11.4 us  [per_device(): lax.all_to_all(d_partial, ('dp', 'seq'), 0, 0, axis_index_groups=PLANES)]
    ppermute x0 -> x5, waiting for transfers between devices: none -> 10.3 us  [the longest x3 5.48 us: swap_seq(): return lax.ppermute(block, 'seq', [(i, i ^ mask) for i in range(S)])]
    all_to_all x0 -> x1, starting transfers between devices: none -> 10.1 us  [per_device(): lax.all_to_all(d_partial, ('dp', 'seq'), 0, 0, axis_index_groups=PLANES)]
    broadcast_in_dim x7 -> x3, local copies, waits for them, and re-layouts: 4.46 us -> 1.59 us  [share(): copies = jnp.broadcast_to(block[None], (count,) + block.shape)]
  transfers between devices with their start and end apart: 5 -> 8, of which waited for: 5 -> 7; matrix products, arithmetic and copies ran while one was open for 3% -> 2% of each run, Pallas kernels for 0% -> 0%
where the time goes in v2:
time: 106 us; the launch traced here: 105 us
  starting transfers between devices  53.7 us (51%)
  waiting for transfers between devices  34.1 us (32%)
  blocking collectives  8.1 us (8%)
  local copies, waits for them, and re-layouts  3.45 us (3%)
  other arithmetic  2.96 us (3%)
  matrix products  2.55 us (2%)
    all_to_all x2, starting transfers between devices, share(): return lax.all_to_all(copies, axis, 0, 0, axis_index_groups=groups)  23.2 us
    ppermute x3, starting transfers between devices, swap_seq(): return lax.ppermute(block, 'seq', [(i, i ^ mask) for i in range(S)])  12.6 us
    all_to_all x2, waiting for transfers between devices, share(): return lax.all_to_all(copies, axis, 0, 0, axis_index_groups=groups)  12.4 us
    all_to_all x1, waiting for transfers between devices, per_device(): lax.all_to_all(d_partial, ('dp', 'seq'), 0, 0, axis_index_groups=PLANES)  11.4 us
    all_to_all x1, starting transfers between devices, per_device(): lax.all_to_all(d_partial, ('dp', 'seq'), 0, 0, axis_index_groups=PLANES)  10.1 us
    all_to_all x1, blocking collectives, share(): return lax.all_to_all(copies, axis, 0, 0, axis_index_groups=groups)  8.1 us
    ppermute x2, starting transfers between devices, swap_y(): return lax.ppermute(block, 'dp', [(i, i ^ mask) for i in range(Z * Y)])  7.85 us
    ppermute x3, waiting for transfers between devices, swap_seq(): return lax.ppermute(block, 'seq', [(i, i ^ mask) for i in range(S)])  5.48 us
  transfers between devices with their start and end apart: 8, of which 7 were waited for; matrix products, arithmetic and copies ran while one was open for 2% of the time, Pallas kernels for 0%

profile of v2, /device:TPU:1, one launch (start us, length us, event | category | flops | bytes accessed | tf_op | source)
XLA Modules:
  0.0 105.2 jit_solution(9955288183562412420)
XLA Ops:
  0.0 0.7 add_bitcast_fusion
  0.9 0.7 fusion.23
  1.8 8.8 %collective-permute-start = (bf16[16,4096]{1,0:T(8,128)(2,1)S(1)}, bf16[16,4096]{1,0:T(8,128)(2,1)S(1)}, u32[]{:S(2)}, u32[]{:S(2)}) collective-permute-start(bf16[16,4096]{1,0:T(8,128)(2,1)S(1)} %get-tuple-element.15), channel_id=1, source_target_pairs={{0,1},{1,0},{2,3},{3,2},{4,5},{5,4},{6,7},{7,6},{8,9},{9,8},{10,11... | collective-permute-start | bytes 393224 | tf_op jit(solution)/shard_map/ppermute | solution.py:19
  10.8 0.8 collective-permute-done
  11.6 1.9 %collective-permute-start.1 = (bf16[16,4096]{1,0:T(8,128)(2,1)S(1)}, bf16[16,4096]{1,0:T(8,128)(2,1)S(1)}, u32[]{:S(2)}, u32[]{:S(2)}) collective-permute-start(bf16[16,4096]{1,0:T(8,128)(2,1)S(1)} %fusion), channel_id=1, source_target_pairs={{0,2},{1,3},{2,0},{3,1},{4,6},{5,7},{6,4},{7,5},{8,10},{9,11},{10,... | collective-permute-start | bytes 393224 | tf_op jit(solution)/shard_map/ppermute | solution.py:19
  13.6 4.7 %collective-permute-done.1 = bf16[16,4096]{1,0:T(8,128)(2,1)S(1)} collective-permute-done((bf16[16,4096]{1,0:T(8,128)(2,1)S(1)}, bf16[16,4096]{1,0:T(8,128)(2,1)S(1)}, u32[]{:S(2)}, u32[]{:S(2)}) %collective-permute-start.1) | collective-permute-done | bytes 131104 | tf_op jit(solution)/shard_map/ppermute | solution.py:19
  18.3 1.9 %collective-permute-start.2 = (bf16[16,4096]{1,0:T(8,128)(2,1)S(1)}, bf16[16,4096]{1,0:T(8,128)(2,1)S(1)}, u32[]{:S(2)}, u32[]{:S(2)}) collective-permute-start(bf16[16,4096]{1,0:T(8,128)(2,1)S(1)} %fusion.1), channel_id=1, source_target_pairs={{0,6},{1,7},{2,4},{3,5},{4,2},{5,3},{6,0},{7,1},{8,14},{9,15},{10,... | collective-permute-start | bytes 393224 | tf_op jit(solution)/shard_map/ppermute | solution.py:19
  20.3 0.9 broadcast_in_dim.17
  21.2 12.0 %all-to-all-start = ((bf16[16,2,4096]{2,1,0:T(2,128)(2,1)}), bf16[16,2,4096]{2,1,0:T(2,128)(2,1)S(1)}, u32[]{:S(2)}, u32[]{:S(2)}) async-start(bf16[16,2,4096]{2,1,0:T(2,128)(2,1)} %broadcast_in_dim.17), calls=%async_computation | async-start | bytes 524288 | tf_op jit(solution)/shard_map/all_to_all | solution.py:15
  33.6 3.2 %collective-permute-start.3 = (bf16[1,16,4096]{2,1,0:T(8,128)(2,1)S(1)}, bf16[1,16,4096]{2,1,0:T(8,128)(2,1)S(1)}, u32[]{:S(2)}, u32[]{:S(2)}) collective-permute-start(bf16[1,16,4096]{2,1,0:T(8,128)(2,1)S(1)} %get-tuple-element.5), channel_id=1, source_target_pairs={{0,8},{8,0},{16,24},{24,16},{32,40},{40,32},{48,56},{56,48},{64,72... | collective-permute-start | bytes 393224 | tf_op jit(solution)/shard_map/ppermute | solution.py:23
  36.8 2.8 %collective-permute-done.3 = bf16[1,16,4096]{2,1,0:T(8,128)(2,1)S(1)} collective-permute-done((bf16[1,16,4096]{2,1,0:T(8,128)(2,1)S(1)}, bf16[1,16,4096]{2,1,0:T(8,128)(2,1)S(1)}, u32[]{:S(2)}, u32[]{:S(2)}) %collective-permute-start.3) | collective-permute-done | bytes 131104 | tf_op jit(solution)/shard_map/ppermute | solution.py:23
  39.6 4.6 %collective-permute-start.4 = (bf16[2,16,4096]{2,1,0:T(8,128)(2,1)S(1)}, bf16[2,16,4096]{2,1,0:T(8,128)(2,1)S(1)}, u32[]{:S(2)}, u32[]{:S(2)}) collective-permute-start(bf16[2,16,4096]{2,1,0:T(8,128)(2,1)S(1)} %pad_maximum_fusion), channel_id=1, source_target_pairs={{0,24},{8,16},{16,8},{24,0},{32,56},{40,48},{48,40},{56,32},{64,88... | collective-permute-start | bytes 786440 | tf_op jit(solution)/shard_map/ppermute | solution.py:23
  44.3 1.7 %all-to-all-done = bf16[16,2,4096]{2,1,0:T(2,128)(2,1)S(1)} async-done(((bf16[16,2,4096]{2,1,0:T(2,128)(2,1)}), bf16[16,2,4096]{2,1,0:T(2,128)(2,1)S(1)}, u32[]{:S(2)}, u32[]{:S(2)}) %all-to-all-start) | async-done | bytes 262176 | tf_op jit(solution)/shard_map/all_to_all | solution.py:15
  46.3 2.0 %collective-permute-done.4 = bf16[2,16,4096]{2,1,0:T(8,128)(2,1)S(1)} collective-permute-done((bf16[2,16,4096]{2,1,0:T(8,128)(2,1)S(1)}, bf16[2,16,4096]{2,1,0:T(8,128)(2,1)S(1)}, u32[]{:S(2)}, u32[]{:S(2)}) %collective-permute-start.4) | collective-permute-done | bytes 262176 | tf_op jit(solution)/shard_map/ppermute | solution.py:23
  48.6 0.6 broadcast_in_dim.18
  49.2 11.2 %all-to-all-start.1 = ((f32[16,1,32]{2,1,0:T(1,128)}), f32[16,1,32]{2,1,0:T(1,128)S(1)}, u32[]{:S(2)}, u32[]{:S(2)}) async-start(f32[16,1,32]{2,1,0:T(1,128)} %broadcast_in_dim.18), calls=%async_computation.1 | async-start | bytes 16384 | tf_op jit(solution)/shard_map/all_to_all | solution.py:15
  60.9 10.7 %all-to-all-done.1 = f32[16,1,32]{2,1,0:T(1,128)S(1)} async-done(((f32[16,1,32]{2,1,0:T(1,128)}), f32[16,1,32]{2,1,0:T(1,128)S(1)}, u32[]{:S(2)}, u32[]{:S(2)}) %all-to-all-start.1) | async-done | bytes 2080 | tf_op jit(solution)/shard_map/all_to_all | solution.py:15
  71.6 0.3 convolution_convert_fusion.1
  72.0 1.1 %reshape.95 = bf16[32,2,4096]{2,1,0:T(2,128)(2,1)} reshape(bf16[64,4096]{1,0:T(8,128)(2,1)S(1)} %convolution_convert_fusion.1) | data formatting | bytes 1048576 | tf_op jit(solution)/shard_map/reshape | solution.py:88
  73.1 10.1 %all-to-all-start.2 = ((bf16[32,2,4096]{2,1,0:T(2,128)(2,1)}), bf16[32,2,4096]{2,1,0:T(2,128)(2,1)S(1)}, u32[]{:S(2)}, u32[]{:S(2)}) async-start(bf16[32,2,4096]{2,1,0:T(2,128)(2,1)} %reshape.95), calls=%async_computation.2 | async-start | bytes 1048576 | tf_op jit(solution)/shard_map/all_to_all | solution.py:89
  83.3 11.4 %all-to-all-done.2 = bf16[32,2,4096]{2,1,0:T(2,128)(2,1)S(1)} async-done(((bf16[32,2,4096]{2,1,0:T(2,128)(2,1)}), bf16[32,2,4096]{2,1,0:T(2,128)(2,1)S(1)}, u32[]{:S(2)}, u32[]{:S(2)}) %all-to-all-start.2) | async-done | bytes 524320 | tf_op jit(solution)/shard_map/all_to_all | solution.py:89
  94.7 0.4 convert_reduce_fusion
  95.5 8.1 %all_to_all.20 = bf16[8,2,4096]{2,1,0:T(2,128)(2,1)S(1)} all-to-all(bf16[8,2,4096]{2,1,0:T(2,128)(2,1)S(1)} %broadcast_in_dim.19), channel_id=1, replica_groups=mesh['dp'=64,'seq'=8] {'seq'}, dimensions={0} | all-to-all | bytes 262144 | tf_op jit(solution)/shard_map/all_to_all | solution.py:15
  103.7 1.5 %convolution_convert_fusion = bf16[128,4096]{1,0:T(8,128)(2,1)} fusion(bf16[16,4096]{1,0:T(8,128)(2,1)S(1)} %reshape.96, s32[128]{0:T(128)S(1)} %iota_add_fusion.1, s32[16]{0:T(128)S(1)} %multiply_reduce_fusion.2, s32[16]{0:T(128)S(1)} %fusion.23), kind=kOutput, calls=%fused_computation | convolution fusion | flops 17307648 | bytes 1180288 | tf_op jit(solution)/shard_map/dot_general | solution.py:100
  (37 shorter events, 2.6 us)
Async XLA Ops:
  0.0 1.5 %copy-start = (bf16[128,4096]{1,0:T(8,128)(2,1)S(1)}, bf16[128,4096]{1,0:T(8,128)(2,1)}, u32[]{:S(2)}) copy-start(bf16[128,4096]{1,0:T(8,128)(2,1)} %param.4) | copy-start | bytes 3145732
  0.0 10.6 %copy-start.1 = (bf16[2,4096]{1,0:T(2,128)(2,1)S(1)}, bf16[2,4096]{1,0:T(2,128)(2,1)}, u32[]{:S(2)}) copy-start(bf16[2,4096]{1,0:T(2,128)(2,1)} %param.6) | copy-start | bytes 49156
  1.8 9.7 %collective-permute-start = (bf16[16,4096]{1,0:T(8,128)(2,1)S(1)}, bf16[16,4096]{1,0:T(8,128)(2,1)S(1)}, u32[]{:S(2)}, u32[]{:S(2)}) collective-permute-start(bf16[16,4096]{1,0:T(8,128)(2,1)S(1)} %get-tuple-element.15), channel_id=1, source_target_pairs={{0,1},{1,0},{2,3},{3,2},{4,5},{5,4},{6,7},{7,6},{8,9},{9,8},{10,11... | collective-permute-start | bytes 393224 | tf_op jit(solution)/shard_map/ppermute | solution.py:19
  11.6 6.6 %collective-permute-start.1 = (bf16[16,4096]{1,0:T(8,128)(2,1)S(1)}, bf16[16,4096]{1,0:T(8,128)(2,1)S(1)}, u32[]{:S(2)}, u32[]{:S(2)}) collective-permute-start(bf16[16,4096]{1,0:T(8,128)(2,1)S(1)} %fusion), channel_id=1, source_target_pairs={{0,2},{1,3},{2,0},{3,1},{4,6},{5,7},{6,4},{7,5},{8,10},{9,11},{10,... | collective-permute-start | bytes 393224 | tf_op jit(solution)/shard_map/ppermute | solution.py:19
  18.3 14.9 %collective-permute-start.2 = (bf16[16,4096]{1,0:T(8,128)(2,1)S(1)}, bf16[16,4096]{1,0:T(8,128)(2,1)S(1)}, u32[]{:S(2)}, u32[]{:S(2)}) collective-permute-start(bf16[16,4096]{1,0:T(8,128)(2,1)S(1)} %fusion.1), channel_id=1, source_target_pairs={{0,6},{1,7},{2,4},{3,5},{4,2},{5,3},{6,0},{7,1},{8,14},{9,15},{10,... | collective-permute-start | bytes 393224 | tf_op jit(solution)/shard_map/ppermute | solution.py:19
  21.2 24.8 %all-to-all-start = ((bf16[16,2,4096]{2,1,0:T(2,128)(2,1)}), bf16[16,2,4096]{2,1,0:T(2,128)(2,1)S(1)}, u32[]{:S(2)}, u32[]{:S(2)}) async-start(bf16[16,2,4096]{2,1,0:T(2,128)(2,1)} %broadcast_in_dim.17), calls=%async_computation | async-start | bytes 524288 | tf_op jit(solution)/shard_map/all_to_all | solution.py:15
  33.6 6.0 %collective-permute-start.3 = (bf16[1,16,4096]{2,1,0:T(8,128)(2,1)S(1)}, bf16[1,16,4096]{2,1,0:T(8,128)(2,1)S(1)}, u32[]{:S(2)}, u32[]{:S(2)}) collective-permute-start(bf16[1,16,4096]{2,1,0:T(8,128)(2,1)S(1)} %get-tuple-element.5), channel_id=1, source_target_pairs={{0,8},{8,0},{16,24},{24,16},{32,40},{40,32},{48,56},{56,48},{64,72... | collective-permute-start | bytes 393224 | tf_op jit(solution)/shard_map/ppermute | solution.py:23
  39.6 20.8 %copy-start.2 = (s32[1024]{0:T(1024)S(1)}, s32[1024]{0:T(1024)}, u32[]{:S(2)}) copy-start(s32[1024]{0:T(1024)} %param.7) | copy-start | bytes 12292
  39.6 8.7 %collective-permute-start.4 = (bf16[2,16,4096]{2,1,0:T(8,128)(2,1)S(1)}, bf16[2,16,4096]{2,1,0:T(8,128)(2,1)S(1)}, u32[]{:S(2)}, u32[]{:S(2)}) collective-permute-start(bf16[2,16,4096]{2,1,0:T(8,128)(2,1)S(1)} %pad_maximum_fusion), channel_id=1, source_target_pairs={{0,24},{8,16},{16,8},{24,0},{32,56},{40,48},{48,40},{56,32},{64,88... | collective-permute-start | bytes 786440 | tf_op jit(solution)/shard_map/ppermute | solution.py:23
  49.2 22.4 %all-to-all-start.1 = ((f32[16,1,32]{2,1,0:T(1,128)}), f32[16,1,32]{2,1,0:T(1,128)S(1)}, u32[]{:S(2)}, u32[]{:S(2)}) async-start(f32[16,1,32]{2,1,0:T(1,128)} %broadcast_in_dim.18), calls=%async_computation.1 | async-start | bytes 16384 | tf_op jit(solution)/shard_map/all_to_all | solution.py:15
  73.1 21.6 %all-to-all-start.2 = ((bf16[32,2,4096]{2,1,0:T(2,128)(2,1)}), bf16[32,2,4096]{2,1,0:T(2,128)(2,1)S(1)}, u32[]{:S(2)}, u32[]{:S(2)}) async-start(bf16[32,2,4096]{2,1,0:T(2,128)(2,1)} %reshape.95), calls=%async_computation.2 | async-start | bytes 1048576 | tf_op jit(solution)/shard_map/all_to_all | solution.py:89

commit v3 on v1

v3 whole, which is shorter than its diff:
```python
import jax
import jax.numpy as jnp
from jax import lax
from jax.sharding import PartitionSpec as P

loss_scale = 1048576.0
inv_temp = 20.0
DP, S = 64, 8


def share(block, axis, count):
    copies = jnp.broadcast_to(block[None], (count,) + block.shape)
    return lax.all_to_all(copies, axis, 0, 0)


def swap_seq(block, mask):
    return lax.ppermute(block, "seq", [(i, i ^ mask) for i in range(S)])


def per_device(token_rows, extra_len, queries, positive):
    row_count, width = token_rows.shape
    pass_count = extra_len.shape[1]
    own = queries.shape[0]
    seq_index = lax.axis_index("seq")
    dp_index = lax.axis_index("dp")

    raw = share(queries, "dp", DP).reshape(DP * own, width).astype(jnp.float32)
    some_queries = (
        raw * lax.rsqrt(jnp.sum(raw * raw, axis=-1, keepdims=True) + 1e-06)
    ).astype(jnp.bfloat16)
    some_positive = lax.dynamic_index_in_dim(
        positive.reshape(DP, S, own), seq_index, 1, keepdims=False
    ).reshape(-1)

    lengths = extra_len[0] + 15
    upto = jnp.tril(jnp.ones((pass_count, pass_count), jnp.int32))
    end_rows = jnp.sum(upto * lengths[None, :], axis=1)
    first_rows = end_rows - lengths
    row_pos = seq_index * row_count + jnp.arange(row_count, dtype=jnp.int32)
    member = (
        (row_pos[None, :] >= first_rows[:, None]) & (row_pos[None, :] < end_rows[:, None])
    ).astype(jnp.bfloat16)
    sums = jnp.dot(member, token_rows, preferred_element_type=jnp.float32)
    for mask in (1, 2, 6):
        sums = sums + swap_seq(sums.astype(jnp.bfloat16), mask).astype(jnp.float32)
    float_len = lengths.astype(jnp.float32)[:, None]
    pooled = sums / float_len
    inv_norm = lax.rsqrt(jnp.sum(pooled * pooled, axis=-1, keepdims=True) + 1e-06)
    embedding = pooled * inv_norm
    embed_half = embedding.astype(jnp.bfloat16)

    scores = (
        lax.dot_general(
            embed_half, some_queries, (((1,), (1,)), ((), ())), preferred_element_type=jnp.float32
        )
        * inv_temp
    )
    exp_scores = jnp.exp(scores)
    part_totals = jnp.sum(exp_scores, axis=0, keepdims=True)
    totals = jnp.sum(share(part_totals, "dp", DP), axis=0)
    pass_ids = dp_index * pass_count + jnp.arange(pass_count, dtype=jnp.int32)
    target = (pass_ids[:, None] == some_positive[None, :]).astype(jnp.float32)
    factor = loss_scale * inv_temp / positive.shape[0]
    coefficients = ((exp_scores / totals - target) * factor).astype(jnp.bfloat16)

    slots = pass_count // S
    d_partial = jnp.dot(coefficients, some_queries, preferred_element_type=jnp.float32)
    d_partial = d_partial.astype(jnp.bfloat16).reshape(S, slots, width)
    d_parts = lax.all_to_all(d_partial, "seq", 0, 0)
    d_embed = jnp.sum(d_parts.astype(jnp.float32), axis=0)
    first = seq_index * slots
    own_embedding = lax.dynamic_slice_in_dim(embedding, first, slots, 0)
    own_norm = lax.dynamic_slice_in_dim(inv_norm, first, slots, 0)
    own_len = lax.dynamic_slice_in_dim(float_len, first, slots, 0)
    d_pooled = own_norm * (
        d_embed - own_embedding * jnp.sum(own_embedding * d_embed, axis=-1, keepdims=True)
    )
    d_sum = (d_pooled / own_len).astype(jnp.bfloat16)
    every_d_sum = share(d_sum, "seq", S).reshape(pass_count, width)
    grads = lax.dot_general(
        member, every_d_sum, (((0,), (0,)), ((), ())), preferred_element_type=jnp.float32
    )
    return grads.astype(jnp.bfloat16)


def solution(mesh):
    return jax.shard_map(
        per_device,
        mesh=mesh,
        in_specs=(P(("dp", "seq"), None), P("dp", None), P(("dp", "seq"), None), P()),
        out_specs=P(("dp", "seq"), None),
        check_vma=False,
    )
```

time: 128 us -> 127 us (level)
  blocking collectives: 22.1 us -> 8.52 us
  starting transfers between devices: 39.3 us -> 45.7 us
  local copies, waits for them, and re-layouts: 6.7 us -> 10.1 us
  matrix products: 2.56 us -> 3.94 us
    all_to_all x1, blocking collectives: 22.1 us -> 8.52 us  [share(): return lax.all_to_all(copies, axis, 0, 0)]
    ppermute x0 -> x3, starting transfers between devices: none -> 10.4 us  [swap_seq(): return lax.ppermute(block, 'seq', [(i, i ^ mask) for i in range(S)])]
    ppermute x0 -> x3, waiting for transfers between devices: none -> 7.28 us  [swap_seq(): return lax.ppermute(block, 'seq', [(i, i ^ mask) for i in range(S)])]
    all_to_all x5 -> x3, waiting for transfers between devices: 53 us -> 47 us  [the longest x2 43.1 us: share(): return lax.all_to_all(copies, axis, 0, 0)]
    all_to_all x5 -> x3, starting transfers between devices: 39.3 us -> 35.4 us  [the longest x2 28.3 us: share(): return lax.all_to_all(copies, axis, 0, 0)]
    another operation x0 -> x2, local copies, waits for them, and re-layouts: none -> 1.39 us
    convert_element_type x0 -> x1, local copies, waits for them, and re-layouts: none -> 1.37 us  [per_device(): raw = share(queries, 'dp', DP).reshape(DP * own, width).astype(jnp.float32)]
    convert_element_type x2 -> x3, other arithmetic: 1.46 us -> 0.16 us  [the longest x1 0.1 us: per_device(): d_sum = (d_pooled / own_len).astype(jnp.bfloat16)]
  transfers between devices with their start and end apart: 5 -> 6, of which waited for: 5 -> 6; matrix products, arithmetic and copies ran while one was open for 3% -> 4% of each run, Pallas kernels for 0% -> 0%
where the time goes in v3:
time: 127 us; the launch traced here: 126 us
  waiting for transfers between devices  54.2 us (43%)
  starting transfers between devices  45.7 us (36%)
  local copies, waits for them, and re-layouts  10.1 us (8%)
  blocking collectives  8.52 us (7%)
  matrix products  3.94 us (3%)
  other arithmetic  3.17 us (2%)
    all_to_all x2, waiting for transfers between devices, share(): return lax.all_to_all(copies, axis, 0, 0)  43.1 us
    all_to_all x2, starting transfers between devices, share(): return lax.all_to_all(copies, axis, 0, 0)  28.3 us
    ppermute x3, starting transfers between devices, swap_seq(): return lax.ppermute(block, 'seq', [(i, i ^ mask) for i in range(S)])  10.4 us
    all_to_all x1, blocking collectives, share(): return lax.all_to_all(copies, axis, 0, 0)  8.52 us
    ppermute x3, waiting for transfers between devices, swap_seq(): return lax.ppermute(block, 'seq', [(i, i ^ mask) for i in range(S)])  7.28 us
    all_to_all x1, starting transfers between devices, per_device(): d_parts = lax.all_to_all(d_partial, 'seq', 0, 0)  7.09 us
    all_to_all x1, waiting for transfers between devices, per_device(): d_parts = lax.all_to_all(d_partial, 'seq', 0, 0)  3.89 us
    broadcast_in_dim x3, local copies, waits for them, and re-layouts, share(): copies = jnp.broadcast_to(block[None], (count,) + block.shape)  3.51 us
  transfers between devices with their start and end apart: 6, of which 6 were waited for; matrix products, arithmetic and copies ran while one was open for 4% of the time, Pallas kernels for 0%

profile of v3, /device:TPU:1, one launch (start us, length us, event | category | flops | bytes accessed | tf_op | source)
XLA Modules:
  0.0 126.0 jit_solution(10856415850514783113)
XLA Ops:
  0.0 2.8 %broadcast_in_dim.14 = bf16[64,2,4096]{2,1,0:T(2,128)(2,1)} broadcast(bf16[2,4096]{1,0:T(2,128)(2,1)} %param.6), dimensions={1,2} | broadcast | bytes 1064960 | tf_op jit(solution)/shard_map/broadcast_in_dim | solution.py:12
  2.8 19.3 %all-to-all-start = ((bf16[64,2,4096]{2,1,0:T(2,128)(2,1)}), bf16[64,2,4096]{2,1,0:T(2,128)(2,1)S(1)}, u32[]{:S(2)}, u32[]{:S(2)}) async-start(bf16[64,2,4096]{2,1,0:T(2,128)(2,1)} %broadcast_in_dim.14), calls=%async_computation | async-start | bytes 2097152 | tf_op jit(solution)/shard_map/all_to_all | solution.py:13
  22.9 2.9 %collective-permute-start = (bf16[16,4096]{1,0:T(8,128)(2,1)S(1)}, bf16[16,4096]{1,0:T(8,128)(2,1)S(1)}, u32[]{:S(2)}, u32[]{:S(2)}) collective-permute-start(bf16[16,4096]{1,0:T(8,128)(2,1)S(1)} %get-tuple-element.9), channel_id=1, source_target_pairs={{0,1},{1,0},{2,3},{3,2},{4,5},{5,4},{6,7},{7,6},{8,9},{9,8},{10,11... | collective-permute-start | bytes 393224 | tf_op jit(solution)/shard_map/ppermute | solution.py:17
  25.7 1.0 collective-permute-done
  26.7 3.1 %collective-permute-start.1 = (bf16[16,4096]{1,0:T(8,128)(2,1)S(1)}, bf16[16,4096]{1,0:T(8,128)(2,1)S(1)}, u32[]{:S(2)}, u32[]{:S(2)}) collective-permute-start(bf16[16,4096]{1,0:T(8,128)(2,1)S(1)} %fusion.1), channel_id=1, source_target_pairs={{0,2},{1,3},{2,0},{3,1},{4,6},{5,7},{6,4},{7,5},{8,10},{9,11},{10,... | collective-permute-start | bytes 393224 | tf_op jit(solution)/shard_map/ppermute | solution.py:17
  29.8 3.5 %collective-permute-done.1 = bf16[16,4096]{1,0:T(8,128)(2,1)S(1)} collective-permute-done((bf16[16,4096]{1,0:T(8,128)(2,1)S(1)}, bf16[16,4096]{1,0:T(8,128)(2,1)S(1)}, u32[]{:S(2)}, u32[]{:S(2)}) %collective-permute-start.1) | collective-permute-done | bytes 131104 | tf_op jit(solution)/shard_map/ppermute | solution.py:17
  33.4 4.4 %collective-permute-start.2 = (bf16[16,4096]{1,0:T(8,128)(2,1)S(1)}, bf16[16,4096]{1,0:T(8,128)(2,1)S(1)}, u32[]{:S(2)}, u32[]{:S(2)}) collective-permute-start(bf16[16,4096]{1,0:T(8,128)(2,1)S(1)} %fusion.3), channel_id=1, source_target_pairs={{0,6},{1,7},{2,4},{3,5},{4,2},{5,3},{6,0},{7,1},{8,14},{9,15},{10,... | collective-permute-start | bytes 393224 | tf_op jit(solution)/shard_map/ppermute | solution.py:17
  37.8 2.8 %collective-permute-done.2 = bf16[16,4096]{1,0:T(8,128)(2,1)S(1)} collective-permute-done((bf16[16,4096]{1,0:T(8,128)(2,1)S(1)}, bf16[16,4096]{1,0:T(8,128)(2,1)S(1)}, u32[]{:S(2)}, u32[]{:S(2)}) %collective-permute-start.2) | collective-permute-done | bytes 131104 | tf_op jit(solution)/shard_map/ppermute | solution.py:17
  40.9 32.6 %all-to-all-done = bf16[64,2,4096]{2,1,0:T(2,128)(2,1)S(1)} async-done(((bf16[64,2,4096]{2,1,0:T(2,128)(2,1)}), bf16[64,2,4096]{2,1,0:T(2,128)(2,1)S(1)}, u32[]{:S(2)}, u32[]{:S(2)}) %all-to-all-start) | async-done | bytes 1048608 | tf_op jit(solution)/shard_map/all_to_all | solution.py:13
  73.5 1.2 multiply_reduce_fusion
  74.9 1.4 %reshape.80 = f32[128,4096]{1,0:T(8,128)S(1)} reshape(bf16[64,2,4096]{2,1,0:T(2,128)(2,1)} %copy-done.1) | data formatting | bytes 3145728 | tf_op jit(solution)/shard_map/convert_element_type | solution.py:27
  77.4 9.0 %all-to-all-start.1 = ((f32[64,1,128]{2,1,0:T(1,128)}), f32[64,1,128]{2,1,0:T(1,128)S(1)}, u32[]{:S(2)}, u32[]{:S(2)}) async-start(f32[64,1,128]{2,1,0:T(1,128)} %broadcast_in_dim.15), calls=%async_computation.1 | async-start | bytes 65536 | tf_op jit(solution)/shard_map/all_to_all | solution.py:13
  86.4 0.9 reshape.77
  87.3 1.1 dynamic-slice_reduce_fusion
  88.4 0.7 eq.16
  89.5 10.5 %all-to-all-done.1 = f32[64,1,128]{2,1,0:T(1,128)S(1)} async-done(((f32[64,1,128]{2,1,0:T(1,128)}), f32[64,1,128]{2,1,0:T(1,128)S(1)}, u32[]{:S(2)}, u32[]{:S(2)}) %all-to-all-start.1) | async-done | bytes 32800 | tf_op jit(solution)/shard_map/all_to_all | solution.py:13
  100.6 1.0 convolution_convert_fusion.1
  101.6 0.8 reshape.78
  102.4 7.1 %all-to-all-start.2 = ((bf16[8,2,4096]{2,1,0:T(2,128)(2,1)}), bf16[8,2,4096]{2,1,0:T(2,128)(2,1)S(1)}, u32[]{:S(2)}, u32[]{:S(2)}) async-start(bf16[8,2,4096]{2,1,0:T(2,128)(2,1)} %reshape.78), calls=%async_computation.2 | async-start | bytes 262144 | tf_op jit(solution)/shard_map/all_to_all | solution.py:69
  109.5 0.7 dynamic-slice.7
  110.2 0.7 dynamic-slice.6
  110.8 3.9 %all-to-all-done.2 = bf16[8,2,4096]{2,1,0:T(2,128)(2,1)S(1)} async-done(((bf16[8,2,4096]{2,1,0:T(2,128)(2,1)}), bf16[8,2,4096]{2,1,0:T(2,128)(2,1)S(1)}, u32[]{:S(2)}, u32[]{:S(2)}) %all-to-all-start.2) | async-done | bytes 131104 | tf_op jit(solution)/shard_map/all_to_all | solution.py:69
  115.2 8.5 %all_to_all.20 = bf16[8,2,4096]{2,1,0:T(2,128)(2,1)S(1)} all-to-all(bf16[8,2,4096]{2,1,0:T(2,128)(2,1)S(1)} %broadcast_in_dim.16), channel_id=1, replica_groups=mesh['dp'=64,'seq'=8] {'seq'}, dimensions={0} | all-to-all | bytes 262144 | tf_op jit(solution)/shard_map/all_to_all | solution.py:13
  123.8 2.2 %convolution_convert_fusion = bf16[128,4096]{1,0:T(8,128)(2,1)} fusion(bf16[16,4096]{1,0:T(8,128)(2,1)S(1)} %reshape.79, s32[128]{0:T(128)} %copy-done.3, s32[16]{0:T(128)S(1)} %multiply_reduce_fusion.3, s32[16]{0:T(128)} %copy-done.4), kind=kOutput, calls=%fused_computation | convolution fusion | flops 17307648 | bytes 1180288 | tf_op jit(solution)/shard_map/dot_general | solution.py:80
  (37 shorter events, 4.0 us)
Async XLA Ops:
  0.0 22.3 %copy-start = (bf16[128,4096]{1,0:T(8,128)(2,1)S(1)}, bf16[128,4096]{1,0:T(8,128)(2,1)}, u32[]{:S(2)}) copy-start(bf16[128,4096]{1,0:T(8,128)(2,1)} %param.4) | copy-start | bytes 3145732
  0.0 22.1 %copy-start.7 = (s32[1,16]{1,0:T(1,128)S(1)}, s32[1,16]{1,0:T(1,128)}, u32[]{:S(2)}) copy-start(s32[1,16]{1,0:T(1,128)} %param.5) | copy-start | bytes 196
  2.8 70.7 %all-to-all-start = ((bf16[64,2,4096]{2,1,0:T(2,128)(2,1)}), bf16[64,2,4096]{2,1,0:T(2,128)(2,1)S(1)}, u32[]{:S(2)}, u32[]{:S(2)}) async-start(bf16[64,2,4096]{2,1,0:T(2,128)(2,1)} %broadcast_in_dim.14), calls=%async_computation | async-start | bytes 2097152 | tf_op jit(solution)/shard_map/all_to_all | solution.py:13
  22.1 18.7 %copy-start.5 = (f32[16]{0:T(128)}, f32[16]{0:T(128)S(1)}, u32[]{:S(2)}) copy-start(f32[16]{0:T(128)S(1)} %get-tuple-element.8) | copy-start | bytes 196
  22.3 0.5 copy-start.3
  22.3 0.6 copy-start.4
  22.9 3.8 %collective-permute-start = (bf16[16,4096]{1,0:T(8,128)(2,1)S(1)}, bf16[16,4096]{1,0:T(8,128)(2,1)S(1)}, u32[]{:S(2)}, u32[]{:S(2)}) collective-permute-start(bf16[16,4096]{1,0:T(8,128)(2,1)S(1)} %get-tuple-element.9), channel_id=1, source_target_pairs={{0,1},{1,0},{2,3},{3,2},{4,5},{5,4},{6,7},{7,6},{8,9},{9,8},{10,11... | collective-permute-start | bytes 393224 | tf_op jit(solution)/shard_map/ppermute | solution.py:17
  26.7 6.6 %collective-permute-start.1 = (bf16[16,4096]{1,0:T(8,128)(2,1)S(1)}, bf16[16,4096]{1,0:T(8,128)(2,1)S(1)}, u32[]{:S(2)}, u32[]{:S(2)}) collective-permute-start(bf16[16,4096]{1,0:T(8,128)(2,1)S(1)} %fusion.1), channel_id=1, source_target_pairs={{0,2},{1,3},{2,0},{3,1},{4,6},{5,7},{6,4},{7,5},{8,10},{9,11},{10,... | collective-permute-start | bytes 393224 | tf_op jit(solution)/shard_map/ppermute | solution.py:17
  33.4 7.2 %collective-permute-start.2 = (bf16[16,4096]{1,0:T(8,128)(2,1)S(1)}, bf16[16,4096]{1,0:T(8,128)(2,1)S(1)}, u32[]{:S(2)}, u32[]{:S(2)}) collective-permute-start(bf16[16,4096]{1,0:T(8,128)(2,1)S(1)} %fusion.3), channel_id=1, source_target_pairs={{0,6},{1,7},{2,4},{3,5},{4,2},{5,3},{6,0},{7,1},{8,14},{9,15},{10,... | collective-permute-start | bytes 393224 | tf_op jit(solution)/shard_map/ppermute | solution.py:17
  40.8 32.7 %copy-start.6 = (f32[16]{0:T(128)}, f32[16]{0:T(128)S(1)}, u32[]{:S(2)}) copy-start(f32[16]{0:T(128)S(1)} %add_rsqrt_fusion.1) | copy-start | bytes 196
  73.5 1.2 copy-start.1
  74.9 11.5 %copy-start.2 = (s32[1024]{0:T(1024)S(1)}, s32[1024]{0:T(1024)}, u32[]{:S(2)}) copy-start(s32[1024]{0:T(1024)} %param.7) | copy-start | bytes 12292
  77.4 22.6 %all-to-all-start.1 = ((f32[64,1,128]{2,1,0:T(1,128)}), f32[64,1,128]{2,1,0:T(1,128)S(1)}, u32[]{:S(2)}, u32[]{:S(2)}) async-start(f32[64,1,128]{2,1,0:T(1,128)} %broadcast_in_dim.15), calls=%async_computation.1 | async-start | bytes 65536 | tf_op jit(solution)/shard_map/all_to_all | solution.py:13
  102.4 12.4 %all-to-all-start.2 = ((bf16[8,2,4096]{2,1,0:T(2,128)(2,1)}), bf16[8,2,4096]{2,1,0:T(2,128)(2,1)S(1)}, u32[]{:S(2)}, u32[]{:S(2)}) async-start(bf16[8,2,4096]{2,1,0:T(2,128)(2,1)} %reshape.78), calls=%async_computation.2 | async-start | bytes 262144 | tf_op jit(solution)/shard_map/all_to_all | solution.py:69

commit v4 on v3

--- a/solution.py
+++ b/solution.py
@@ -5,16 +5,23 @@
 
 loss_scale = 1048576.0
 inv_temp = 20.0
-DP, S = 64, 8
+Z, Y, S = 16, 4, 8
+Z_GROUPS = [[z * Y + y for z in range(Z)] for y in range(Y)]
+PAIRS = [[p * 2 * S + i for i in range(2 * S)] for p in range(Z * Y // 2)]
+LINES = [[z * Y + y for z in range(Z) for y in (low, 3 - low)] for low in range(2)]
 
 
-def share(block, axis, count):
+def share(block, axis, count, groups=None):
     copies = jnp.broadcast_to(block[None], (count,) + block.shape)
-    return lax.all_to_all(copies, axis, 0, 0)
+    return lax.all_to_all(copies, axis, 0, 0, axis_index_groups=groups)
 
 
 def swap_seq(block, mask):
     return lax.ppermute(block, "seq", [(i, i ^ mask) for i in range(S)])
+
+
+def swap_y(block, mask):
+    return lax.ppermute(block, "dp", [(i, i ^ mask) for i in range(Z * Y)])
 
 
 def per_device(token_rows, extra_len, queries, positive):
@@ -23,14 +30,18 @@
     own = queries.shape[0]
     seq_index = lax.axis_index("seq")
     dp_index = lax.axis_index("dp")
+    y_index = dp_index & (Y - 1)
 
-    raw = share(queries, "dp", DP).reshape(DP * own, width).astype(jnp.float32)
-    some_queries = (
-        raw * lax.rsqrt(jnp.sum(raw * raw, axis=-1, keepdims=True) + 1e-06)
+    query_float = queries.astype(jnp.float32)
+    query_norm = (
+        query_float * lax.rsqrt(jnp.sum(query_float * query_float, axis=-1, keepdims=True) + 1e-06)
     ).astype(jnp.bfloat16)
-    some_positive = lax.dynamic_index_in_dim(
-        positive.reshape(DP, S, own), seq_index, 1, keepdims=False
-    ).reshape(-1)
+    own_line = share(query_norm, "dp", Z, Z_GROUPS).reshape(Z * own, width)
+    other_line = swap_y(own_line, 3)
+    by_line = positive.reshape(Z, Y, S, own)
+
+    def line_positive(y):
+        return lax.dynamic_slice(by_line, (0, y, seq_index, 0), (Z, 1, 1, own)).reshape(-1)
 
     lengths = extra_len[0] + 15
     upto = jnp.tril(jnp.ones((pass_count, pass_count), jnp.int32))
@@ -47,26 +58,46 @@
     pooled = sums / float_len
     inv_norm = lax.rsqrt(jnp.sum(pooled * pooled, axis=-1, keepdims=True) + 1e-06)
     embedding = pooled * inv_norm
+
+    odd = (y_index & 1) == 1
     embed_half = embedding.astype(jnp.bfloat16)
+    beside = swap_y(embed_half, 1)
+    embeds = jnp.concatenate(
+        [jnp.where(odd, beside, embed_half), jnp.where(odd, embed_half, beside)], axis=0
+    )
 
-    scores = (
-        lax.dot_general(
-            embed_half, some_queries, (((1,), (1,)), ((), ())), preferred_element_type=jnp.float32
+    def exp_scores(line):
+        return jnp.exp(
+            lax.dot_general(
+                embeds, line, (((1,), (1,)), ((), ())), preferred_element_type=jnp.float32
+            )
+            * inv_temp
         )
-        * inv_temp
-    )
-    exp_scores = jnp.exp(scores)
-    part_totals = jnp.sum(exp_scores, axis=0, keepdims=True)
-    totals = jnp.sum(share(part_totals, "dp", DP), axis=0)
-    pass_ids = dp_index * pass_count + jnp.arange(pass_count, dtype=jnp.int32)
-    target = (pass_ids[:, None] == some_positive[None, :]).astype(jnp.float32)
+
+    own_exp, other_exp = exp_scores(own_line), exp_scores(other_line)
+    own_part, other_part = jnp.sum(own_exp, axis=0), jnp.sum(other_exp, axis=0)
+    high = y_index >= 2
+    parts = jnp.stack([jnp.where(high, other_part, own_part), jnp.where(high, own_part, other_part)])
+    totals = jnp.sum(share(parts, "dp", 2 * Z, LINES), axis=0)
+    own_total = jnp.where(high, totals[1], totals[0])
+    other_total = jnp.where(high, totals[0], totals[1])
+    pass_ids = (dp_index - (y_index & 1)) * pass_count + jnp.arange(2 * pass_count, dtype=jnp.int32)
     factor = loss_scale * inv_temp / positive.shape[0]
-    coefficients = ((exp_scores / totals - target) * factor).astype(jnp.bfloat16)
+
+    def coefficients(exps, total, y):
+        target = (pass_ids[:, None] == line_positive(y)[None, :]).astype(jnp.float32)
+        return ((exps / total[None, :] - target) * factor).astype(jnp.bfloat16)
 
     slots = pass_count // S
-    d_partial = jnp.dot(coefficients, some_queries, preferred_element_type=jnp.float32)
-    d_partial = d_partial.astype(jnp.bfloat16).reshape(S, slots, width)
-    d_parts = lax.all_to_all(d_partial, "seq", 0, 0)
+    d_partial = jnp.dot(
+        coefficients(own_exp, own_total, y_index), own_line, preferred_element_type=jnp.float32
+    ) + jnp.dot(
+        coefficients(other_exp, other_total, 3 - y_index),
+        other_line,
+        preferred_element_type=jnp.float32,
+    )
+    d_partial = d_partial.astype(jnp.bfloat16).reshape(2 * S, slots, width)
+    d_parts = lax.all_to_all(d_partial, ("dp", "seq"), 0, 0, axis_index_groups=PAIRS)
     d_embed = jnp.sum(d_parts.astype(jnp.float32), axis=0)
     first = seq_index * slots
     own_embedding = lax.dynamic_slice_in_dim(embedding, first, slots, 0)

time: 127 us -> 110 us (0.87)
  waiting for transfers between devices: 54.2 us -> 38.2 us
  starting transfers between devices: 45.7 us -> 54.1 us
  local copies, waits for them, and re-layouts: 10.1 us -> 3.24 us
    all_to_all x3, waiting for transfers between devices: 47 us -> 29.3 us  [the longest x2 22.2 us: share(): return lax.all_to_all(copies, axis, 0, 0, axis_index_groups=groups)]
    ppermute x0 -> x2, starting transfers between devices: none -> 7.85 us  [swap_y(): return lax.ppermute(block, 'dp', [(i, i ^ mask) for i in range(Z * Y)])]
    ppermute x0 -> x2, waiting for transfers between devices: none -> 3.47 us  [swap_y(): return lax.ppermute(block, 'dp', [(i, i ^ mask) for i in range(Z * Y)])]
    ppermute x3, starting transfers between devices: 10.4 us -> 12.6 us  [swap_seq(): return lax.ppermute(block, 'seq', [(i, i ^ mask) for i in range(S)])]
    broadcast_in_dim x3, local copies, waits for them, and re-layouts: 3.51 us -> 1.6 us  [share(): copies = jnp.broadcast_to(block[None], (count,) + block.shape)]
    ppermute x3, waiting for transfers between devices: 7.28 us -> 5.48 us  [swap_seq(): return lax.ppermute(block, 'seq', [(i, i ^ mask) for i in range(S)])]
    all_to_all x3, starting transfers between devices: 35.4 us -> 33.6 us  [the longest x2 26.5 us: share(): return lax.all_to_all(copies, axis, 0, 0, axis_index_groups=groups)]
    reduce_sum x2, other arithmetic: 1.78 us -> 0.19 us  [the longest x1 0.15 us: per_device(): jnp.sum(query_float * query_float, axis=-1, keepdims=True) + 1e-06]
  transfers between devices with their start and end apart: 6 -> 8, of which waited for: 6 -> 6; matrix products, arithmetic and copies ran while one was open for 4% -> 2% of each run, Pallas kernels for 0% -> 0%
where the time goes in v4:
time: 110 us
  starting transfers between devices  54.1 us (49%)
  waiting for transfers between devices  38.2 us (35%)
  blocking collectives  8.47 us (8%)
  local copies, waits for them, and re-layouts  3.24 us (3%)
  matrix products  2.82 us (3%)
  other arithmetic  2.74 us (2%)
    all_to_all x2, starting transfers between devices, share(): return lax.all_to_all(copies, axis, 0, 0, axis_index_groups=groups)  26.5 us
    all_to_all x2, waiting for transfers between devices, share(): return lax.all_to_all(copies, axis, 0, 0, axis_index_groups=groups)  22.2 us
    ppermute x3, starting transfers between devices, swap_seq(): return lax.ppermute(block, 'seq', [(i, i ^ mask) for i in range(S)])  12.6 us
    all_to_all x1, blocking collectives, share(): return lax.all_to_all(copies, axis, 0, 0, axis_index_groups=groups)  8.47 us
    ppermute x2, starting transfers between devices, swap_y(): return lax.ppermute(block, 'dp', [(i, i ^ mask) for i in range(Z * Y)])  7.85 us
    all_to_all x1, waiting for transfers between devices, per_device(): lax.all_to_all(d_partial, ('dp', 'seq'), 0, 0, axis_index_groups=PAIRS)  7.09 us
    all_to_all x1, starting transfers between devices, per_device(): lax.all_to_all(d_partial, ('dp', 'seq'), 0, 0, axis_index_groups=PAIRS)  7.09 us
    ppermute x3, waiting for transfers between devices, swap_seq(): return lax.ppermute(block, 'seq', [(i, i ^ mask) for i in range(S)])  5.48 us
  transfers between devices with their start and end apart: 8, of which 6 were waited for; matrix products, arithmetic and copies ran while one was open for 2% of the time, Pallas kernels for 0%

profile of v4, /device:TPU:1, one launch (start us, length us, event | category | flops | bytes accessed | tf_op | source)
XLA Modules:
  0.0 109.8 jit_solution(6809744469181804373)
XLA Ops:
  0.0 0.7 add_bitcast_fusion
  0.9 0.7 fusion.33
  1.5 0.3 fusion.35
  1.8 8.8 %collective-permute-start = (bf16[16,4096]{1,0:T(8,128)(2,1)S(1)}, bf16[16,4096]{1,0:T(8,128)(2,1)S(1)}, u32[]{:S(2)}, u32[]{:S(2)}) collective-permute-start(bf16[16,4096]{1,0:T(8,128)(2,1)S(1)} %get-tuple-element.19), channel_id=1, source_target_pairs={{0,1},{1,0},{2,3},{3,2},{4,5},{5,4},{6,7},{7,6},{8,9},{9,8},{10,11... | collective-permute-start | bytes 393224 | tf_op jit(solution)/shard_map/ppermute | solution.py:20
  10.8 0.8 collective-permute-done
  11.6 1.9 %collective-permute-start.1 = (bf16[16,4096]{1,0:T(8,128)(2,1)S(1)}, bf16[16,4096]{1,0:T(8,128)(2,1)S(1)}, u32[]{:S(2)}, u32[]{:S(2)}) collective-permute-start(bf16[16,4096]{1,0:T(8,128)(2,1)S(1)} %fusion.3), channel_id=1, source_target_pairs={{0,2},{1,3},{2,0},{3,1},{4,6},{5,7},{6,4},{7,5},{8,10},{9,11},{10,... | collective-permute-start | bytes 393224 | tf_op jit(solution)/shard_map/ppermute | solution.py:20
  13.6 4.7 %collective-permute-done.1 = bf16[16,4096]{1,0:T(8,128)(2,1)S(1)} collective-permute-done((bf16[16,4096]{1,0:T(8,128)(2,1)S(1)}, bf16[16,4096]{1,0:T(8,128)(2,1)S(1)}, u32[]{:S(2)}, u32[]{:S(2)}) %collective-permute-start.1) | collective-permute-done | bytes 131104 | tf_op jit(solution)/shard_map/ppermute | solution.py:20
  18.3 1.9 %collective-permute-start.2 = (bf16[16,4096]{1,0:T(8,128)(2,1)S(1)}, bf16[16,4096]{1,0:T(8,128)(2,1)S(1)}, u32[]{:S(2)}, u32[]{:S(2)}) collective-permute-start(bf16[16,4096]{1,0:T(8,128)(2,1)S(1)} %fusion.4), channel_id=1, source_target_pairs={{0,6},{1,7},{2,4},{3,5},{4,2},{5,3},{6,0},{7,1},{8,14},{9,15},{10,... | collective-permute-start | bytes 393224 | tf_op jit(solution)/shard_map/ppermute | solution.py:20
  20.3 0.9 broadcast_in_dim.14
  21.2 12.0 %all-to-all-start = ((bf16[16,2,4096]{2,1,0:T(2,128)(2,1)}), bf16[16,2,4096]{2,1,0:T(2,128)(2,1)S(1)}, u32[]{:S(2)}, u32[]{:S(2)}) async-start(bf16[16,2,4096]{2,1,0:T(2,128)(2,1)} %broadcast_in_dim.14), calls=%async_computation | async-start | bytes 524288 | tf_op jit(solution)/shard_map/all_to_all | solution.py:16
  33.6 3.2 %collective-permute-start.3 = (bf16[16,4096]{1,0:T(8,128)(2,1)S(1)}, bf16[16,4096]{1,0:T(8,128)(2,1)S(1)}, u32[]{:S(2)}, u32[]{:S(2)}) collective-permute-start(bf16[16,4096]{1,0:T(8,128)(2,1)S(1)} %get-tuple-element.7), channel_id=1, source_target_pairs={{0,8},{8,0},{16,24},{24,16},{32,40},{40,32},{48,56},{56,48},{64,72... | collective-permute-start | bytes 393224 | tf_op jit(solution)/shard_map/ppermute | solution.py:24
  36.8 9.2 %all-to-all-done = bf16[16,2,4096]{2,1,0:T(2,128)(2,1)S(1)} async-done(((bf16[16,2,4096]{2,1,0:T(2,128)(2,1)}), bf16[16,2,4096]{2,1,0:T(2,128)(2,1)S(1)}, u32[]{:S(2)}, u32[]{:S(2)}) %all-to-all-start) | async-done | bytes 262176 | tf_op jit(solution)/shard_map/all_to_all | solution.py:16
  46.1 4.6 %collective-permute-start.4 = (bf16[32,4096]{1,0:T(8,128)(2,1)S(1)}, bf16[32,4096]{1,0:T(8,128)(2,1)S(1)}, u32[]{:S(2)}, u32[]{:S(2)}) collective-permute-start(bf16[32,4096]{1,0:T(8,128)(2,1)S(1)} %reshape.92), channel_id=1, source_target_pairs={{0,24},{8,16},{16,8},{24,0},{32,56},{40,48},{48,40},{56,32},{64,88... | collective-permute-start | bytes 786440 | tf_op jit(solution)/shard_map/ppermute | solution.py:24
  51.0 3.5 %collective-permute-done.4 = bf16[32,4096]{1,0:T(8,128)(2,1)S(1)} collective-permute-done((bf16[32,4096]{1,0:T(8,128)(2,1)S(1)}, bf16[32,4096]{1,0:T(8,128)(2,1)S(1)}, u32[]{:S(2)}, u32[]{:S(2)}) %collective-permute-start.4) | collective-permute-done | bytes 262176 | tf_op jit(solution)/shard_map/ppermute | solution.py:24
  54.8 0.6 broadcast_in_dim.15
  55.4 14.5 %all-to-all-start.1 = ((f32[32,2,32]{2,1,0:T(2,128)}), f32[32,2,32]{2,1,0:T(2,128)S(1)}, u32[]{:S(2)}, u32[]{:S(2)}) async-start(f32[32,2,32]{2,1,0:T(2,128)} %broadcast_in_dim.15), calls=%async_computation.1 | async-start | bytes 65536 | tf_op jit(solution)/shard_map/all_to_all | solution.py:16
  70.4 13.0 %all-to-all-done.1 = f32[32,2,32]{2,1,0:T(2,128)S(1)} async-done(((f32[32,2,32]{2,1,0:T(2,128)}), f32[32,2,32]{2,1,0:T(2,128)S(1)}, u32[]{:S(2)}, u32[]{:S(2)}) %all-to-all-start.1) | async-done | bytes 8224 | tf_op jit(solution)/shard_map/all_to_all | solution.py:16
  83.4 0.3 fusion.8
  83.7 0.3 fusion
  84.0 0.9 reshape.94
  84.9 7.1 %all-to-all-start.2 = ((bf16[16,2,4096]{2,1,0:T(2,128)(2,1)}), bf16[16,2,4096]{2,1,0:T(2,128)(2,1)S(1)}, u32[]{:S(2)}, u32[]{:S(2)}) async-start(bf16[16,2,4096]{2,1,0:T(2,128)(2,1)} %reshape.94), calls=%async_computation.2 | async-start | bytes 524288 | tf_op jit(solution)/shard_map/all_to_all | solution.py:100
  92.1 7.1 %all-to-all-done.2 = bf16[16,2,4096]{2,1,0:T(2,128)(2,1)S(1)} async-done(((bf16[16,2,4096]{2,1,0:T(2,128)(2,1)}), bf16[16,2,4096]{2,1,0:T(2,128)(2,1)S(1)}, u32[]{:S(2)}, u32[]{:S(2)}) %all-to-all-start.2) | async-done | bytes 262176 | tf_op jit(solution)/shard_map/all_to_all | solution.py:100
  99.8 8.5 %all_to_all.20 = bf16[8,2,4096]{2,1,0:T(2,128)(2,1)S(1)} all-to-all(bf16[8,2,4096]{2,1,0:T(2,128)(2,1)S(1)} %broadcast_in_dim.16), channel_id=1, replica_groups=mesh['dp'=64,'seq'=8] {'seq'}, dimensions={0} | all-to-all | bytes 262144 | tf_op jit(solution)/shard_map/all_to_all | solution.py:16
  108.3 1.5 %convolution_convert_fusion = bf16[128,4096]{1,0:T(8,128)(2,1)} fusion(bf16[16,4096]{1,0:T(8,128)(2,1)S(1)} %reshape.95, s32[128]{0:T(128)S(1)} %iota_add_fusion.1, s32[16]{0:T(128)S(1)} %multiply_reduce_fusion.2, s32[16]{0:T(128)S(1)} %fusion.33), kind=kOutput, calls=%fused_computation | convolution fusion | flops 17307648 | bytes 1180288 | tf_op jit(solution)/shard_map/dot_general | solution.py:111
  (38 shorter events, 2.6 us)
Async XLA Ops:
  0.0 1.5 %copy-start = (bf16[128,4096]{1,0:T(8,128)(2,1)S(1)}, bf16[128,4096]{1,0:T(8,128)(2,1)}, u32[]{:S(2)}) copy-start(bf16[128,4096]{1,0:T(8,128)(2,1)} %param.4) | copy-start | bytes 3145732
  0.0 10.6 %copy-start.1 = (bf16[2,4096]{1,0:T(2,128)(2,1)S(1)}, bf16[2,4096]{1,0:T(2,128)(2,1)}, u32[]{:S(2)}) copy-start(bf16[2,4096]{1,0:T(2,128)(2,1)} %param.6) | copy-start | bytes 49156
  1.8 9.7 %collective-permute-start = (bf16[16,4096]{1,0:T(8,128)(2,1)S(1)}, bf16[16,4096]{1,0:T(8,128)(2,1)S(1)}, u32[]{:S(2)}, u32[]{:S(2)}) collective-permute-start(bf16[16,4096]{1,0:T(8,128)(2,1)S(1)} %get-tuple-element.19), channel_id=1, source_target_pairs={{0,1},{1,0},{2,3},{3,2},{4,5},{5,4},{6,7},{7,6},{8,9},{9,8},{10,11... | collective-permute-start | bytes 393224 | tf_op jit(solution)/shard_map/ppermute | solution.py:20
  11.6 6.6 %collective-permute-start.1 = (bf16[16,4096]{1,0:T(8,128)(2,1)S(1)}, bf16[16,4096]{1,0:T(8,128)(2,1)S(1)}, u32[]{:S(2)}, u32[]{:S(2)}) collective-permute-start(bf16[16,4096]{1,0:T(8,128)(2,1)S(1)} %fusion.3), channel_id=1, source_target_pairs={{0,2},{1,3},{2,0},{3,1},{4,6},{5,7},{6,4},{7,5},{8,10},{9,11},{10,... | collective-permute-start | bytes 393224 | tf_op jit(solution)/shard_map/ppermute | solution.py:20
  18.3 14.9 %collective-permute-start.2 = (bf16[16,4096]{1,0:T(8,128)(2,1)S(1)}, bf16[16,4096]{1,0:T(8,128)(2,1)S(1)}, u32[]{:S(2)}, u32[]{:S(2)}) collective-permute-start(bf16[16,4096]{1,0:T(8,128)(2,1)S(1)} %fusion.4), channel_id=1, source_target_pairs={{0,6},{1,7},{2,4},{3,5},{4,2},{5,3},{6,0},{7,1},{8,14},{9,15},{10,... | collective-permute-start | bytes 393224 | tf_op jit(solution)/shard_map/ppermute | solution.py:20
  21.2 24.8 %all-to-all-start = ((bf16[16,2,4096]{2,1,0:T(2,128)(2,1)}), bf16[16,2,4096]{2,1,0:T(2,128)(2,1)S(1)}, u32[]{:S(2)}, u32[]{:S(2)}) async-start(bf16[16,2,4096]{2,1,0:T(2,128)(2,1)} %broadcast_in_dim.14), calls=%async_computation | async-start | bytes 524288 | tf_op jit(solution)/shard_map/all_to_all | solution.py:16
  33.6 17.2 %collective-permute-start.3 = (bf16[16,4096]{1,0:T(8,128)(2,1)S(1)}, bf16[16,4096]{1,0:T(8,128)(2,1)S(1)}, u32[]{:S(2)}, u32[]{:S(2)}) collective-permute-start(bf16[16,4096]{1,0:T(8,128)(2,1)S(1)} %get-tuple-element.7), channel_id=1, source_target_pairs={{0,8},{8,0},{16,24},{24,16},{32,40},{40,32},{48,56},{56,48},{64,72... | collective-permute-start | bytes 393224 | tf_op jit(solution)/shard_map/ppermute | solution.py:24
  46.1 23.8 %copy-start.2 = (s32[1024]{0:T(1024)S(1)}, s32[1024]{0:T(1024)}, u32[]{:S(2)}) copy-start(s32[1024]{0:T(1024)} %param.7) | copy-start | bytes 12292
  46.1 8.4 %collective-permute-start.4 = (bf16[32,4096]{1,0:T(8,128)(2,1)S(1)}, bf16[32,4096]{1,0:T(8,128)(2,1)S(1)}, u32[]{:S(2)}, u32[]{:S(2)}) collective-permute-start(bf16[32,4096]{1,0:T(8,128)(2,1)S(1)} %reshape.92), channel_id=1, source_target_pairs={{0,24},{8,16},{16,8},{24,0},{32,56},{40,48},{48,40},{56,32},{64,88... | collective-permute-start | bytes 786440 | tf_op jit(solution)/shard_map/ppermute | solution.py:24
  55.4 28.0 %all-to-all-start.1 = ((f32[32,2,32]{2,1,0:T(2,128)}), f32[32,2,32]{2,1,0:T(2,128)S(1)}, u32[]{:S(2)}, u32[]{:S(2)}) async-start(f32[32,2,32]{2,1,0:T(2,128)} %broadcast_in_dim.15), calls=%async_computation.1 | async-start | bytes 65536 | tf_op jit(solution)/shard_map/all_to_all | solution.py:16
  84.9 14.3 %all-to-all-start.2 = ((bf16[16,2,4096]{2,1,0:T(2,128)(2,1)}), bf16[16,2,4096]{2,1,0:T(2,128)(2,1)S(1)}, u32[]{:S(2)}, u32[]{:S(2)}) async-start(bf16[16,2,4096]{2,1,0:T(2,128)(2,1)} %reshape.94), calls=%async_computation.2 | async-start | bytes 524288 | tf_op jit(solution)/shard_map/all_to_all | solution.py:100

commit v5 on v4

--- a/solution.py
+++ b/solution.py
@@ -8,7 +8,9 @@
 Z, Y, S = 16, 4, 8
 Z_GROUPS = [[z * Y + y for z in range(Z)] for y in range(Y)]
 PAIRS = [[p * 2 * S + i for i in range(2 * S)] for p in range(Z * Y // 2)]
-LINES = [[z * Y + y for z in range(Z) for y in (low, 3 - low)] for low in range(2)]
+LINES = [
+    [(z + Z // 2) % Z * Y + y for z in range(Z) for y in (low, 3 - low)] for low in range(2)
+]
 
 
 def share(block, axis, count, groups=None):
@@ -52,8 +54,13 @@
         (row_pos[None, :] >= first_rows[:, None]) & (row_pos[None, :] < end_rows[:, None])
     ).astype(jnp.bfloat16)
     sums = jnp.dot(member, token_rows, preferred_element_type=jnp.float32)
-    for mask in (1, 2, 6):
-        sums = sums + swap_seq(sums.astype(jnp.bfloat16), mask).astype(jnp.float32)
+
+    def over_seq(step, sums):
+        for mask in (1, 2, 6):
+            sums = sums + swap_seq(sums.astype(jnp.bfloat16), mask).astype(jnp.float32)
+        return sums
+
+    sums = lax.fori_loop(0, jnp.minimum(lengths[0], 1), over_seq, sums)
     float_len = lengths.astype(jnp.float32)[:, None]
     pooled = sums / float_len
     inv_norm = lax.rsqrt(jnp.sum(pooled * pooled, axis=-1, keepdims=True) + 1e-06)

time: 110 us -> 97.9 us (0.89)
  waiting for transfers between devices: 38.2 us -> 22.1 us
  starting transfers between devices: 54.1 us -> 55.8 us
  other arithmetic: 2.74 us -> 4.37 us
    all_to_all x2, waiting for transfers between devices: 22.2 us -> 3.87 us  [share(): return lax.all_to_all(copies, axis, 0, 0, axis_index_groups=groups)]
    all_to_all x2, starting transfers between devices: 26.5 us -> 29.7 us  [share(): return lax.all_to_all(copies, axis, 0, 0, axis_index_groups=groups)]
    ppermute x3, starting transfers between devices: 12.6 us -> 10.4 us  [swap_seq(): return lax.ppermute(block, 'seq', [(i, i ^ mask) for i in range(S)])]
    all_to_all x1, starting transfers between devices: 7.09 us -> 8.75 us  [per_device(): lax.all_to_all(d_partial, ('dp', 'seq'), 0, 0, axis_index_groups=PAIRS)]
    ppermute x3, waiting for transfers between devices: 5.48 us -> 6.98 us  [swap_seq(): return lax.ppermute(block, 'seq', [(i, i ^ mask) for i in range(S)])]
  transfers between devices with their start and end apart: 8 -> 8, of which waited for: 6 -> 6; matrix products, arithmetic and copies ran while one was open for 2% -> 3% of each run, Pallas kernels for 0% -> 0%
where the time goes in v5:
time: 97.9 us; the launch traced here: 97.2 us
  starting transfers between devices  55.8 us (57%)
  waiting for transfers between devices  22.1 us (23%)
  blocking collectives  8.45 us (9%)
  other arithmetic  4.37 us (4%)
  local copies, waits for them, and re-layouts  3.24 us (3%)
  matrix products  2.83 us (3%)
    all_to_all x2, starting transfers between devices, share(): return lax.all_to_all(copies, axis, 0, 0, axis_index_groups=groups)  29.7 us
    ppermute x3, starting transfers between devices, swap_seq(): return lax.ppermute(block, 'seq', [(i, i ^ mask) for i in range(S)])  10.4 us
    all_to_all x1, starting transfers between devices, per_device(): lax.all_to_all(d_partial, ('dp', 'seq'), 0, 0, axis_index_groups=PAIRS)  8.75 us
    all_to_all x1, blocking collectives, share(): return lax.all_to_all(copies, axis, 0, 0, axis_index_groups=groups)  8.45 us
    all_to_all x1, waiting for transfers between devices, per_device(): lax.all_to_all(d_partial, ('dp', 'seq'), 0, 0, axis_index_groups=PAIRS)  7.03 us
    ppermute x2, starting transfers between devices, swap_y(): return lax.ppermute(block, 'dp', [(i, i ^ mask) for i in range(Z * Y)])  7.01 us
    ppermute x3, waiting for transfers between devices, swap_seq(): return lax.ppermute(block, 'seq', [(i, i ^ mask) for i in range(S)])  6.98 us
    ppermute x2, waiting for transfers between devices, swap_y(): return lax.ppermute(block, 'dp', [(i, i ^ mask) for i in range(Z * Y)])  4.23 us
  transfers between devices with their start and end apart: 8, of which 6 were waited for; matrix products, arithmetic and copies ran while one was open for 3% of the time, Pallas kernels for 0%

profile of v5, /device:TPU:1, one launch (start us, length us, event | category | flops | bytes accessed | tf_op | source)
XLA Modules:
  0.0 97.2 jit_solution(12413641948814666298)
XLA Ops:
  0.0 1.0 fusion.5
  1.0 0.8 fusion.6
  1.8 0.9 broadcast_in_dim.14
  2.7 15.7 %all-to-all-start = ((bf16[16,2,4096]{2,1,0:T(2,128)(2,1)}), bf16[16,2,4096]{2,1,0:T(2,128)(2,1)S(1)}, u32[]{:S(2)}, u32[]{:S(2)}) async-start(bf16[16,2,4096]{2,1,0:T(2,128)(2,1)} %broadcast_in_dim.14), calls=%async_computation | async-start | bytes 524288 | tf_op jit(solution)/shard_map/all_to_all | solution.py:18
  18.4 0.7 bitcast_convert_fusion
  19.2 0.7 bitcast_subtract_fusion
  20.2 17.6 %while.10 = (s32[]{:T(128)}, f32[16,4096]{1,0:T(8,128)S(1)}, s32[]{:T(128)}, s32[]{:T(128)}) while((s32[]{:T(128)}, f32[16,4096]{1,0:T(8,128)S(1)}, s32[]{:T(128)}, s32[]{:T(128)}) %tuple.27), condition=%wide.region_2.3_spmd, body=%wide.region_1.2_spmd.sunk | while | flops 983042 | bytes 4063405 | solution.py:63
  20.3 2.9 %collective-permute-start = (bf16[16,4096]{1,0:T(8,128)(2,1)S(1)}, bf16[16,4096]{1,0:T(8,128)(2,1)S(1)}, u32[]{:S(2)}, u32[]{:S(2)}) collective-permute-start(bf16[16,4096]{1,0:T(8,128)(2,1)S(1)} %convert_element_type.126), channel_id=1, source_target_pairs={{0,1},{1,0},{2,3},{3,2},{4,5},{5,4},{6,7},{7,6},{8,9},{9,8},{10,11... | collective-permute-start | bytes 393224 | tf_op jit(solution)/shard_map/while/body/ppermute | solution.py:22
  23.1 1.0 collective-permute-done
  24.1 3.1 %collective-permute-start.1 = (bf16[16,4096]{1,0:T(8,128)(2,1)S(1)}, bf16[16,4096]{1,0:T(8,128)(2,1)S(1)}, u32[]{:S(2)}, u32[]{:S(2)}) collective-permute-start(bf16[16,4096]{1,0:T(8,128)(2,1)S(1)} %fusion.44), channel_id=1, source_target_pairs={{0,2},{1,3},{2,0},{3,1},{4,6},{5,7},{6,4},{7,5},{8,10},{9,11},{10,... | collective-permute-start | bytes 393224 | tf_op jit(solution)/shard_map/while/body/ppermute | solution.py:22
  27.3 3.5 %collective-permute-done.1 = bf16[16,4096]{1,0:T(8,128)(2,1)S(1)} collective-permute-done((bf16[16,4096]{1,0:T(8,128)(2,1)S(1)}, bf16[16,4096]{1,0:T(8,128)(2,1)S(1)}, u32[]{:S(2)}, u32[]{:S(2)}) %collective-permute-start.1) | collective-permute-done | bytes 131104 | tf_op jit(solution)/shard_map/while/body/ppermute | solution.py:22
  30.8 4.4 %collective-permute-start.2 = (bf16[16,4096]{1,0:T(8,128)(2,1)S(1)}, bf16[16,4096]{1,0:T(8,128)(2,1)S(1)}, u32[]{:S(2)}, u32[]{:S(2)}) collective-permute-start(bf16[16,4096]{1,0:T(8,128)(2,1)S(1)} %fusion.45), channel_id=1, source_target_pairs={{0,6},{1,7},{2,4},{3,5},{4,2},{5,3},{6,0},{7,1},{8,14},{9,15},{10,... | collective-permute-start | bytes 393224 | tf_op jit(solution)/shard_map/while/body/ppermute | solution.py:22
  35.2 2.5 %collective-permute-done.2 = bf16[16,4096]{1,0:T(8,128)(2,1)S(1)} collective-permute-done((bf16[16,4096]{1,0:T(8,128)(2,1)S(1)}, bf16[16,4096]{1,0:T(8,128)(2,1)S(1)}, u32[]{:S(2)}, u32[]{:S(2)}) %collective-permute-start.2) | collective-permute-done | bytes 131104 | tf_op jit(solution)/shard_map/while/body/ppermute | solution.py:22
  38.3 3.2 %collective-permute-start.3 = (bf16[16,4096]{1,0:T(8,128)(2,1)S(1)}, bf16[16,4096]{1,0:T(8,128)(2,1)S(1)}, u32[]{:S(2)}, u32[]{:S(2)}) collective-permute-start(bf16[16,4096]{1,0:T(8,128)(2,1)S(1)} %get-tuple-element.32), channel_id=1, source_target_pairs={{0,8},{8,0},{16,24},{24,16},{32,40},{40,32},{48,56},{56,48},{64,72... | collective-permute-start | bytes 393224 | tf_op jit(solution)/shard_map/ppermute | solution.py:26
  41.6 3.8 %collective-permute-start.4 = (bf16[32,4096]{1,0:T(8,128)(2,1)S(1)}, bf16[32,4096]{1,0:T(8,128)(2,1)S(1)}, u32[]{:S(2)}, u32[]{:S(2)}) collective-permute-start(bf16[32,4096]{1,0:T(8,128)(2,1)S(1)} %reshape.98), channel_id=1, source_target_pairs={{0,24},{8,16},{16,8},{24,0},{32,56},{40,48},{48,40},{56,32},{64,88... | collective-permute-start | bytes 786440 | tf_op jit(solution)/shard_map/ppermute | solution.py:26
  45.7 4.2 %collective-permute-done.4 = bf16[32,4096]{1,0:T(8,128)(2,1)S(1)} collective-permute-done((bf16[32,4096]{1,0:T(8,128)(2,1)S(1)}, bf16[32,4096]{1,0:T(8,128)(2,1)S(1)}, u32[]{:S(2)}, u32[]{:S(2)}) %collective-permute-start.4) | collective-permute-done | bytes 262176 | tf_op jit(solution)/shard_map/ppermute | solution.py:26
  50.2 0.6 broadcast_in_dim.15
  50.8 14.0 %all-to-all-start.1 = ((f32[32,2,32]{2,1,0:T(2,128)}), f32[32,2,32]{2,1,0:T(2,128)S(1)}, u32[]{:S(2)}, u32[]{:S(2)}) async-start(f32[32,2,32]{2,1,0:T(2,128)} %broadcast_in_dim.15), calls=%async_computation.1 | async-start | bytes 65536 | tf_op jit(solution)/shard_map/all_to_all | solution.py:18
  65.3 3.9 %all-to-all-done.1 = f32[32,2,32]{2,1,0:T(2,128)S(1)} async-done(((f32[32,2,32]{2,1,0:T(2,128)}), f32[32,2,32]{2,1,0:T(2,128)S(1)}, u32[]{:S(2)}, u32[]{:S(2)}) %all-to-all-start.1) | async-done | bytes 8224 | tf_op jit(solution)/shard_map/all_to_all | solution.py:18
  69.7 0.9 reshape.100
  70.6 8.8 %all-to-all-start.2 = ((bf16[16,2,4096]{2,1,0:T(2,128)(2,1)}), bf16[16,2,4096]{2,1,0:T(2,128)(2,1)S(1)}, u32[]{:S(2)}, u32[]{:S(2)}) async-start(bf16[16,2,4096]{2,1,0:T(2,128)(2,1)} %reshape.100), calls=%async_computation.2 | async-start | bytes 524288 | tf_op jit(solution)/shard_map/all_to_all | solution.py:107
  79.5 7.0 %all-to-all-done.2 = bf16[16,2,4096]{2,1,0:T(2,128)(2,1)S(1)} async-done(((bf16[16,2,4096]{2,1,0:T(2,128)(2,1)}), bf16[16,2,4096]{2,1,0:T(2,128)(2,1)S(1)}, u32[]{:S(2)}, u32[]{:S(2)}) %all-to-all-start.2) | async-done | bytes 262176 | tf_op jit(solution)/shard_map/all_to_all | solution.py:107
  87.1 8.5 %all_to_all.20 = bf16[8,2,4096]{2,1,0:T(2,128)(2,1)S(1)} all-to-all(bf16[8,2,4096]{2,1,0:T(2,128)(2,1)S(1)} %broadcast_in_dim.16), channel_id=1, replica_groups=mesh['dp'=64,'seq'=8] {'seq'}, dimensions={0} | all-to-all | bytes 262144 | tf_op jit(solution)/shard_map/all_to_all | solution.py:18
  95.6 1.5 %convolution_convert_fusion = bf16[128,4096]{1,0:T(8,128)(2,1)} fusion(bf16[16,4096]{1,0:T(8,128)(2,1)S(1)} %reshape.101, s32[128]{0:T(128)S(1)} %iota_add_fusion.1, s32[16]{0:T(128)S(1)} %multiply_reduce_fusion.2, s32[16]{0:T(128)S(1)} %bitcast_subtract_fusion), kind=kOutput, calls=%fused_computation.5 | convolution fusion | flops 17307648 | bytes 1180288 | tf_op jit(solution)/shard_map/dot_general | solution.py:118
  (39 shorter events, 3.4 us)
Async XLA Ops:
  0.0 19.9 %copy-start = (bf16[128,4096]{1,0:T(8,128)(2,1)S(1)}, bf16[128,4096]{1,0:T(8,128)(2,1)}, u32[]{:S(2)}) copy-start(bf16[128,4096]{1,0:T(8,128)(2,1)} %param.6) | copy-start | bytes 3145732
  2.7 38.8 %all-to-all-start = ((bf16[16,2,4096]{2,1,0:T(2,128)(2,1)}), bf16[16,2,4096]{2,1,0:T(2,128)(2,1)S(1)}, u32[]{:S(2)}, u32[]{:S(2)}) async-start(bf16[16,2,4096]{2,1,0:T(2,128)(2,1)} %broadcast_in_dim.14), calls=%async_computation | async-start | bytes 524288 | tf_op jit(solution)/shard_map/all_to_all | solution.py:18
  20.3 3.8 %collective-permute-start = (bf16[16,4096]{1,0:T(8,128)(2,1)S(1)}, bf16[16,4096]{1,0:T(8,128)(2,1)S(1)}, u32[]{:S(2)}, u32[]{:S(2)}) collective-permute-start(bf16[16,4096]{1,0:T(8,128)(2,1)S(1)} %convert_element_type.126), channel_id=1, source_target_pairs={{0,1},{1,0},{2,3},{3,2},{4,5},{5,4},{6,7},{7,6},{8,9},{9,8},{10,11... | collective-permute-start | bytes 393224 | tf_op jit(solution)/shard_map/while/body/ppermute | solution.py:22
  24.1 6.6 %collective-permute-start.1 = (bf16[16,4096]{1,0:T(8,128)(2,1)S(1)}, bf16[16,4096]{1,0:T(8,128)(2,1)S(1)}, u32[]{:S(2)}, u32[]{:S(2)}) collective-permute-start(bf16[16,4096]{1,0:T(8,128)(2,1)S(1)} %fusion.44), channel_id=1, source_target_pairs={{0,2},{1,3},{2,0},{3,1},{4,6},{5,7},{6,4},{7,5},{8,10},{9,11},{10,... | collective-permute-start | bytes 393224 | tf_op jit(solution)/shard_map/while/body/ppermute | solution.py:22
  30.8 6.9 %collective-permute-start.2 = (bf16[16,4096]{1,0:T(8,128)(2,1)S(1)}, bf16[16,4096]{1,0:T(8,128)(2,1)S(1)}, u32[]{:S(2)}, u32[]{:S(2)}) collective-permute-start(bf16[16,4096]{1,0:T(8,128)(2,1)S(1)} %fusion.45), channel_id=1, source_target_pairs={{0,6},{1,7},{2,4},{3,5},{4,2},{5,3},{6,0},{7,1},{8,14},{9,15},{10,... | collective-permute-start | bytes 393224 | tf_op jit(solution)/shard_map/while/body/ppermute | solution.py:22
  38.3 7.2 %collective-permute-start.3 = (bf16[16,4096]{1,0:T(8,128)(2,1)S(1)}, bf16[16,4096]{1,0:T(8,128)(2,1)S(1)}, u32[]{:S(2)}, u32[]{:S(2)}) collective-permute-start(bf16[16,4096]{1,0:T(8,128)(2,1)S(1)} %get-tuple-element.32), channel_id=1, source_target_pairs={{0,8},{8,0},{16,24},{24,16},{32,40},{40,32},{48,56},{56,48},{64,72... | collective-permute-start | bytes 393224 | tf_op jit(solution)/shard_map/ppermute | solution.py:26
  41.6 23.2 %copy-start.1 = (s32[1024]{0:T(1024)S(1)}, s32[1024]{0:T(1024)}, u32[]{:S(2)}) copy-start(s32[1024]{0:T(1024)} %param.9) | copy-start | bytes 12292
  41.6 8.3 %collective-permute-start.4 = (bf16[32,4096]{1,0:T(8,128)(2,1)S(1)}, bf16[32,4096]{1,0:T(8,128)(2,1)S(1)}, u32[]{:S(2)}, u32[]{:S(2)}) collective-permute-start(bf16[32,4096]{1,0:T(8,128)(2,1)S(1)} %reshape.98), channel_id=1, source_target_pairs={{0,24},{8,16},{16,8},{24,0},{32,56},{40,48},{48,40},{56,32},{64,88... | collective-permute-start | bytes 786440 | tf_op jit(solution)/shard_map/ppermute | solution.py:26
  50.8 18.3 %all-to-all-start.1 = ((f32[32,2,32]{2,1,0:T(2,128)}), f32[32,2,32]{2,1,0:T(2,128)S(1)}, u32[]{:S(2)}, u32[]{:S(2)}) async-start(f32[32,2,32]{2,1,0:T(2,128)} %broadcast_in_dim.15), calls=%async_computation.1 | async-start | bytes 65536 | tf_op jit(solution)/shard_map/all_to_all | solution.py:18
  70.6 15.9 %all-to-all-start.2 = ((bf16[16,2,4096]{2,1,0:T(2,128)(2,1)}), bf16[16,2,4096]{2,1,0:T(2,128)(2,1)S(1)}, u32[]{:S(2)}, u32[]{:S(2)}) async-start(bf16[16,2,4096]{2,1,0:T(2,128)(2,1)} %reshape.100), calls=%async_computation.2 | async-start | bytes 524288 | tf_op jit(solution)/shard_map/all_to_all | solution.py:107

commit v6 on v5

--- a/solution.py
+++ b/solution.py
@@ -1,6 +1,8 @@
 import jax
 import jax.numpy as jnp
 from jax import lax
+from jax.experimental import pallas as pl
+from jax.experimental.pallas import tpu as pltpu
 from jax.sharding import PartitionSpec as P
 
 loss_scale = 1048576.0
@@ -16,6 +18,24 @@
 def share(block, axis, count, groups=None):
     copies = jnp.broadcast_to(block[None], (count,) + block.shape)
     return lax.all_to_all(copies, axis, 0, 0, axis_index_groups=groups)
+
+
+def normalized_copies(queries, count):
+    def kernel(in_ref, out_ref):
+        query = in_ref[...].astype(jnp.float32)
+        scale = lax.rsqrt(jnp.sum(query * query, axis=-1, keepdims=True) + 1e-06)
+        rounded = (query * scale).astype(jnp.bfloat16)
+        for i in range(count):
+            out_ref[i] = rounded
+
+    return pl.pallas_call(
+        kernel,
+        out_shape=jax.ShapeDtypeStruct((count,) + queries.shape, jnp.bfloat16),
+        in_specs=[pl.BlockSpec(memory_space=pltpu.VMEM)],
+        out_specs=pl.BlockSpec(memory_space=pltpu.VMEM),
+        compiler_params=pltpu.CompilerParams(vmem_limit_bytes=8 << 20),
+        name="normalized_copies",
+    )(queries)
 
 
 def swap_seq(block, mask):
@@ -34,18 +54,15 @@
     dp_index = lax.axis_index("dp")
     y_index = dp_index & (Y - 1)
 
-    query_float = queries.astype(jnp.float32)
-    query_norm = (
-        query_float * lax.rsqrt(jnp.sum(query_float * query_float, axis=-1, keepdims=True) + 1e-06)
-    ).astype(jnp.bfloat16)
-    own_line = share(query_norm, "dp", Z, Z_GROUPS).reshape(Z * own, width)
-    other_line = swap_y(own_line, 3)
+    copies = normalized_copies(queries, Z)
+    own_line = lax.all_to_all(copies, "dp", 0, 0, axis_index_groups=Z_GROUPS)
+    own_line = own_line.reshape(Z * own, width)
     by_line = positive.reshape(Z, Y, S, own)
 
     def line_positive(y):
         return lax.dynamic_slice(by_line, (0, y, seq_index, 0), (Z, 1, 1, own)).reshape(-1)
 
-    lengths = extra_len[0] + 15
+    lengths = lax.optimization_barrier(extra_len[0] + 15)
     upto = jnp.tril(jnp.ones((pass_count, pass_count), jnp.int32))
     end_rows = jnp.sum(upto * lengths[None, :], axis=1)
     first_rows = end_rows - lengths
@@ -67,8 +84,10 @@
     embedding = pooled * inv_norm
 
     odd = (y_index & 1) == 1
-    embed_half = embedding.astype(jnp.bfloat16)
-    beside = swap_y(embed_half, 1)
+    embed_half, own_line = lax.optimization_barrier((embedding.astype(jnp.bfloat16), own_line))
+    own_line, other_line, beside = lax.optimization_barrier(
+        (own_line, swap_y(own_line, 3), swap_y(embed_half, 1))
+    )
     embeds = jnp.concatenate(
         [jnp.where(odd, beside, embed_half), jnp.where(odd, embed_half, beside)], axis=0
     )

time: 97.9 us -> 95.2 us (0.972)
  other arithmetic: 4.37 us -> 1.95 us
  starting transfers between devices: 55.8 us -> 54.7 us
    all_to_all x2 -> x1, starting transfers between devices: 29.7 us -> 13.7 us  [share(): return lax.all_to_all(copies, axis, 0, 0, axis_index_groups=groups)]
    all_to_all x0 -> x1, starting transfers between devices: none -> 15.7 us  [per_device(): own_line = lax.all_to_all(copies, 'dp', 0, 0, axis_index_groups=Z_GROUPS)]
    all_to_all x2 -> x1, waiting for transfers between devices: 3.87 us -> 3.87 us  [share(): return lax.all_to_all(copies, axis, 0, 0, axis_index_groups=groups)]
  transfers between devices with their start and end apart: 8 -> 8, of which waited for: 6 -> 6; matrix products, arithmetic and copies ran while one was open for 3% -> 2% of each run, Pallas kernels for 0% -> 0%
where the time goes in v6:
time: 95.2 us; the launch traced here: 94.5 us
  starting transfers between devices  54.7 us (57%)
  waiting for transfers between devices  22.2 us (23%)
  blocking collectives  8.45 us (9%)
  local copies, waits for them, and re-layouts  3.14 us (3%)
  matrix products  2.86 us (3%)
  other arithmetic  1.95 us (2%)
    all_to_all x1, starting transfers between devices, per_device(): own_line = lax.all_to_all(copies, 'dp', 0, 0, axis_index_groups=Z_GROUPS)  15.7 us
    all_to_all x1, starting transfers between devices, share(): return lax.all_to_all(copies, axis, 0, 0, axis_index_groups=groups)  13.7 us
    ppermute x3, starting transfers between devices, swap_seq(): return lax.ppermute(block, 'seq', [(i, i ^ mask) for i in range(S)])  10.4 us
    all_to_all x1, blocking collectives, share(): return lax.all_to_all(copies, axis, 0, 0, axis_index_groups=groups)  8.45 us
    all_to_all x1, starting transfers between devices, per_device(): lax.all_to_all(d_partial, ('dp', 'seq'), 0, 0, axis_index_groups=PAIRS)  8.37 us
    ppermute x3, waiting for transfers between devices, swap_seq(): return lax.ppermute(block, 'seq', [(i, i ^ mask) for i in range(S)])  7.26 us
    all_to_all x1, waiting for transfers between devices, per_device(): lax.all_to_all(d_partial, ('dp', 'seq'), 0, 0, axis_index_groups=PAIRS)  7.03 us
    ppermute x2, starting transfers between devices, swap_y(): return lax.ppermute(block, 'dp', [(i, i ^ mask) for i in range(Z * Y)])  6.56 us
  transfers between devices with their start and end apart: 8, of which 6 were waited for; matrix products, arithmetic and copies ran while one was open for 2% of the time, Pallas kernels for 0%

profile of v6, /device:TPU:1, one launch (start us, length us, event | category | flops | bytes accessed | tf_op | source)
XLA Modules:
  0.0 94.5 jit_solution(4652032953774319942)
XLA Ops:
  0.0 0.8 copy-done.1
  0.8 0.9 normalized_copies.1
  1.7 15.7 %all-to-all-start = ((bf16[16,2,4096]{2,1,0:T(2,128)(2,1)}), bf16[16,2,4096]{2,1,0:T(2,128)(2,1)S(1)}, u32[]{:S(2)}, u32[]{:S(2)}) async-start(bf16[16,2,4096]{2,1,0:T(2,128)(2,1)} %normalized_copies.1), calls=%async_computation | async-start | bytes 524288 | tf_op jit(solution)/shard_map/all_to_all | solution.py:58
  17.4 0.7 add_bitcast_fusion
  18.3 0.3 fusion.15
  18.6 17.9 %while.10 = (s32[]{:T(128)}, f32[16,4096]{1,0:T(8,128)S(1)}, s32[]{:T(128)}, s32[]{:T(128)}) while((s32[]{:T(128)}, f32[16,4096]{1,0:T(8,128)S(1)}, s32[]{:T(128)}, s32[]{:T(128)}) %tuple.30), condition=%wide.region_2.3_spmd, body=%wide.region_1.2_spmd.sunk | while | flops 983042 | bytes 4063405 | solution.py:80
  18.6 2.9 %collective-permute-start = (bf16[16,4096]{1,0:T(8,128)(2,1)S(1)}, bf16[16,4096]{1,0:T(8,128)(2,1)S(1)}, u32[]{:S(2)}, u32[]{:S(2)}) collective-permute-start(bf16[16,4096]{1,0:T(8,128)(2,1)S(1)} %convert_element_type.107), channel_id=1, source_target_pairs={{0,1},{1,0},{2,3},{3,2},{4,5},{5,4},{6,7},{7,6},{8,9},{9,8},{10,11... | collective-permute-start | bytes 393224 | tf_op jit(solution)/shard_map/while/body/ppermute | solution.py:42
  21.5 1.0 %collective-permute-done = bf16[16,4096]{1,0:T(8,128)(2,1)S(1)} collective-permute-done((bf16[16,4096]{1,0:T(8,128)(2,1)S(1)}, bf16[16,4096]{1,0:T(8,128)(2,1)S(1)}, u32[]{:S(2)}, u32[]{:S(2)}) %collective-permute-start) | collective-permute-done | bytes 131104 | tf_op jit(solution)/shard_map/while/body/ppermute | solution.py:42
  22.5 3.1 %collective-permute-start.1 = (bf16[16,4096]{1,0:T(8,128)(2,1)S(1)}, bf16[16,4096]{1,0:T(8,128)(2,1)S(1)}, u32[]{:S(2)}, u32[]{:S(2)}) collective-permute-start(bf16[16,4096]{1,0:T(8,128)(2,1)S(1)} %fusion.42), channel_id=1, source_target_pairs={{0,2},{1,3},{2,0},{3,1},{4,6},{5,7},{6,4},{7,5},{8,10},{9,11},{10,... | collective-permute-start | bytes 393224 | tf_op jit(solution)/shard_map/while/body/ppermute | solution.py:42
  25.6 3.5 %collective-permute-done.1 = bf16[16,4096]{1,0:T(8,128)(2,1)S(1)} collective-permute-done((bf16[16,4096]{1,0:T(8,128)(2,1)S(1)}, bf16[16,4096]{1,0:T(8,128)(2,1)S(1)}, u32[]{:S(2)}, u32[]{:S(2)}) %collective-permute-start.1) | collective-permute-done | bytes 131104 | tf_op jit(solution)/shard_map/while/body/ppermute | solution.py:42
  29.1 4.4 %collective-permute-start.2 = (bf16[16,4096]{1,0:T(8,128)(2,1)S(1)}, bf16[16,4096]{1,0:T(8,128)(2,1)S(1)}, u32[]{:S(2)}, u32[]{:S(2)}) collective-permute-start(bf16[16,4096]{1,0:T(8,128)(2,1)S(1)} %fusion.43), channel_id=1, source_target_pairs={{0,6},{1,7},{2,4},{3,5},{4,2},{5,3},{6,0},{7,1},{8,14},{9,15},{10,... | collective-permute-start | bytes 393224 | tf_op jit(solution)/shard_map/while/body/ppermute | solution.py:42
  33.5 2.8 %collective-permute-done.2 = bf16[16,4096]{1,0:T(8,128)(2,1)S(1)} collective-permute-done((bf16[16,4096]{1,0:T(8,128)(2,1)S(1)}, bf16[16,4096]{1,0:T(8,128)(2,1)S(1)}, u32[]{:S(2)}, u32[]{:S(2)}) %collective-permute-start.2) | collective-permute-done | bytes 131104 | tf_op jit(solution)/shard_map/while/body/ppermute | solution.py:42
  37.0 4.6 %collective-permute-start.3 = (bf16[32,4096]{1,0:T(8,128)(2,1)S(1)}, bf16[32,4096]{1,0:T(8,128)(2,1)S(1)}, u32[]{:S(2)}, u32[]{:S(2)}) collective-permute-start(bf16[32,4096]{1,0:T(8,128)(2,1)S(1)} %reshape.78), channel_id=1, source_target_pairs={{0,24},{8,16},{16,8},{24,0},{32,56},{40,48},{48,40},{56,32},{64,88... | collective-permute-start | bytes 786440 | tf_op jit(solution)/shard_map/ppermute | solution.py:46
  41.7 1.9 %collective-permute-start.4 = (bf16[16,4096]{1,0:T(8,128)(2,1)S(1)}, bf16[16,4096]{1,0:T(8,128)(2,1)S(1)}, u32[]{:S(2)}, u32[]{:S(2)}) collective-permute-start(bf16[16,4096]{1,0:T(8,128)(2,1)S(1)} %get-tuple-element.30), channel_id=1, source_target_pairs={{0,8},{8,0},{16,24},{24,16},{32,40},{40,32},{48,56},{56,48},{64,72... | collective-permute-start | bytes 393224 | tf_op jit(solution)/shard_map/ppermute | solution.py:46
  43.6 4.1 %collective-permute-done.4 = bf16[16,4096]{1,0:T(8,128)(2,1)S(1)} collective-permute-done((bf16[16,4096]{1,0:T(8,128)(2,1)S(1)}, bf16[16,4096]{1,0:T(8,128)(2,1)S(1)}, u32[]{:S(2)}, u32[]{:S(2)}) %collective-permute-start.4) | collective-permute-done | bytes 131104 | tf_op jit(solution)/shard_map/ppermute | solution.py:46
  48.2 0.6 broadcast_in_dim.12
  48.8 13.7 %all-to-all-start.1 = ((f32[32,2,32]{2,1,0:T(2,128)}), f32[32,2,32]{2,1,0:T(2,128)S(1)}, u32[]{:S(2)}, u32[]{:S(2)}) async-start(f32[32,2,32]{2,1,0:T(2,128)} %broadcast_in_dim.12), calls=%async_computation.1 | async-start | bytes 65536 | tf_op jit(solution)/shard_map/all_to_all | solution.py:20
  63.0 3.9 %all-to-all-done.1 = f32[32,2,32]{2,1,0:T(2,128)S(1)} async-done(((f32[32,2,32]{2,1,0:T(2,128)}), f32[32,2,32]{2,1,0:T(2,128)S(1)}, u32[]{:S(2)}, u32[]{:S(2)}) %all-to-all-start.1) | async-done | bytes 8224 | tf_op jit(solution)/shard_map/all_to_all | solution.py:20
  67.2 0.3 fusion.2
  67.5 0.9 reshape.80
  68.4 8.4 %all-to-all-start.2 = ((bf16[16,2,4096]{2,1,0:T(2,128)(2,1)}), bf16[16,2,4096]{2,1,0:T(2,128)(2,1)S(1)}, u32[]{:S(2)}, u32[]{:S(2)}) async-start(bf16[16,2,4096]{2,1,0:T(2,128)(2,1)} %reshape.80), calls=%async_computation.2 | async-start | bytes 524288 | tf_op jit(solution)/shard_map/all_to_all | solution.py:126
  76.9 7.0 %all-to-all-done.2 = bf16[16,2,4096]{2,1,0:T(2,128)(2,1)S(1)} async-done(((bf16[16,2,4096]{2,1,0:T(2,128)(2,1)}), bf16[16,2,4096]{2,1,0:T(2,128)(2,1)S(1)}, u32[]{:S(2)}, u32[]{:S(2)}) %all-to-all-start.2) | async-done | bytes 262176 | tf_op jit(solution)/shard_map/all_to_all | solution.py:126
  84.5 8.5 %all_to_all.20 = bf16[8,2,4096]{2,1,0:T(2,128)(2,1)S(1)} all-to-all(bf16[8,2,4096]{2,1,0:T(2,128)(2,1)S(1)} %broadcast_in_dim.13), channel_id=1, replica_groups=mesh['dp'=64,'seq'=8] {'seq'}, dimensions={0} | all-to-all | bytes 262144 | tf_op jit(solution)/shard_map/all_to_all | solution.py:20
  93.0 1.5 %convolution_convert_fusion = bf16[128,4096]{1,0:T(8,128)(2,1)} fusion(bf16[16,4096]{1,0:T(8,128)(2,1)S(1)} %reshape.81, s32[128]{0:T(128)S(1)} %iota_add_fusion.1, s32[16]{0:T(128)S(1)} %multiply_reduce_fusion.2, s32[16]{0:T(128)S(1)} %get-tuple-element.51), kind=kOutput, calls=%fused_computation.5 | convolution fusion | flops 17307648 | bytes 1180288 | tf_op jit(solution)/shard_map/dot_general | solution.py:137
  (38 shorter events, 2.9 us)
Async XLA Ops:
  0.0 18.3 %copy-start = (bf16[128,4096]{1,0:T(8,128)(2,1)S(1)}, bf16[128,4096]{1,0:T(8,128)(2,1)}, u32[]{:S(2)}) copy-start(bf16[128,4096]{1,0:T(8,128)(2,1)} %param.6) | copy-start | bytes 3145732
  0.0 0.8 copy-start.1
  1.7 35.2 %all-to-all-start = ((bf16[16,2,4096]{2,1,0:T(2,128)(2,1)}), bf16[16,2,4096]{2,1,0:T(2,128)(2,1)S(1)}, u32[]{:S(2)}, u32[]{:S(2)}) async-start(bf16[16,2,4096]{2,1,0:T(2,128)(2,1)} %normalized_copies.1), calls=%async_computation | async-start | bytes 524288 | tf_op jit(solution)/shard_map/all_to_all | solution.py:58
  18.6 3.8 %collective-permute-start = (bf16[16,4096]{1,0:T(8,128)(2,1)S(1)}, bf16[16,4096]{1,0:T(8,128)(2,1)S(1)}, u32[]{:S(2)}, u32[]{:S(2)}) collective-permute-start(bf16[16,4096]{1,0:T(8,128)(2,1)S(1)} %convert_element_type.107), channel_id=1, source_target_pairs={{0,1},{1,0},{2,3},{3,2},{4,5},{5,4},{6,7},{7,6},{8,9},{9,8},{10,11... | collective-permute-start | bytes 393224 | tf_op jit(solution)/shard_map/while/body/ppermute | solution.py:42
  22.5 6.6 %collective-permute-start.1 = (bf16[16,4096]{1,0:T(8,128)(2,1)S(1)}, bf16[16,4096]{1,0:T(8,128)(2,1)S(1)}, u32[]{:S(2)}, u32[]{:S(2)}) collective-permute-start(bf16[16,4096]{1,0:T(8,128)(2,1)S(1)} %fusion.42), channel_id=1, source_target_pairs={{0,2},{1,3},{2,0},{3,1},{4,6},{5,7},{6,4},{7,5},{8,10},{9,11},{10,... | collective-permute-start | bytes 393224 | tf_op jit(solution)/shard_map/while/body/ppermute | solution.py:42
  29.1 7.2 %collective-permute-start.2 = (bf16[16,4096]{1,0:T(8,128)(2,1)S(1)}, bf16[16,4096]{1,0:T(8,128)(2,1)S(1)}, u32[]{:S(2)}, u32[]{:S(2)}) collective-permute-start(bf16[16,4096]{1,0:T(8,128)(2,1)S(1)} %fusion.43), channel_id=1, source_target_pairs={{0,6},{1,7},{2,4},{3,5},{4,2},{5,3},{6,0},{7,1},{8,14},{9,15},{10,... | collective-permute-start | bytes 393224 | tf_op jit(solution)/shard_map/while/body/ppermute | solution.py:42
  37.0 25.6 %copy-start.2 = (s32[1024]{0:T(1024)S(1)}, s32[1024]{0:T(1024)}, u32[]{:S(2)}) copy-start(s32[1024]{0:T(1024)} %param.9) | copy-start | bytes 12292
  37.0 10.7 %collective-permute-start.3 = (bf16[32,4096]{1,0:T(8,128)(2,1)S(1)}, bf16[32,4096]{1,0:T(8,128)(2,1)S(1)}, u32[]{:S(2)}, u32[]{:S(2)}) collective-permute-start(bf16[32,4096]{1,0:T(8,128)(2,1)S(1)} %reshape.78), channel_id=1, source_target_pairs={{0,24},{8,16},{16,8},{24,0},{32,56},{40,48},{48,40},{56,32},{64,88... | collective-permute-start | bytes 786440 | tf_op jit(solution)/shard_map/ppermute | solution.py:46
  41.7 6.0 %collective-permute-start.4 = (bf16[16,4096]{1,0:T(8,128)(2,1)S(1)}, bf16[16,4096]{1,0:T(8,128)(2,1)S(1)}, u32[]{:S(2)}, u32[]{:S(2)}) collective-permute-start(bf16[16,4096]{1,0:T(8,128)(2,1)S(1)} %get-tuple-element.30), channel_id=1, source_target_pairs={{0,8},{8,0},{16,24},{24,16},{32,40},{40,32},{48,56},{56,48},{64,72... | collective-permute-start | bytes 393224 | tf_op jit(solution)/shard_map/ppermute | solution.py:46
  48.8 18.0 %all-to-all-start.1 = ((f32[32,2,32]{2,1,0:T(2,128)}), f32[32,2,32]{2,1,0:T(2,128)S(1)}, u32[]{:S(2)}, u32[]{:S(2)}) async-start(f32[32,2,32]{2,1,0:T(2,128)} %broadcast_in_dim.12), calls=%async_computation.1 | async-start | bytes 65536 | tf_op jit(solution)/shard_map/all_to_all | solution.py:20
  68.4 15.6 %all-to-all-start.2 = ((bf16[16,2,4096]{2,1,0:T(2,128)(2,1)}), bf16[16,2,4096]{2,1,0:T(2,128)(2,1)S(1)}, u32[]{:S(2)}, u32[]{:S(2)}) async-start(bf16[16,2,4096]{2,1,0:T(2,128)(2,1)} %reshape.80), calls=%async_computation.2 | async-start | bytes 524288 | tf_op jit(solution)/shard_map/all_to_all | solution.py:126

commit v7 on v6

--- a/solution.py
+++ b/solution.py
@@ -36,6 +36,92 @@
         compiler_params=pltpu.CompilerParams(vmem_limit_bytes=8 << 20),
         name="normalized_copies",
     )(queries)
+
+
+def dot_rows(left, right):
+    return lax.dot_general(
+        left, right, (((1,), (1,)), ((), ())), preferred_element_type=jnp.float32
+    )
+
+
+def score(embeds, own_line, other_line, count):
+    passes, queries = embeds[0].shape[0], own_line.shape[0]
+
+    def kernel(here_ref, beside_ref, own_ref, other_ref, own_out, other_out, sums_out):
+        y_index = lax.axis_index("dp") & (Y - 1)
+        odd, high = (y_index & 1) == 1, y_index >= 2
+        embeddings = jnp.concatenate([here_ref[...], beside_ref[...]], axis=0)
+        parts = []
+        for line_ref, out_ref in ((own_ref, own_out), (other_ref, other_out)):
+            line = line_ref[...]
+            quarter = line.shape[1] // 4
+            dots = [
+                dot_rows(
+                    embeddings[:, k * quarter : (k + 1) * quarter],
+                    line[:, k * quarter : (k + 1) * quarter],
+                )
+                for k in range(4)
+            ]
+            exps = jnp.exp((dots[0] + dots[1] + dots[2] + dots[3]) * inv_temp)
+            out_ref[:passes] = jnp.where(odd, exps[passes:], exps[:passes])
+            out_ref[passes:] = jnp.where(odd, exps[:passes], exps[passes:])
+            parts.append(jnp.sum(exps, axis=0, keepdims=True))
+        first = jnp.where(high, parts[1], parts[0])
+        second = jnp.where(high, parts[0], parts[1])
+        row = lax.broadcasted_iota(jnp.int32, (2, queries), 0)
+        both = jnp.where(row == 0, first, second)
+        sums_out[...] = jnp.broadcast_to(both[None], sums_out.shape)
+
+    vmem = pl.BlockSpec(memory_space=pltpu.VMEM)
+    exps = jax.ShapeDtypeStruct((2 * passes, queries), jnp.float32)
+    return pl.pallas_call(
+        kernel,
+        out_shape=(exps, exps, jax.ShapeDtypeStruct((count, 2, queries), jnp.float32)),
+        in_specs=[vmem] * 4,
+        out_specs=(vmem, vmem, vmem),
+        compiler_params=pltpu.CompilerParams(vmem_limit_bytes=16 << 20),
+        name="score",
+    )(*embeds, own_line, other_line)
+
+
+def gradients(own_exp, other_exp, part_totals, own_line, other_line, own_at, other_at, factor):
+    passes, queries = own_exp.shape
+    width = own_line.shape[1] // S
+
+    def kernel(
+        own_exp_ref, other_exp_ref, totals_ref, own_ref, other_ref, own_at_ref, other_at_ref, out_ref
+    ):
+        dp_index = lax.axis_index("dp")
+        high = (dp_index & (Y - 1)) >= 2
+        totals = jnp.sum(totals_ref[...], axis=0)
+        low_total, high_total = totals[0:1], totals[1:2]
+        passage = lax.broadcasted_iota(jnp.int32, (passes, queries), 0)
+        passage += (dp_index - (dp_index & 1)) * (passes // 2)
+
+        def coefficients(exp_ref, total, at_ref):
+            target = (passage == at_ref[...]).astype(jnp.float32)
+            return ((exp_ref[...] / total - target) * factor).astype(jnp.bfloat16)
+
+        own = coefficients(own_exp_ref, jnp.where(high, high_total, low_total), own_at_ref)
+        other = coefficients(other_exp_ref, jnp.where(high, low_total, high_total), other_at_ref)
+        for part in range(S):
+            columns = pl.ds(part * width, width)
+            block = jnp.dot(
+                own, own_ref[:, columns], preferred_element_type=jnp.float32
+            ) + jnp.dot(other, other_ref[:, columns], preferred_element_type=jnp.float32)
+            block = block.astype(jnp.bfloat16)
+            out_ref[part] = block[: passes // 2]
+            out_ref[S + part] = block[passes // 2 :]
+
+    vmem = pl.BlockSpec(memory_space=pltpu.VMEM)
+    return pl.pallas_call(
+        kernel,
+        out_shape=jax.ShapeDtypeStruct((2 * S, passes // 2, width), jnp.bfloat16),
+        in_specs=[vmem] * 7,
+        out_specs=vmem,
+        compiler_params=pltpu.CompilerParams(vmem_limit_bytes=16 << 20),
+        name="gradients",
+    )(own_exp, other_exp, part_totals, own_line, other_line, own_at, other_at)
 
 
 def swap_seq(block, mask):
@@ -83,57 +169,31 @@
     inv_norm = lax.rsqrt(jnp.sum(pooled * pooled, axis=-1, keepdims=True) + 1e-06)
     embedding = pooled * inv_norm
 
-    odd = (y_index & 1) == 1
     embed_half, own_line = lax.optimization_barrier((embedding.astype(jnp.bfloat16), own_line))
     own_line, other_line, beside = lax.optimization_barrier(
         (own_line, swap_y(own_line, 3), swap_y(embed_half, 1))
     )
-    embeds = jnp.concatenate(
-        [jnp.where(odd, beside, embed_half), jnp.where(odd, embed_half, beside)], axis=0
-    )
-
-    def exp_scores(line):
-        return jnp.exp(
-            lax.dot_general(
-                embeds, line, (((1,), (1,)), ((), ())), preferred_element_type=jnp.float32
-            )
-            * inv_temp
-        )
-
-    own_exp, other_exp = exp_scores(own_line), exp_scores(other_line)
-    own_part, other_part = jnp.sum(own_exp, axis=0), jnp.sum(other_exp, axis=0)
-    high = y_index >= 2
-    parts = jnp.stack([jnp.where(high, other_part, own_part), jnp.where(high, own_part, other_part)])
-    totals = jnp.sum(share(parts, "dp", 2 * Z, LINES), axis=0)
-    own_total = jnp.where(high, totals[1], totals[0])
-    other_total = jnp.where(high, totals[0], totals[1])
-    pass_ids = (dp_index - (y_index & 1)) * pass_count + jnp.arange(2 * pass_count, dtype=jnp.int32)
-    factor = loss_scale * inv_temp / positive.shape[0]
-
-    def coefficients(exps, total, y):
-        target = (pass_ids[:, None] == line_positive(y)[None, :]).astype(jnp.float32)
-        return ((exps / total[None, :] - target) * factor).astype(jnp.bfloat16)
-
-    slots = pass_count // S
-    d_partial = jnp.dot(
-        coefficients(own_exp, own_total, y_index), own_line, preferred_element_type=jnp.float32
-    ) + jnp.dot(
-        coefficients(other_exp, other_total, 3 - y_index),
+    own_exp, other_exp, parts = score((embed_half, beside), own_line, other_line, 2 * Z)
+    part_totals = lax.all_to_all(parts, "dp", 0, 0, axis_index_groups=LINES)
+
+    d_partial = gradients(
+        own_exp,
+        other_exp,
+        part_totals,
+        own_line,
         other_line,
-        preferred_element_type=jnp.float32,
-    )
-    d_partial = d_partial.astype(jnp.bfloat16).reshape(2 * S, slots, width)
+        line_positive(y_index)[None, :],
+        line_positive(3 - y_index)[None, :],
+        loss_scale * inv_temp / positive.shape[0],
+    )
     d_parts = lax.all_to_all(d_partial, ("dp", "seq"), 0, 0, axis_index_groups=PAIRS)
-    d_embed = jnp.sum(d_parts.astype(jnp.float32), axis=0)
-    first = seq_index * slots
-    own_embedding = lax.dynamic_slice_in_dim(embedding, first, slots, 0)
-    own_norm = lax.dynamic_slice_in_dim(inv_norm, first, slots, 0)
-    own_len = lax.dynamic_slice_in_dim(float_len, first, slots, 0)
-    d_pooled = own_norm * (
-        d_embed - own_embedding * jnp.sum(own_embedding * d_embed, axis=-1, keepdims=True)
-    )
-    d_sum = (d_pooled / own_len).astype(jnp.bfloat16)
-    every_d_sum = share(d_sum, "seq", S).reshape(pass_count, width)
+    d_own = jnp.sum(d_parts.astype(jnp.float32), axis=0).astype(jnp.bfloat16)
+    d_embed = share(d_own, "seq", S).transpose(1, 0, 2).reshape(pass_count, width)
+    d_embed = d_embed.astype(jnp.float32)
+    d_pooled = inv_norm * (
+        d_embed - embedding * jnp.sum(embedding * d_embed, axis=-1, keepdims=True)
+    )
+    every_d_sum = (d_pooled / float_len).astype(jnp.bfloat16)
     grads = lax.dot_general(
         member, every_d_sum, (((0,), (0,)), ((), ())), preferred_element_type=jnp.float32
     )

time: 95.2 us -> 93.2 us (0.979)
  blocking collectives: 8.45 us -> 23.8 us
  starting transfers between devices: 54.7 us -> 46.4 us
  waiting for transfers between devices: 22.2 us -> 15.2 us
  local copies, waits for them, and re-layouts: 3.14 us -> 1.38 us
  Pallas kernels: 0.86 us -> 2.1 us
  matrix products: 2.86 us -> 1.83 us
    all_to_all x0 -> x1, blocking collectives: none -> 15.3 us  [per_device(): lax.all_to_all(d_partial, ('dp', 'seq'), 0, 0, axis_index_groups=PAIRS)]
    all_to_all x2 -> x1, starting transfers between devices: 22.1 us -> 13.7 us  [per_device(): part_totals = lax.all_to_all(parts, 'dp', 0, 0, axis_index_groups=LINES)]
    all_to_all x2 -> x1, waiting for transfers between devices: 10.9 us -> 3.88 us  [per_device(): part_totals = lax.all_to_all(parts, 'dp', 0, 0, axis_index_groups=LINES)]
    pallas_call x0 -> x2, Pallas kernels: none -> 1.24 us  [the longest x1 0.92 us: score(): pl.pallas_call(kernel, out_shape=(exps, exps, jax.ShapeDtypeStruct((count...]
    dot_general x4 -> x0, matrix products: 1.04 us -> none  [the longest x2 0.5 us: exp_scores(): lax.dot_general(embeds, line, (((1,), (1,)), ((), ())), preferred_element...]
  transfers between devices with their start and end apart: 8 -> 7, of which waited for: 6 -> 5; matrix products, arithmetic and copies ran while one was open for 2% -> 2% of each run, Pallas kernels for 0% -> 0%
where the time goes in v7:
time: 93.2 us; the launch traced here: 92.6 us
  starting transfers between devices  46.4 us (50%)
  blocking collectives  23.8 us (26%)
  waiting for transfers between devices  15.2 us (16%)
  Pallas kernels  2.1 us (2%)
  matrix products  1.83 us (2%)
  other arithmetic  1.67 us (2%)
  local copies, waits for them, and re-layouts  1.38 us (1%)
    all_to_all x1, starting transfers between devices, per_device(): own_line = lax.all_to_all(copies, 'dp', 0, 0, axis_index_groups=Z_GROUPS)  15.7 us
    all_to_all x1, blocking collectives, per_device(): lax.all_to_all(d_partial, ('dp', 'seq'), 0, 0, axis_index_groups=PAIRS)  15.3 us
    all_to_all x1, starting transfers between devices, per_device(): part_totals = lax.all_to_all(parts, 'dp', 0, 0, axis_index_groups=LINES)  13.7 us
    ppermute x3, starting transfers between devices, swap_seq(): return lax.ppermute(block, 'seq', [(i, i ^ mask) for i in range(S)])  10.4 us
    all_to_all x1, blocking collectives, share(): return lax.all_to_all(copies, axis, 0, 0, axis_index_groups=groups)  8.45 us
    ppermute x3, waiting for transfers between devices, swap_seq(): return lax.ppermute(block, 'seq', [(i, i ^ mask) for i in range(S)])  7.26 us
    ppermute x2, starting transfers between devices, swap_y(): return lax.ppermute(block, 'dp', [(i, i ^ mask) for i in range(Z * Y)])  6.56 us
    ppermute x2, waiting for transfers between devices, swap_y(): return lax.ppermute(block, 'dp', [(i, i ^ mask) for i in range(Z * Y)])  4.08 us
  transfers between devices with their start and end apart: 7, of which 5 were waited for; matrix products, arithmetic and copies ran while one was open for 2% of the time, Pallas kernels for 0%

profile of v7, /device:TPU:1, one launch (start us, length us, event | category | flops | bytes accessed | tf_op | source)
XLA Modules:
  0.0 92.6 jit_solution(16543441039826740851)
XLA Ops:
  0.0 0.8 copy-done.1
  0.8 0.9 normalized_copies.1
  1.7 15.7 %all-to-all-start = ((bf16[16,2,4096]{2,1,0:T(2,128)(2,1)}), bf16[16,2,4096]{2,1,0:T(2,128)(2,1)S(1)}, u32[]{:S(2)}, u32[]{:S(2)}) async-start(bf16[16,2,4096]{2,1,0:T(2,128)(2,1)} %normalized_copies.1), calls=%async_computation | async-start | bytes 524288 | tf_op jit(solution)/shard_map/all_to_all | solution.py:144
  17.4 0.7 add_bitcast_fusion
  18.3 0.3 fusion.5
  18.6 17.9 %while.10 = (s32[]{:T(128)}, f32[16,4096]{1,0:T(8,128)S(1)}, s32[]{:T(128)}, s32[]{:T(128)}) while((s32[]{:T(128)}, f32[16,4096]{1,0:T(8,128)S(1)}, s32[]{:T(128)}, s32[]{:T(128)}) %tuple.24), condition=%wide.region_2.3_spmd, body=%wide.region_1.2_spmd.sunk | while | flops 983042 | bytes 4063405 | solution.py:166
  18.6 2.9 %collective-permute-start = (bf16[16,4096]{1,0:T(8,128)(2,1)S(1)}, bf16[16,4096]{1,0:T(8,128)(2,1)S(1)}, u32[]{:S(2)}, u32[]{:S(2)}) collective-permute-start(bf16[16,4096]{1,0:T(8,128)(2,1)S(1)} %convert_element_type.91), channel_id=1, source_target_pairs={{0,1},{1,0},{2,3},{3,2},{4,5},{5,4},{6,7},{7,6},{8,9},{9,8},{10,11... | collective-permute-start | bytes 393224 | tf_op jit(solution)/shard_map/while/body/ppermute | solution.py:128
  21.5 1.0 %collective-permute-done = bf16[16,4096]{1,0:T(8,128)(2,1)S(1)} collective-permute-done((bf16[16,4096]{1,0:T(8,128)(2,1)S(1)}, bf16[16,4096]{1,0:T(8,128)(2,1)S(1)}, u32[]{:S(2)}, u32[]{:S(2)}) %collective-permute-start) | collective-permute-done | bytes 131104 | tf_op jit(solution)/shard_map/while/body/ppermute | solution.py:128
  22.5 3.1 %collective-permute-start.1 = (bf16[16,4096]{1,0:T(8,128)(2,1)S(1)}, bf16[16,4096]{1,0:T(8,128)(2,1)S(1)}, u32[]{:S(2)}, u32[]{:S(2)}) collective-permute-start(bf16[16,4096]{1,0:T(8,128)(2,1)S(1)} %fusion.16), channel_id=1, source_target_pairs={{0,2},{1,3},{2,0},{3,1},{4,6},{5,7},{6,4},{7,5},{8,10},{9,11},{10,... | collective-permute-start | bytes 393224 | tf_op jit(solution)/shard_map/while/body/ppermute | solution.py:128
  25.6 3.5 %collective-permute-done.1 = bf16[16,4096]{1,0:T(8,128)(2,1)S(1)} collective-permute-done((bf16[16,4096]{1,0:T(8,128)(2,1)S(1)}, bf16[16,4096]{1,0:T(8,128)(2,1)S(1)}, u32[]{:S(2)}, u32[]{:S(2)}) %collective-permute-start.1) | collective-permute-done | bytes 131104 | tf_op jit(solution)/shard_map/while/body/ppermute | solution.py:128
  29.1 4.4 %collective-permute-start.2 = (bf16[16,4096]{1,0:T(8,128)(2,1)S(1)}, bf16[16,4096]{1,0:T(8,128)(2,1)S(1)}, u32[]{:S(2)}, u32[]{:S(2)}) collective-permute-start(bf16[16,4096]{1,0:T(8,128)(2,1)S(1)} %fusion.17), channel_id=1, source_target_pairs={{0,6},{1,7},{2,4},{3,5},{4,2},{5,3},{6,0},{7,1},{8,14},{9,15},{10,... | collective-permute-start | bytes 393224 | tf_op jit(solution)/shard_map/while/body/ppermute | solution.py:128
  33.5 2.8 %collective-permute-done.2 = bf16[16,4096]{1,0:T(8,128)(2,1)S(1)} collective-permute-done((bf16[16,4096]{1,0:T(8,128)(2,1)S(1)}, bf16[16,4096]{1,0:T(8,128)(2,1)S(1)}, u32[]{:S(2)}, u32[]{:S(2)}) %collective-permute-start.2) | collective-permute-done | bytes 131104 | tf_op jit(solution)/shard_map/while/body/ppermute | solution.py:128
  36.5 0.2 multiply_reduce_fusion.1
  37.0 4.6 %collective-permute-start.3 = (bf16[32,4096]{1,0:T(8,128)(2,1)S(1)}, bf16[32,4096]{1,0:T(8,128)(2,1)S(1)}, u32[]{:S(2)}, u32[]{:S(2)}) collective-permute-start(bf16[32,4096]{1,0:T(8,128)(2,1)S(1)} %reshape.29.own_ref), channel_id=1, source_target_pairs={{0,24},{8,16},{16,8},{24,0},{32,56},{40,48},{48,40},{56,32},{64,88... | collective-permute-start | bytes 786440 | tf_op jit(solution)/shard_map/ppermute | solution.py:132
  41.6 1.9 %collective-permute-start.4 = (bf16[16,4096]{1,0:T(8,128)(2,1)S(1)}, bf16[16,4096]{1,0:T(8,128)(2,1)S(1)}, u32[]{:S(2)}, u32[]{:S(2)}) collective-permute-start(bf16[16,4096]{1,0:T(8,128)(2,1)S(1)} %multiply_convert_fusion.here_ref), channel_id=1, source_target_pairs={{0,8},{8,0},{16,24},{24,16},{32,40},{40,32},{48,56},{56,48},{64,72... | collective-permute-start | bytes 393224 | tf_op jit(solution)/shard_map/ppermute | solution.py:132
  43.6 4.1 %collective-permute-done.4.beside_ref = bf16[16,4096]{1,0:T(8,128)(2,1)S(1)} collective-permute-done((bf16[16,4096]{1,0:T(8,128)(2,1)S(1)}, bf16[16,4096]{1,0:T(8,128)(2,1)S(1)}, u32[]{:S(2)}, u32[]{:S(2)}) %collective-permute-start.4) | collective-permute-done | bytes 131104 | tf_op jit(solution)/shard_map/ppermute | solution.py:132
  47.7 0.9 score.1
  48.6 13.7 %all-to-all-start.1 = ((f32[32,2,32]{2,1,0:T(2,128)}), f32[32,2,32]{2,1,0:T(2,128)S(1)}, u32[]{:S(2)}, u32[]{:S(2)}) async-start(f32[32,2,32]{2,1,0:T(2,128)} %get-tuple-element.39), calls=%async_computation.1 | async-start | bytes 65536 | tf_op jit(solution)/shard_map/all_to_all | solution.py:177
  62.7 3.9 %all-to-all-done.1.totals_ref = f32[32,2,32]{2,1,0:T(2,128)S(1)} async-done(((f32[32,2,32]{2,1,0:T(2,128)}), f32[32,2,32]{2,1,0:T(2,128)S(1)}, u32[]{:S(2)}, u32[]{:S(2)}) %all-to-all-start.1) | async-done | bytes 8224 | tf_op jit(solution)/shard_map/all_to_all | solution.py:177
  66.6 0.3 gradients.1
  66.9 15.3 %all_to_all.20 = bf16[16,16,512]{2,1,0:T(8,128)(2,1)S(1)} all-to-all(bf16[16,16,512]{2,1,0:T(8,128)(2,1)S(1)} %gradients.1), channel_id=1, replica_groups={{0,1,2,3,4,5,6,7,8,9,10,11,12,13,14,15},{16,17,18,19,20,21,22,23,24,25,..., dimensions={0} | all-to-all | bytes 524288 | tf_op jit(solution)/shard_map/all_to_all | solution.py:189
  82.3 8.5 %all_to_all.21 = bf16[8,16,512]{2,1,0:T(8,128)(2,1)S(1)} all-to-all(bf16[8,16,512]{2,1,0:T(8,128)(2,1)S(1)} %broadcast_in_dim.10), channel_id=1, replica_groups=mesh['dp'=64,'seq'=8] {'seq'}, dimensions={0} | all-to-all | bytes 262144 | tf_op jit(solution)/shard_map/all_to_all | solution.py:20
  90.8 0.2 multiply_reduce_fusion
  91.1 1.5 %convolution_convert_fusion = bf16[128,4096]{1,0:T(8,128)(2,1)} fusion(f32[16,4096]{1,0:T(8,128)S(1)} %bitcast.10, f32[16]{0:T(128)S(1)} %multiply_reduce_fusion, f32[16]{0:T(128)S(1)} %add_rsqrt_fusion, f32[16]{0:T(128)S(1)} %get-tuple-element.48, s32[128]{0:T(128)S(1)} %iota_add_fusion, s32[16]{0:T(128)S(1)} %multiply_reduce_fusion.2, ...), kind=kOutput, calls=%fused_computation.5 | convolution fusion | flops 17766400 | bytes 1573696 | tf_op jit(solution)/shard_map/dot_general | solution.py:197
  (25 shorter events, 1.1 us)
Async XLA Ops:
  0.0 18.3 %copy-start = (bf16[128,4096]{1,0:T(8,128)(2,1)S(1)}, bf16[128,4096]{1,0:T(8,128)(2,1)}, u32[]{:S(2)}) copy-start(bf16[128,4096]{1,0:T(8,128)(2,1)} %param.6) | copy-start | bytes 3145732
  0.0 0.8 copy-start.1
  1.7 35.2 %all-to-all-start = ((bf16[16,2,4096]{2,1,0:T(2,128)(2,1)}), bf16[16,2,4096]{2,1,0:T(2,128)(2,1)S(1)}, u32[]{:S(2)}, u32[]{:S(2)}) async-start(bf16[16,2,4096]{2,1,0:T(2,128)(2,1)} %normalized_copies.1), calls=%async_computation | async-start | bytes 524288 | tf_op jit(solution)/shard_map/all_to_all | solution.py:144
  18.6 3.8 %collective-permute-start = (bf16[16,4096]{1,0:T(8,128)(2,1)S(1)}, bf16[16,4096]{1,0:T(8,128)(2,1)S(1)}, u32[]{:S(2)}, u32[]{:S(2)}) collective-permute-start(bf16[16,4096]{1,0:T(8,128)(2,1)S(1)} %convert_element_type.91), channel_id=1, source_target_pairs={{0,1},{1,0},{2,3},{3,2},{4,5},{5,4},{6,7},{7,6},{8,9},{9,8},{10,11... | collective-permute-start | bytes 393224 | tf_op jit(solution)/shard_map/while/body/ppermute | solution.py:128
  22.5 6.6 %collective-permute-start.1 = (bf16[16,4096]{1,0:T(8,128)(2,1)S(1)}, bf16[16,4096]{1,0:T(8,128)(2,1)S(1)}, u32[]{:S(2)}, u32[]{:S(2)}) collective-permute-start(bf16[16,4096]{1,0:T(8,128)(2,1)S(1)} %fusion.16), channel_id=1, source_target_pairs={{0,2},{1,3},{2,0},{3,1},{4,6},{5,7},{6,4},{7,5},{8,10},{9,11},{10,... | collective-permute-start | bytes 393224 | tf_op jit(solution)/shard_map/while/body/ppermute | solution.py:128
  29.1 7.2 %collective-permute-start.2 = (bf16[16,4096]{1,0:T(8,128)(2,1)S(1)}, bf16[16,4096]{1,0:T(8,128)(2,1)S(1)}, u32[]{:S(2)}, u32[]{:S(2)}) collective-permute-start(bf16[16,4096]{1,0:T(8,128)(2,1)S(1)} %fusion.17), channel_id=1, source_target_pairs={{0,6},{1,7},{2,4},{3,5},{4,2},{5,3},{6,0},{7,1},{8,14},{9,15},{10,... | collective-permute-start | bytes 393224 | tf_op jit(solution)/shard_map/while/body/ppermute | solution.py:128
  36.5 25.7 %copy-start.2 = (s32[1024]{0:T(1024)S(1)}, s32[1024]{0:T(1024)}, u32[]{:S(2)}) copy-start(s32[1024]{0:T(1024)} %param.9) | copy-start | bytes 12292
  37.0 10.7 %collective-permute-start.3 = (bf16[32,4096]{1,0:T(8,128)(2,1)S(1)}, bf16[32,4096]{1,0:T(8,128)(2,1)S(1)}, u32[]{:S(2)}, u32[]{:S(2)}) collective-permute-start(bf16[32,4096]{1,0:T(8,128)(2,1)S(1)} %reshape.29.own_ref), channel_id=1, source_target_pairs={{0,24},{8,16},{16,8},{24,0},{32,56},{40,48},{48,40},{56,32},{64,88... | collective-permute-start | bytes 786440 | tf_op jit(solution)/shard_map/ppermute | solution.py:132
  41.6 6.0 %collective-permute-start.4 = (bf16[16,4096]{1,0:T(8,128)(2,1)S(1)}, bf16[16,4096]{1,0:T(8,128)(2,1)S(1)}, u32[]{:S(2)}, u32[]{:S(2)}) collective-permute-start(bf16[16,4096]{1,0:T(8,128)(2,1)S(1)} %multiply_convert_fusion.here_ref), channel_id=1, source_target_pairs={{0,8},{8,0},{16,24},{24,16},{32,40},{40,32},{48,56},{56,48},{64,72... | collective-permute-start | bytes 393224 | tf_op jit(solution)/shard_map/ppermute | solution.py:132
  48.6 18.0 %all-to-all-start.1 = ((f32[32,2,32]{2,1,0:T(2,128)}), f32[32,2,32]{2,1,0:T(2,128)S(1)}, u32[]{:S(2)}, u32[]{:S(2)}) async-start(f32[32,2,32]{2,1,0:T(2,128)} %get-tuple-element.39), calls=%async_computation.1 | async-start | bytes 65536 | tf_op jit(solution)/shard_map/all_to_all | solution.py:177

commit v8 on v7

--- a/solution.py
+++ b/solution.py
@@ -8,10 +8,11 @@
 loss_scale = 1048576.0
 inv_temp = 20.0
 Z, Y, S = 16, 4, 8
-Z_GROUPS = [[z * Y + y for z in range(Z)] for y in range(Y)]
+FIRST, SECOND = 14, 8
+Z_GROUPS = [[(z + FIRST) % Z * Y + y for z in range(Z)] for y in range(Y)]
 PAIRS = [[p * 2 * S + i for i in range(2 * S)] for p in range(Z * Y // 2)]
 LINES = [
-    [(z + Z // 2) % Z * Y + y for z in range(Z) for y in (low, 3 - low)] for low in range(2)
+    [(z + SECOND) % Z * Y + y for z in range(Z) for y in (low, 3 - low)] for low in range(2)
 ]
 
 
@@ -140,15 +141,15 @@
     dp_index = lax.axis_index("dp")
     y_index = dp_index & (Y - 1)
 
+    lengths = extra_len[0] + 15
+    lengths, queries = lax.optimization_barrier((lengths, queries))
     copies = normalized_copies(queries, Z)
     own_line = lax.all_to_all(copies, "dp", 0, 0, axis_index_groups=Z_GROUPS)
-    own_line = own_line.reshape(Z * own, width)
-    by_line = positive.reshape(Z, Y, S, own)
+    by_line = jnp.roll(positive.reshape(Z, Y, S, own), -FIRST, axis=0)
 
     def line_positive(y):
         return lax.dynamic_slice(by_line, (0, y, seq_index, 0), (Z, 1, 1, own)).reshape(-1)
 
-    lengths = lax.optimization_barrier(extra_len[0] + 15)
     upto = jnp.tril(jnp.ones((pass_count, pass_count), jnp.int32))
     end_rows = jnp.sum(upto * lengths[None, :], axis=1)
     first_rows = end_rows - lengths
@@ -173,6 +174,8 @@
     own_line, other_line, beside = lax.optimization_barrier(
         (own_line, swap_y(own_line, 3), swap_y(embed_half, 1))
     )
+    own_line = own_line.reshape(Z * own, width)
+    other_line = other_line.reshape(Z * own, width)
     own_exp, other_exp, parts = score((embed_half, beside), own_line, other_line, 2 * Z)
     part_totals = lax.all_to_all(parts, "dp", 0, 0, axis_index_groups=LINES)
 

time: 93.2 us -> 91.9 us (0.986)
  starting transfers between devices: 46.4 us -> 44.9 us
  waiting for transfers between devices: 15.2 us -> 14.1 us
    all_to_all x1, starting transfers between devices: 13.7 us -> 11.7 us  [per_device(): part_totals = lax.all_to_all(parts, 'dp', 0, 0, axis_index_groups=LINES)]
    ppermute x2, waiting for transfers between devices: 4.08 us -> 3.11 us  [swap_y(): return lax.ppermute(block, 'dp', [(i, i ^ mask) for i in range(Z * Y)])]
  transfers between devices with their start and end apart: 7 -> 7, of which waited for: 5 -> 5; matrix products, arithmetic and copies ran while one was open for 2% -> 3% of each run, Pallas kernels for 0% -> 0%
where the time goes in v8:
time: 91.9 us; the launch traced here: 91.3 us
  starting transfers between devices  44.9 us (49%)
  blocking collectives  24.1 us (26%)
  waiting for transfers between devices  14.1 us (15%)
  local copies, waits for them, and re-layouts  2.23 us (2%)
  Pallas kernels  2.1 us (2%)
  other arithmetic  1.84 us (2%)
  matrix products  1.83 us (2%)
    all_to_all x1, starting transfers between devices, per_device(): own_line = lax.all_to_all(copies, 'dp', 0, 0, axis_index_groups=Z_GROUPS)  15.9 us
    all_to_all x1, blocking collectives, per_device(): lax.all_to_all(d_partial, ('dp', 'seq'), 0, 0, axis_index_groups=PAIRS)  15.7 us
    all_to_all x1, starting transfers between devices, per_device(): part_totals = lax.all_to_all(parts, 'dp', 0, 0, axis_index_groups=LINES)  11.7 us
    ppermute x3, starting transfers between devices, swap_seq(): return lax.ppermute(block, 'seq', [(i, i ^ mask) for i in range(S)])  10.6 us
    all_to_all x1, blocking collectives, share(): return lax.all_to_all(copies, axis, 0, 0, axis_index_groups=groups)  8.45 us
    ppermute x3, waiting for transfers between devices, swap_seq(): return lax.ppermute(block, 'seq', [(i, i ^ mask) for i in range(S)])  6.98 us
    ppermute x2, starting transfers between devices, swap_y(): return lax.ppermute(block, 'dp', [(i, i ^ mask) for i in range(Z * Y)])  6.56 us
    all_to_all x1, waiting for transfers between devices, per_device(): part_totals = lax.all_to_all(parts, 'dp', 0, 0, axis_index_groups=LINES)  3.98 us
  transfers between devices with their start and end apart: 7, of which 5 were waited for; matrix products, arithmetic and copies ran while one was open for 3% of the time, Pallas kernels for 0%

profile of v8, /device:TPU:1, one launch (start us, length us, event | category | flops | bytes accessed | tf_op | source)
XLA Modules:
  0.0 91.3 jit_solution(12037199410776076066)
XLA Ops:
  0.0 0.7 add_bitcast_fusion
  0.8 0.7 copy-done.1
  1.5 0.9 normalized_copies.1
  2.3 15.9 %all-to-all-start = ((bf16[16,2,4096]{2,1,0:T(2,128)(2,1)}), bf16[16,2,4096]{2,1,0:T(2,128)(2,1)S(1)}, u32[]{:S(2)}, u32[]{:S(2)}) async-start(bf16[16,2,4096]{2,1,0:T(2,128)(2,1)} %normalized_copies.1), calls=%async_computation | async-start | bytes 524288 | tf_op jit(solution)/shard_map/all_to_all | solution.py:147
  18.4 0.3 fusion.5
  18.8 17.9 %while.10 = (s32[]{:T(128)}, f32[16,4096]{1,0:T(8,128)S(1)}, s32[]{:T(128)}, s32[]{:T(128)}) while((s32[]{:T(128)}, f32[16,4096]{1,0:T(8,128)S(1)}, s32[]{:T(128)}, s32[]{:T(128)}) %tuple.26), condition=%wide.region_2.3_spmd, body=%wide.region_1.2_spmd.sunk | while | flops 983042 | bytes 4063405 | solution.py:167
  18.8 3.1 %collective-permute-start = (bf16[16,4096]{1,0:T(8,128)(2,1)S(1)}, bf16[16,4096]{1,0:T(8,128)(2,1)S(1)}, u32[]{:S(2)}, u32[]{:S(2)}) collective-permute-start(bf16[16,4096]{1,0:T(8,128)(2,1)S(1)} %convert_element_type.91), channel_id=1, source_target_pairs={{0,1},{1,0},{2,3},{3,2},{4,5},{5,4},{6,7},{7,6},{8,9},{9,8},{10,11... | collective-permute-start | bytes 393224 | tf_op jit(solution)/shard_map/while/body/ppermute | solution.py:129
  21.9 1.0 %collective-permute-done = bf16[16,4096]{1,0:T(8,128)(2,1)S(1)} collective-permute-done((bf16[16,4096]{1,0:T(8,128)(2,1)S(1)}, bf16[16,4096]{1,0:T(8,128)(2,1)S(1)}, u32[]{:S(2)}, u32[]{:S(2)}) %collective-permute-start) | collective-permute-done | bytes 131104 | tf_op jit(solution)/shard_map/while/body/ppermute | solution.py:129
  22.9 3.1 %collective-permute-start.1 = (bf16[16,4096]{1,0:T(8,128)(2,1)S(1)}, bf16[16,4096]{1,0:T(8,128)(2,1)S(1)}, u32[]{:S(2)}, u32[]{:S(2)}) collective-permute-start(bf16[16,4096]{1,0:T(8,128)(2,1)S(1)} %fusion.18), channel_id=1, source_target_pairs={{0,2},{1,3},{2,0},{3,1},{4,6},{5,7},{6,4},{7,5},{8,10},{9,11},{10,... | collective-permute-start | bytes 393224 | tf_op jit(solution)/shard_map/while/body/ppermute | solution.py:129
  26.1 3.5 %collective-permute-done.1 = bf16[16,4096]{1,0:T(8,128)(2,1)S(1)} collective-permute-done((bf16[16,4096]{1,0:T(8,128)(2,1)S(1)}, bf16[16,4096]{1,0:T(8,128)(2,1)S(1)}, u32[]{:S(2)}, u32[]{:S(2)}) %collective-permute-start.1) | collective-permute-done | bytes 131104 | tf_op jit(solution)/shard_map/while/body/ppermute | solution.py:129
  29.6 4.4 %collective-permute-start.2 = (bf16[16,4096]{1,0:T(8,128)(2,1)S(1)}, bf16[16,4096]{1,0:T(8,128)(2,1)S(1)}, u32[]{:S(2)}, u32[]{:S(2)}) collective-permute-start(bf16[16,4096]{1,0:T(8,128)(2,1)S(1)} %fusion.19), channel_id=1, source_target_pairs={{0,6},{1,7},{2,4},{3,5},{4,2},{5,3},{6,0},{7,1},{8,14},{9,15},{10,... | collective-permute-start | bytes 393224 | tf_op jit(solution)/shard_map/while/body/ppermute | solution.py:129
  34.0 2.5 %collective-permute-done.2 = bf16[16,4096]{1,0:T(8,128)(2,1)S(1)} collective-permute-done((bf16[16,4096]{1,0:T(8,128)(2,1)S(1)}, bf16[16,4096]{1,0:T(8,128)(2,1)S(1)}, u32[]{:S(2)}, u32[]{:S(2)}) %collective-permute-start.2) | collective-permute-done | bytes 131104 | tf_op jit(solution)/shard_map/while/body/ppermute | solution.py:129
  37.0 4.6 %collective-permute-start.3 = (bf16[16,2,4096]{2,1,0:T(2,128)(2,1)S(1)}, bf16[16,2,4096]{2,1,0:T(2,128)(2,1)S(1)}, u32[]{:S(2)}, u32[]{:S(2)}) collective-permute-start(bf16[16,2,4096]{2,1,0:T(2,128)(2,1)S(1)} %all-to-all-done), channel_id=1, source_target_pairs={{0,24},{8,16},{16,8},{24,0},{32,56},{40,48},{48,40},{56,32},{64,88... | collective-permute-start | bytes 786440 | tf_op jit(solution)/shard_map/ppermute | solution.py:133
  41.7 1.9 %collective-permute-start.4 = (bf16[16,4096]{1,0:T(8,128)(2,1)S(1)}, bf16[16,4096]{1,0:T(8,128)(2,1)S(1)}, u32[]{:S(2)}, u32[]{:S(2)}) collective-permute-start(bf16[16,4096]{1,0:T(8,128)(2,1)S(1)} %multiply_convert_fusion.here_ref), channel_id=1, source_target_pairs={{0,8},{8,0},{16,24},{24,16},{32,40},{40,32},{48,56},{56,48},{64,72... | collective-permute-start | bytes 393224 | tf_op jit(solution)/shard_map/ppermute | solution.py:133
  43.8 0.3 copy.11
  44.3 0.3 copy.12
  44.6 3.1 %collective-permute-done.4.beside_ref = bf16[16,4096]{1,0:T(8,128)(2,1)S(1)} collective-permute-done((bf16[16,4096]{1,0:T(8,128)(2,1)S(1)}, bf16[16,4096]{1,0:T(8,128)(2,1)S(1)}, u32[]{:S(2)}, u32[]{:S(2)}) %collective-permute-start.4) | collective-permute-done | bytes 131104 | tf_op jit(solution)/shard_map/ppermute | solution.py:133
  47.9 0.9 %score.1 = (f32[32,32]{1,0:T(8,128)S(1)}, f32[32,32]{1,0:T(8,128)S(1)}, f32[32,2,32]{2,1,0:T(2,128)}) custom-call(bf16[16,4096]{1,0:T(8,128)(2,1)S(1)} %multiply_convert_fusion.here_ref, bf16[16,4096]{1,0:T(8,128)(2,1)S(1)} %collective-permute-done.4.beside_ref, bf16[32,4096]{1,0:T(8,128)(2,1)S(1)} %reshape.48.own_ref, bf16[32,4096]{1,0:T(8,128)(2,1)S(1)} %reshape.49.other_ref), custom_call_target="tpu_custom_call" | custom-call | tf_op jit(solution)/shard_map/score/pallas_call | solution.py:78
  48.8 11.7 %all-to-all-start.1 = ((f32[32,2,32]{2,1,0:T(2,128)}), f32[32,2,32]{2,1,0:T(2,128)S(1)}, u32[]{:S(2)}, u32[]{:S(2)}) async-start(f32[32,2,32]{2,1,0:T(2,128)} %get-tuple-element.43), calls=%async_computation.1 | async-start | bytes 65536 | tf_op jit(solution)/shard_map/all_to_all | solution.py:180
  61.0 4.0 %all-to-all-done.1.totals_ref = f32[32,2,32]{2,1,0:T(2,128)S(1)} async-done(((f32[32,2,32]{2,1,0:T(2,128)}), f32[32,2,32]{2,1,0:T(2,128)S(1)}, u32[]{:S(2)}, u32[]{:S(2)}) %all-to-all-start.1) | async-done | bytes 8224 | tf_op jit(solution)/shard_map/all_to_all | solution.py:180
  65.0 0.3 gradients.1
  65.3 15.7 %all_to_all.20 = bf16[16,16,512]{2,1,0:T(8,128)(2,1)S(1)} all-to-all(bf16[16,16,512]{2,1,0:T(8,128)(2,1)S(1)} %gradients.1), channel_id=1, replica_groups={{0,1,2,3,4,5,6,7,8,9,10,11,12,13,14,15},{16,17,18,19,20,21,22,23,24,25,..., dimensions={0} | all-to-all | bytes 524288 | tf_op jit(solution)/shard_map/all_to_all | solution.py:192
  81.0 8.5 %all_to_all.21 = bf16[8,16,512]{2,1,0:T(8,128)(2,1)S(1)} all-to-all(bf16[8,16,512]{2,1,0:T(8,128)(2,1)S(1)} %broadcast_in_dim.10), channel_id=1, replica_groups=mesh['dp'=64,'seq'=8] {'seq'}, dimensions={0} | all-to-all | bytes 262144 | tf_op jit(solution)/shard_map/all_to_all | solution.py:21
  89.8 1.5 %convolution_convert_fusion = bf16[128,4096]{1,0:T(8,128)(2,1)} fusion(f32[16,4096]{1,0:T(8,128)S(1)} %bitcast.19, f32[16]{0:T(128)S(1)} %multiply_reduce_fusion, f32[16]{0:T(128)S(1)} %add_rsqrt_fusion, f32[16]{0:T(128)S(1)} %get-tuple-element.52, s32[128]{0:T(128)S(1)} %iota_add_fusion, s32[16]{0:T(128)S(1)} %multiply_reduce_fusion.2, ...), kind=kOutput, calls=%fused_computation.5 | convolution fusion | flops 17766400 | bytes 1573696 | tf_op jit(solution)/shard_map/dot_general | solution.py:200
  (32 shorter events, 2.0 us)
Async XLA Ops:
  0.0 18.4 %copy-start = (bf16[128,4096]{1,0:T(8,128)(2,1)S(1)}, bf16[128,4096]{1,0:T(8,128)(2,1)}, u32[]{:S(2)}) copy-start(bf16[128,4096]{1,0:T(8,128)(2,1)} %param.6) | copy-start | bytes 3145732
  0.7 0.7 copy-start.1
  2.3 34.7 %all-to-all-start = ((bf16[16,2,4096]{2,1,0:T(2,128)(2,1)}), bf16[16,2,4096]{2,1,0:T(2,128)(2,1)S(1)}, u32[]{:S(2)}, u32[]{:S(2)}) async-start(bf16[16,2,4096]{2,1,0:T(2,128)(2,1)} %normalized_copies.1), calls=%async_computation | async-start | bytes 524288 | tf_op jit(solution)/shard_map/all_to_all | solution.py:147
  18.8 24.9 %copy-start.2 = (s32[1024]{0:T(1024)S(1)}, s32[1024]{0:T(1024)}, u32[]{:S(2)}) copy-start(s32[1024]{0:T(1024)} %param.9) | copy-start | bytes 12292
  18.8 4.1 %collective-permute-start = (bf16[16,4096]{1,0:T(8,128)(2,1)S(1)}, bf16[16,4096]{1,0:T(8,128)(2,1)S(1)}, u32[]{:S(2)}, u32[]{:S(2)}) collective-permute-start(bf16[16,4096]{1,0:T(8,128)(2,1)S(1)} %convert_element_type.91), channel_id=1, source_target_pairs={{0,1},{1,0},{2,3},{3,2},{4,5},{5,4},{6,7},{7,6},{8,9},{9,8},{10,11... | collective-permute-start | bytes 393224 | tf_op jit(solution)/shard_map/while/body/ppermute | solution.py:129
  22.9 6.6 %collective-permute-start.1 = (bf16[16,4096]{1,0:T(8,128)(2,1)S(1)}, bf16[16,4096]{1,0:T(8,128)(2,1)S(1)}, u32[]{:S(2)}, u32[]{:S(2)}) collective-permute-start(bf16[16,4096]{1,0:T(8,128)(2,1)S(1)} %fusion.18), channel_id=1, source_target_pairs={{0,2},{1,3},{2,0},{3,1},{4,6},{5,7},{6,4},{7,5},{8,10},{9,11},{10,... | collective-permute-start | bytes 393224 | tf_op jit(solution)/shard_map/while/body/ppermute | solution.py:129
  29.6 6.9 %collective-permute-start.2 = (bf16[16,4096]{1,0:T(8,128)(2,1)S(1)}, bf16[16,4096]{1,0:T(8,128)(2,1)S(1)}, u32[]{:S(2)}, u32[]{:S(2)}) collective-permute-start(bf16[16,4096]{1,0:T(8,128)(2,1)S(1)} %fusion.19), channel_id=1, source_target_pairs={{0,6},{1,7},{2,4},{3,5},{4,2},{5,3},{6,0},{7,1},{8,14},{9,15},{10,... | collective-permute-start | bytes 393224 | tf_op jit(solution)/shard_map/while/body/ppermute | solution.py:129
  37.0 10.7 %collective-permute-start.3 = (bf16[16,2,4096]{2,1,0:T(2,128)(2,1)S(1)}, bf16[16,2,4096]{2,1,0:T(2,128)(2,1)S(1)}, u32[]{:S(2)}, u32[]{:S(2)}) collective-permute-start(bf16[16,2,4096]{2,1,0:T(2,128)(2,1)S(1)} %all-to-all-done), channel_id=1, source_target_pairs={{0,24},{8,16},{16,8},{24,0},{32,56},{40,48},{48,40},{56,32},{64,88... | collective-permute-start | bytes 786440 | tf_op jit(solution)/shard_map/ppermute | solution.py:133
  41.7 6.0 %collective-permute-start.4 = (bf16[16,4096]{1,0:T(8,128)(2,1)S(1)}, bf16[16,4096]{1,0:T(8,128)(2,1)S(1)}, u32[]{:S(2)}, u32[]{:S(2)}) collective-permute-start(bf16[16,4096]{1,0:T(8,128)(2,1)S(1)} %multiply_convert_fusion.here_ref), channel_id=1, source_target_pairs={{0,8},{8,0},{16,24},{24,16},{32,40},{40,32},{48,56},{56,48},{64,72... | collective-permute-start | bytes 393224 | tf_op jit(solution)/shard_map/ppermute | solution.py:133
  48.8 16.2 %all-to-all-start.1 = ((f32[32,2,32]{2,1,0:T(2,128)}), f32[32,2,32]{2,1,0:T(2,128)S(1)}, u32[]{:S(2)}, u32[]{:S(2)}) async-start(f32[32,2,32]{2,1,0:T(2,128)} %get-tuple-element.43), calls=%async_computation.1 | async-start | bytes 65536 | tf_op jit(solution)/shard_map/all_to_all | solution.py:180

commit v9 on v8

--- a/solution.py
+++ b/solution.py
@@ -10,7 +10,8 @@
 Z, Y, S = 16, 4, 8
 FIRST, SECOND = 14, 8
 Z_GROUPS = [[(z + FIRST) % Z * Y + y for z in range(Z)] for y in range(Y)]
-PAIRS = [[p * 2 * S + i for i in range(2 * S)] for p in range(Z * Y // 2)]
+SEQ = [(s + 4) % S for s in range(S)]
+PAIRS = [[(2 * p + i) * S + s for i in range(2) for s in SEQ] for p in range(Z * Y // 2)]
 LINES = [
     [(z + SECOND) % Z * Y + y for z in range(Z) for y in (low, 3 - low)] for low in range(2)
 ]
@@ -191,7 +192,7 @@
     )
     d_parts = lax.all_to_all(d_partial, ("dp", "seq"), 0, 0, axis_index_groups=PAIRS)
     d_own = jnp.sum(d_parts.astype(jnp.float32), axis=0).astype(jnp.bfloat16)
-    d_embed = share(d_own, "seq", S).transpose(1, 0, 2).reshape(pass_count, width)
+    d_embed = share(d_own, "seq", S, [SEQ]).transpose(1, 0, 2).reshape(pass_count, width)
     d_embed = d_embed.astype(jnp.float32)
     d_pooled = inv_norm * (
         d_embed - embedding * jnp.sum(embedding * d_embed, axis=-1, keepdims=True)

time: 91.9 us -> 89.7 us (0.976)
  blocking collectives: 24.1 us -> 21.9 us
    all_to_all x1, blocking collectives: 15.7 us -> 14.6 us  [per_device(): lax.all_to_all(d_partial, ('dp', 'seq'), 0, 0, axis_index_groups=PAIRS)]
    all_to_all x1, blocking collectives: 8.45 us -> 7.37 us  [share(): return lax.all_to_all(copies, axis, 0, 0, axis_index_groups=groups)]
where the time goes in v9:
time: 89.7 us; the launch traced here: 89.1 us
  starting transfers between devices  44.9 us (50%)
  blocking collectives  21.9 us (24%)
  waiting for transfers between devices  14.1 us (16%)
  local copies, waits for them, and re-layouts  2.23 us (2%)
  Pallas kernels  2.1 us (2%)
  other arithmetic  1.84 us (2%)
  matrix products  1.83 us (2%)
    all_to_all x1, starting transfers between devices, per_device(): own_line = lax.all_to_all(copies, 'dp', 0, 0, axis_index_groups=Z_GROUPS)  15.9 us
    all_to_all x1, blocking collectives, per_device(): lax.all_to_all(d_partial, ('dp', 'seq'), 0, 0, axis_index_groups=PAIRS)  14.6 us
    all_to_all x1, starting transfers between devices, per_device(): part_totals = lax.all_to_all(parts, 'dp', 0, 0, axis_index_groups=LINES)  11.7 us
    ppermute x3, starting transfers between devices, swap_seq(): return lax.ppermute(block, 'seq', [(i, i ^ mask) for i in range(S)])  10.7 us
    all_to_all x1, blocking collectives, share(): return lax.all_to_all(copies, axis, 0, 0, axis_index_groups=groups)  7.37 us
    ppermute x3, waiting for transfers between devices, swap_seq(): return lax.ppermute(block, 'seq', [(i, i ^ mask) for i in range(S)])  6.98 us
    ppermute x2, starting transfers between devices, swap_y(): return lax.ppermute(block, 'dp', [(i, i ^ mask) for i in range(Z * Y)])  6.56 us
    all_to_all x1, waiting for transfers between devices, per_device(): part_totals = lax.all_to_all(parts, 'dp', 0, 0, axis_index_groups=LINES)  3.98 us
  transfers between devices with their start and end apart: 7, of which 5 were waited for; matrix products, arithmetic and copies ran while one was open for 3% of the time, Pallas kernels for 0%

profile of v9, /device:TPU:1, one launch (start us, length us, event | category | flops | bytes accessed | tf_op | source)
XLA Modules:
  0.0 89.1 jit_solution(16156927682098757487)
XLA Ops:
  0.0 0.7 add_bitcast_fusion
  0.8 0.7 copy-done.1
  1.5 0.9 normalized_copies.1
  2.3 15.9 %all-to-all-start = ((bf16[16,2,4096]{2,1,0:T(2,128)(2,1)}), bf16[16,2,4096]{2,1,0:T(2,128)(2,1)S(1)}, u32[]{:S(2)}, u32[]{:S(2)}) async-start(bf16[16,2,4096]{2,1,0:T(2,128)(2,1)} %normalized_copies.1), calls=%async_computation | async-start | bytes 524288 | tf_op jit(solution)/shard_map/all_to_all | solution.py:148
  18.4 0.3 fusion.5
  18.8 17.9 %while.10 = (s32[]{:T(128)}, f32[16,4096]{1,0:T(8,128)S(1)}, s32[]{:T(128)}, s32[]{:T(128)}) while((s32[]{:T(128)}, f32[16,4096]{1,0:T(8,128)S(1)}, s32[]{:T(128)}, s32[]{:T(128)}) %tuple.26), condition=%wide.region_2.3_spmd, body=%wide.region_1.2_spmd.sunk | while | flops 983042 | bytes 4063405 | solution.py:168
  18.8 3.1 %collective-permute-start = (bf16[16,4096]{1,0:T(8,128)(2,1)S(1)}, bf16[16,4096]{1,0:T(8,128)(2,1)S(1)}, u32[]{:S(2)}, u32[]{:S(2)}) collective-permute-start(bf16[16,4096]{1,0:T(8,128)(2,1)S(1)} %convert_element_type.91), channel_id=1, source_target_pairs={{0,1},{1,0},{2,3},{3,2},{4,5},{5,4},{6,7},{7,6},{8,9},{9,8},{10,11... | collective-permute-start | bytes 393224 | tf_op jit(solution)/shard_map/while/body/ppermute | solution.py:130
  21.9 1.0 %collective-permute-done = bf16[16,4096]{1,0:T(8,128)(2,1)S(1)} collective-permute-done((bf16[16,4096]{1,0:T(8,128)(2,1)S(1)}, bf16[16,4096]{1,0:T(8,128)(2,1)S(1)}, u32[]{:S(2)}, u32[]{:S(2)}) %collective-permute-start) | collective-permute-done | bytes 131104 | tf_op jit(solution)/shard_map/while/body/ppermute | solution.py:130
  22.9 3.1 %collective-permute-start.1 = (bf16[16,4096]{1,0:T(8,128)(2,1)S(1)}, bf16[16,4096]{1,0:T(8,128)(2,1)S(1)}, u32[]{:S(2)}, u32[]{:S(2)}) collective-permute-start(bf16[16,4096]{1,0:T(8,128)(2,1)S(1)} %fusion.18), channel_id=1, source_target_pairs={{0,2},{1,3},{2,0},{3,1},{4,6},{5,7},{6,4},{7,5},{8,10},{9,11},{10,... | collective-permute-start | bytes 393224 | tf_op jit(solution)/shard_map/while/body/ppermute | solution.py:130
  26.1 3.5 %collective-permute-done.1 = bf16[16,4096]{1,0:T(8,128)(2,1)S(1)} collective-permute-done((bf16[16,4096]{1,0:T(8,128)(2,1)S(1)}, bf16[16,4096]{1,0:T(8,128)(2,1)S(1)}, u32[]{:S(2)}, u32[]{:S(2)}) %collective-permute-start.1) | collective-permute-done | bytes 131104 | tf_op jit(solution)/shard_map/while/body/ppermute | solution.py:130
  29.6 4.4 %collective-permute-start.2 = (bf16[16,4096]{1,0:T(8,128)(2,1)S(1)}, bf16[16,4096]{1,0:T(8,128)(2,1)S(1)}, u32[]{:S(2)}, u32[]{:S(2)}) collective-permute-start(bf16[16,4096]{1,0:T(8,128)(2,1)S(1)} %fusion.19), channel_id=1, source_target_pairs={{0,6},{1,7},{2,4},{3,5},{4,2},{5,3},{6,0},{7,1},{8,14},{9,15},{10,... | collective-permute-start | bytes 393224 | tf_op jit(solution)/shard_map/while/body/ppermute | solution.py:130
  34.0 2.5 %collective-permute-done.2 = bf16[16,4096]{1,0:T(8,128)(2,1)S(1)} collective-permute-done((bf16[16,4096]{1,0:T(8,128)(2,1)S(1)}, bf16[16,4096]{1,0:T(8,128)(2,1)S(1)}, u32[]{:S(2)}, u32[]{:S(2)}) %collective-permute-start.2) | collective-permute-done | bytes 131104 | tf_op jit(solution)/shard_map/while/body/ppermute | solution.py:130
  37.0 4.6 %collective-permute-start.3 = (bf16[16,2,4096]{2,1,0:T(2,128)(2,1)S(1)}, bf16[16,2,4096]{2,1,0:T(2,128)(2,1)S(1)}, u32[]{:S(2)}, u32[]{:S(2)}) collective-permute-start(bf16[16,2,4096]{2,1,0:T(2,128)(2,1)S(1)} %all-to-all-done), channel_id=1, source_target_pairs={{0,24},{8,16},{16,8},{24,0},{32,56},{40,48},{48,40},{56,32},{64,88... | collective-permute-start | bytes 786440 | tf_op jit(solution)/shard_map/ppermute | solution.py:134
  41.7 1.9 %collective-permute-start.4 = (bf16[16,4096]{1,0:T(8,128)(2,1)S(1)}, bf16[16,4096]{1,0:T(8,128)(2,1)S(1)}, u32[]{:S(2)}, u32[]{:S(2)}) collective-permute-start(bf16[16,4096]{1,0:T(8,128)(2,1)S(1)} %multiply_convert_fusion.here_ref), channel_id=1, source_target_pairs={{0,8},{8,0},{16,24},{24,16},{32,40},{40,32},{48,56},{56,48},{64,72... | collective-permute-start | bytes 393224 | tf_op jit(solution)/shard_map/ppermute | solution.py:134
  43.8 0.3 copy.11
  44.3 0.3 copy.12
  44.6 3.1 %collective-permute-done.4.beside_ref = bf16[16,4096]{1,0:T(8,128)(2,1)S(1)} collective-permute-done((bf16[16,4096]{1,0:T(8,128)(2,1)S(1)}, bf16[16,4096]{1,0:T(8,128)(2,1)S(1)}, u32[]{:S(2)}, u32[]{:S(2)}) %collective-permute-start.4) | collective-permute-done | bytes 131104 | tf_op jit(solution)/shard_map/ppermute | solution.py:134
  47.9 0.9 %score.1 = (f32[32,32]{1,0:T(8,128)S(1)}, f32[32,32]{1,0:T(8,128)S(1)}, f32[32,2,32]{2,1,0:T(2,128)}) custom-call(bf16[16,4096]{1,0:T(8,128)(2,1)S(1)} %multiply_convert_fusion.here_ref, bf16[16,4096]{1,0:T(8,128)(2,1)S(1)} %collective-permute-done.4.beside_ref, bf16[32,4096]{1,0:T(8,128)(2,1)S(1)} %reshape.48.own_ref, bf16[32,4096]{1,0:T(8,128)(2,1)S(1)} %reshape.49.other_ref), custom_call_target="tpu_custom_call" | custom-call | tf_op jit(solution)/shard_map/score/pallas_call | solution.py:79
  48.8 11.7 %all-to-all-start.1 = ((f32[32,2,32]{2,1,0:T(2,128)}), f32[32,2,32]{2,1,0:T(2,128)S(1)}, u32[]{:S(2)}, u32[]{:S(2)}) async-start(f32[32,2,32]{2,1,0:T(2,128)} %get-tuple-element.43), calls=%async_computation.1 | async-start | bytes 65536 | tf_op jit(solution)/shard_map/all_to_all | solution.py:181
  61.0 4.0 %all-to-all-done.1.totals_ref = f32[32,2,32]{2,1,0:T(2,128)S(1)} async-done(((f32[32,2,32]{2,1,0:T(2,128)}), f32[32,2,32]{2,1,0:T(2,128)S(1)}, u32[]{:S(2)}, u32[]{:S(2)}) %all-to-all-start.1) | async-done | bytes 8224 | tf_op jit(solution)/shard_map/all_to_all | solution.py:181
  65.0 0.3 gradients.1
  65.3 14.6 %all_to_all.20 = bf16[16,16,512]{2,1,0:T(8,128)(2,1)S(1)} all-to-all(bf16[16,16,512]{2,1,0:T(8,128)(2,1)S(1)} %gradients.1), channel_id=1, replica_groups={{4,5,6,7,0,1,2,3,12,13,14,15,8,9,10,11},{20,21,22,23,16,17,18,19,28,29,..., dimensions={0} | all-to-all | bytes 524288 | tf_op jit(solution)/shard_map/all_to_all | solution.py:193
  80.0 7.4 %all_to_all.21 = bf16[8,16,512]{2,1,0:T(8,128)(2,1)S(1)} all-to-all(bf16[8,16,512]{2,1,0:T(8,128)(2,1)S(1)} %broadcast_in_dim.10), channel_id=1, replica_groups={{4,5,6,7,0,1,2,3},{12,13,14,15,8,9,10,11},{20,21,22,23,16,17,18,19},{28..., dimensions={0} | all-to-all | bytes 262144 | tf_op jit(solution)/shard_map/all_to_all | solution.py:22
  87.6 1.5 %convolution_convert_fusion = bf16[128,4096]{1,0:T(8,128)(2,1)} fusion(f32[16,4096]{1,0:T(8,128)S(1)} %bitcast.19, f32[16]{0:T(128)S(1)} %multiply_reduce_fusion, f32[16]{0:T(128)S(1)} %add_rsqrt_fusion, f32[16]{0:T(128)S(1)} %get-tuple-element.52, s32[128]{0:T(128)S(1)} %iota_add_fusion, s32[16]{0:T(128)S(1)} %multiply_reduce_fusion.2, ...), kind=kOutput, calls=%fused_computation.5 | convolution fusion | flops 17766400 | bytes 1573696 | tf_op jit(solution)/shard_map/dot_general | solution.py:201
  (32 shorter events, 2.0 us)
Async XLA Ops:
  0.0 18.4 %copy-start = (bf16[128,4096]{1,0:T(8,128)(2,1)S(1)}, bf16[128,4096]{1,0:T(8,128)(2,1)}, u32[]{:S(2)}) copy-start(bf16[128,4096]{1,0:T(8,128)(2,1)} %param.6) | copy-start | bytes 3145732
  0.7 0.7 copy-start.1
  2.3 34.7 %all-to-all-start = ((bf16[16,2,4096]{2,1,0:T(2,128)(2,1)}), bf16[16,2,4096]{2,1,0:T(2,128)(2,1)S(1)}, u32[]{:S(2)}, u32[]{:S(2)}) async-start(bf16[16,2,4096]{2,1,0:T(2,128)(2,1)} %normalized_copies.1), calls=%async_computation | async-start | bytes 524288 | tf_op jit(solution)/shard_map/all_to_all | solution.py:148
  18.8 24.9 %copy-start.2 = (s32[1024]{0:T(1024)S(1)}, s32[1024]{0:T(1024)}, u32[]{:S(2)}) copy-start(s32[1024]{0:T(1024)} %param.9) | copy-start | bytes 12292
  18.8 4.1 %collective-permute-start = (bf16[16,4096]{1,0:T(8,128)(2,1)S(1)}, bf16[16,4096]{1,0:T(8,128)(2,1)S(1)}, u32[]{:S(2)}, u32[]{:S(2)}) collective-permute-start(bf16[16,4096]{1,0:T(8,128)(2,1)S(1)} %convert_element_type.91), channel_id=1, source_target_pairs={{0,1},{1,0},{2,3},{3,2},{4,5},{5,4},{6,7},{7,6},{8,9},{9,8},{10,11... | collective-permute-start | bytes 393224 | tf_op jit(solution)/shard_map/while/body/ppermute | solution.py:130
  22.9 6.6 %collective-permute-start.1 = (bf16[16,4096]{1,0:T(8,128)(2,1)S(1)}, bf16[16,4096]{1,0:T(8,128)(2,1)S(1)}, u32[]{:S(2)}, u32[]{:S(2)}) collective-permute-start(bf16[16,4096]{1,0:T(8,128)(2,1)S(1)} %fusion.18), channel_id=1, source_target_pairs={{0,2},{1,3},{2,0},{3,1},{4,6},{5,7},{6,4},{7,5},{8,10},{9,11},{10,... | collective-permute-start | bytes 393224 | tf_op jit(solution)/shard_map/while/body/ppermute | solution.py:130
  29.6 6.9 %collective-permute-start.2 = (bf16[16,4096]{1,0:T(8,128)(2,1)S(1)}, bf16[16,4096]{1,0:T(8,128)(2,1)S(1)}, u32[]{:S(2)}, u32[]{:S(2)}) collective-permute-start(bf16[16,4096]{1,0:T(8,128)(2,1)S(1)} %fusion.19), channel_id=1, source_target_pairs={{0,6},{1,7},{2,4},{3,5},{4,2},{5,3},{6,0},{7,1},{8,14},{9,15},{10,... | collective-permute-start | bytes 393224 | tf_op jit(solution)/shard_map/while/body/ppermute | solution.py:130
  37.0 10.7 %collective-permute-start.3 = (bf16[16,2,4096]{2,1,0:T(2,128)(2,1)S(1)}, bf16[16,2,4096]{2,1,0:T(2,128)(2,1)S(1)}, u32[]{:S(2)}, u32[]{:S(2)}) collective-permute-start(bf16[16,2,4096]{2,1,0:T(2,128)(2,1)S(1)} %all-to-all-done), channel_id=1, source_target_pairs={{0,24},{8,16},{16,8},{24,0},{32,56},{40,48},{48,40},{56,32},{64,88... | collective-permute-start | bytes 786440 | tf_op jit(solution)/shard_map/ppermute | solution.py:134
  41.7 6.0 %collective-permute-start.4 = (bf16[16,4096]{1,0:T(8,128)(2,1)S(1)}, bf16[16,4096]{1,0:T(8,128)(2,1)S(1)}, u32[]{:S(2)}, u32[]{:S(2)}) collective-permute-start(bf16[16,4096]{1,0:T(8,128)(2,1)S(1)} %multiply_convert_fusion.here_ref), channel_id=1, source_target_pairs={{0,8},{8,0},{16,24},{24,16},{32,40},{40,32},{48,56},{56,48},{64,72... | collective-permute-start | bytes 393224 | tf_op jit(solution)/shard_map/ppermute | solution.py:134
  48.8 16.2 %all-to-all-start.1 = ((f32[32,2,32]{2,1,0:T(2,128)}), f32[32,2,32]{2,1,0:T(2,128)S(1)}, u32[]{:S(2)}, u32[]{:S(2)}) async-start(f32[32,2,32]{2,1,0:T(2,128)} %get-tuple-element.43), calls=%async_computation.1 | async-start | bytes 65536 | tf_op jit(solution)/shard_map/all_to_all | solution.py:181

commit v10 on v9

--- a/solution.py
+++ b/solution.py
@@ -13,7 +13,7 @@
 SEQ = [(s + 4) % S for s in range(S)]
 PAIRS = [[(2 * p + i) * S + s for i in range(2) for s in SEQ] for p in range(Z * Y // 2)]
 LINES = [
-    [(z + SECOND) % Z * Y + y for z in range(Z) for y in (low, 3 - low)] for low in range(2)
+    [(z + SECOND) % Z * Y + y for z in range(Z) for y in (3 - low, low)] for low in range(2)
 ]
 
 

time: 89.7 us -> 89.5 us (level)
  waiting for transfers between devices: 14.1 us -> 12 us
  starting transfers between devices: 44.9 us -> 46.9 us
    all_to_all x1, waiting for transfers between devices: 3.98 us -> 1.87 us  [per_device(): part_totals = lax.all_to_all(parts, 'dp', 0, 0, axis_index_groups=LINES)]
    all_to_all x1, starting transfers between devices: 11.7 us -> 13.7 us  [per_device(): part_totals = lax.all_to_all(parts, 'dp', 0, 0, axis_index_groups=LINES)]
where the time goes in v10:
time: 89.5 us; the launch traced here: 89 us
  starting transfers between devices  46.9 us (52%)
  blocking collectives  21.9 us (24%)
  waiting for transfers between devices  12 us (13%)
  local copies, waits for them, and re-layouts  2.23 us (2%)
  Pallas kernels  2.1 us (2%)
  other arithmetic  1.84 us (2%)
  matrix products  1.83 us (2%)
    all_to_all x1, starting transfers between devices, per_device(): own_line = lax.all_to_all(copies, 'dp', 0, 0, axis_index_groups=Z_GROUPS)  15.9 us
    all_to_all x1, blocking collectives, per_device(): lax.all_to_all(d_partial, ('dp', 'seq'), 0, 0, axis_index_groups=PAIRS)  14.5 us
    all_to_all x1, starting transfers between devices, per_device(): part_totals = lax.all_to_all(parts, 'dp', 0, 0, axis_index_groups=LINES)  13.7 us
    ppermute x3, starting transfers between devices, swap_seq(): return lax.ppermute(block, 'seq', [(i, i ^ mask) for i in range(S)])  10.7 us
    all_to_all x1, blocking collectives, share(): return lax.all_to_all(copies, axis, 0, 0, axis_index_groups=groups)  7.37 us
    ppermute x3, waiting for transfers between devices, swap_seq(): return lax.ppermute(block, 'seq', [(i, i ^ mask) for i in range(S)])  6.98 us
    ppermute x2, starting transfers between devices, swap_y(): return lax.ppermute(block, 'dp', [(i, i ^ mask) for i in range(Z * Y)])  6.56 us
    ppermute x2, waiting for transfers between devices, swap_y(): return lax.ppermute(block, 'dp', [(i, i ^ mask) for i in range(Z * Y)])  3.11 us
  transfers between devices with their start and end apart: 7, of which 5 were waited for; matrix products, arithmetic and copies ran while one was open for 3% of the time, Pallas kernels for 0%

profile of v10, /device:TPU:1, one launch (start us, length us, event | category | flops | bytes accessed | tf_op | source)
XLA Modules:
  0.0 89.0 jit_solution(6095708956501883495)
XLA Ops:
  0.0 0.7 add_bitcast_fusion
  0.8 0.7 copy-done.1
  1.5 0.9 normalized_copies.1
  2.3 15.9 %all-to-all-start = ((bf16[16,2,4096]{2,1,0:T(2,128)(2,1)}), bf16[16,2,4096]{2,1,0:T(2,128)(2,1)S(1)}, u32[]{:S(2)}, u32[]{:S(2)}) async-start(bf16[16,2,4096]{2,1,0:T(2,128)(2,1)} %normalized_copies.1), calls=%async_computation | async-start | bytes 524288 | tf_op jit(solution)/shard_map/all_to_all | solution.py:148
  18.4 0.3 fusion.5
  18.8 17.9 %while.10 = (s32[]{:T(128)}, f32[16,4096]{1,0:T(8,128)S(1)}, s32[]{:T(128)}, s32[]{:T(128)}) while((s32[]{:T(128)}, f32[16,4096]{1,0:T(8,128)S(1)}, s32[]{:T(128)}, s32[]{:T(128)}) %tuple.26), condition=%wide.region_2.3_spmd, body=%wide.region_1.2_spmd.sunk | while | flops 983042 | bytes 4063405 | solution.py:168
  18.8 3.1 %collective-permute-start = (bf16[16,4096]{1,0:T(8,128)(2,1)S(1)}, bf16[16,4096]{1,0:T(8,128)(2,1)S(1)}, u32[]{:S(2)}, u32[]{:S(2)}) collective-permute-start(bf16[16,4096]{1,0:T(8,128)(2,1)S(1)} %convert_element_type.91), channel_id=1, source_target_pairs={{0,1},{1,0},{2,3},{3,2},{4,5},{5,4},{6,7},{7,6},{8,9},{9,8},{10,11... | collective-permute-start | bytes 393224 | tf_op jit(solution)/shard_map/while/body/ppermute | solution.py:130
  21.9 1.0 %collective-permute-done = bf16[16,4096]{1,0:T(8,128)(2,1)S(1)} collective-permute-done((bf16[16,4096]{1,0:T(8,128)(2,1)S(1)}, bf16[16,4096]{1,0:T(8,128)(2,1)S(1)}, u32[]{:S(2)}, u32[]{:S(2)}) %collective-permute-start) | collective-permute-done | bytes 131104 | tf_op jit(solution)/shard_map/while/body/ppermute | solution.py:130
  22.9 3.1 %collective-permute-start.1 = (bf16[16,4096]{1,0:T(8,128)(2,1)S(1)}, bf16[16,4096]{1,0:T(8,128)(2,1)S(1)}, u32[]{:S(2)}, u32[]{:S(2)}) collective-permute-start(bf16[16,4096]{1,0:T(8,128)(2,1)S(1)} %fusion.18), channel_id=1, source_target_pairs={{0,2},{1,3},{2,0},{3,1},{4,6},{5,7},{6,4},{7,5},{8,10},{9,11},{10,... | collective-permute-start | bytes 393224 | tf_op jit(solution)/shard_map/while/body/ppermute | solution.py:130
  26.1 3.5 %collective-permute-done.1 = bf16[16,4096]{1,0:T(8,128)(2,1)S(1)} collective-permute-done((bf16[16,4096]{1,0:T(8,128)(2,1)S(1)}, bf16[16,4096]{1,0:T(8,128)(2,1)S(1)}, u32[]{:S(2)}, u32[]{:S(2)}) %collective-permute-start.1) | collective-permute-done | bytes 131104 | tf_op jit(solution)/shard_map/while/body/ppermute | solution.py:130
  29.6 4.4 %collective-permute-start.2 = (bf16[16,4096]{1,0:T(8,128)(2,1)S(1)}, bf16[16,4096]{1,0:T(8,128)(2,1)S(1)}, u32[]{:S(2)}, u32[]{:S(2)}) collective-permute-start(bf16[16,4096]{1,0:T(8,128)(2,1)S(1)} %fusion.19), channel_id=1, source_target_pairs={{0,6},{1,7},{2,4},{3,5},{4,2},{5,3},{6,0},{7,1},{8,14},{9,15},{10,... | collective-permute-start | bytes 393224 | tf_op jit(solution)/shard_map/while/body/ppermute | solution.py:130
  34.0 2.5 %collective-permute-done.2 = bf16[16,4096]{1,0:T(8,128)(2,1)S(1)} collective-permute-done((bf16[16,4096]{1,0:T(8,128)(2,1)S(1)}, bf16[16,4096]{1,0:T(8,128)(2,1)S(1)}, u32[]{:S(2)}, u32[]{:S(2)}) %collective-permute-start.2) | collective-permute-done | bytes 131104 | tf_op jit(solution)/shard_map/while/body/ppermute | solution.py:130
  37.0 4.6 %collective-permute-start.3 = (bf16[16,2,4096]{2,1,0:T(2,128)(2,1)S(1)}, bf16[16,2,4096]{2,1,0:T(2,128)(2,1)S(1)}, u32[]{:S(2)}, u32[]{:S(2)}) collective-permute-start(bf16[16,2,4096]{2,1,0:T(2,128)(2,1)S(1)} %all-to-all-done), channel_id=1, source_target_pairs={{0,24},{8,16},{16,8},{24,0},{32,56},{40,48},{48,40},{56,32},{64,88... | collective-permute-start | bytes 786440 | tf_op jit(solution)/shard_map/ppermute | solution.py:134
  41.7 1.9 %collective-permute-start.4 = (bf16[16,4096]{1,0:T(8,128)(2,1)S(1)}, bf16[16,4096]{1,0:T(8,128)(2,1)S(1)}, u32[]{:S(2)}, u32[]{:S(2)}) collective-permute-start(bf16[16,4096]{1,0:T(8,128)(2,1)S(1)} %multiply_convert_fusion.here_ref), channel_id=1, source_target_pairs={{0,8},{8,0},{16,24},{24,16},{32,40},{40,32},{48,56},{56,48},{64,72... | collective-permute-start | bytes 393224 | tf_op jit(solution)/shard_map/ppermute | solution.py:134
  43.8 0.3 copy.11
  44.3 0.3 copy.12
  44.6 3.1 %collective-permute-done.4.beside_ref = bf16[16,4096]{1,0:T(8,128)(2,1)S(1)} collective-permute-done((bf16[16,4096]{1,0:T(8,128)(2,1)S(1)}, bf16[16,4096]{1,0:T(8,128)(2,1)S(1)}, u32[]{:S(2)}, u32[]{:S(2)}) %collective-permute-start.4) | collective-permute-done | bytes 131104 | tf_op jit(solution)/shard_map/ppermute | solution.py:134
  47.9 0.9 %score.1 = (f32[32,32]{1,0:T(8,128)S(1)}, f32[32,32]{1,0:T(8,128)S(1)}, f32[32,2,32]{2,1,0:T(2,128)}) custom-call(bf16[16,4096]{1,0:T(8,128)(2,1)S(1)} %multiply_convert_fusion.here_ref, bf16[16,4096]{1,0:T(8,128)(2,1)S(1)} %collective-permute-done.4.beside_ref, bf16[32,4096]{1,0:T(8,128)(2,1)S(1)} %reshape.48.own_ref, bf16[32,4096]{1,0:T(8,128)(2,1)S(1)} %reshape.49.other_ref), custom_call_target="tpu_custom_call" | custom-call | tf_op jit(solution)/shard_map/score/pallas_call | solution.py:79
  48.8 13.7 %all-to-all-start.1 = ((f32[32,2,32]{2,1,0:T(2,128)}), f32[32,2,32]{2,1,0:T(2,128)S(1)}, u32[]{:S(2)}, u32[]{:S(2)}) async-start(f32[32,2,32]{2,1,0:T(2,128)} %get-tuple-element.43), calls=%async_computation.1 | async-start | bytes 65536 | tf_op jit(solution)/shard_map/all_to_all | solution.py:181
  63.0 1.9 %all-to-all-done.1.totals_ref = f32[32,2,32]{2,1,0:T(2,128)S(1)} async-done(((f32[32,2,32]{2,1,0:T(2,128)}), f32[32,2,32]{2,1,0:T(2,128)S(1)}, u32[]{:S(2)}, u32[]{:S(2)}) %all-to-all-start.1) | async-done | bytes 8224 | tf_op jit(solution)/shard_map/all_to_all | solution.py:181
  64.9 0.3 gradients.1
  65.2 14.5 %all_to_all.20 = bf16[16,16,512]{2,1,0:T(8,128)(2,1)S(1)} all-to-all(bf16[16,16,512]{2,1,0:T(8,128)(2,1)S(1)} %gradients.1), channel_id=1, replica_groups={{4,5,6,7,0,1,2,3,12,13,14,15,8,9,10,11},{20,21,22,23,16,17,18,19,28,29,..., dimensions={0} | all-to-all | bytes 524288 | tf_op jit(solution)/shard_map/all_to_all | solution.py:193
  79.8 7.4 %all_to_all.21 = bf16[8,16,512]{2,1,0:T(8,128)(2,1)S(1)} all-to-all(bf16[8,16,512]{2,1,0:T(8,128)(2,1)S(1)} %broadcast_in_dim.10), channel_id=1, replica_groups={{4,5,6,7,0,1,2,3},{12,13,14,15,8,9,10,11},{20,21,22,23,16,17,18,19},{28..., dimensions={0} | all-to-all | bytes 262144 | tf_op jit(solution)/shard_map/all_to_all | solution.py:22
  87.5 1.5 %convolution_convert_fusion = bf16[128,4096]{1,0:T(8,128)(2,1)} fusion(f32[16,4096]{1,0:T(8,128)S(1)} %bitcast.19, f32[16]{0:T(128)S(1)} %multiply_reduce_fusion, f32[16]{0:T(128)S(1)} %add_rsqrt_fusion, f32[16]{0:T(128)S(1)} %get-tuple-element.52, s32[128]{0:T(128)S(1)} %iota_add_fusion, s32[16]{0:T(128)S(1)} %multiply_reduce_fusion.2, ...), kind=kOutput, calls=%fused_computation.5 | convolution fusion | flops 17766400 | bytes 1573696 | tf_op jit(solution)/shard_map/dot_general | solution.py:201
  (32 shorter events, 2.0 us)
Async XLA Ops:
  0.0 18.4 %copy-start = (bf16[128,4096]{1,0:T(8,128)(2,1)S(1)}, bf16[128,4096]{1,0:T(8,128)(2,1)}, u32[]{:S(2)}) copy-start(bf16[128,4096]{1,0:T(8,128)(2,1)} %param.6) | copy-start | bytes 3145732
  0.7 0.7 copy-start.1
  2.3 34.7 %all-to-all-start = ((bf16[16,2,4096]{2,1,0:T(2,128)(2,1)}), bf16[16,2,4096]{2,1,0:T(2,128)(2,1)S(1)}, u32[]{:S(2)}, u32[]{:S(2)}) async-start(bf16[16,2,4096]{2,1,0:T(2,128)(2,1)} %normalized_copies.1), calls=%async_computation | async-start | bytes 524288 | tf_op jit(solution)/shard_map/all_to_all | solution.py:148
  18.8 24.9 %copy-start.2 = (s32[1024]{0:T(1024)S(1)}, s32[1024]{0:T(1024)}, u32[]{:S(2)}) copy-start(s32[1024]{0:T(1024)} %param.9) | copy-start | bytes 12292
  18.8 4.1 %collective-permute-start = (bf16[16,4096]{1,0:T(8,128)(2,1)S(1)}, bf16[16,4096]{1,0:T(8,128)(2,1)S(1)}, u32[]{:S(2)}, u32[]{:S(2)}) collective-permute-start(bf16[16,4096]{1,0:T(8,128)(2,1)S(1)} %convert_element_type.91), channel_id=1, source_target_pairs={{0,1},{1,0},{2,3},{3,2},{4,5},{5,4},{6,7},{7,6},{8,9},{9,8},{10,11... | collective-permute-start | bytes 393224 | tf_op jit(solution)/shard_map/while/body/ppermute | solution.py:130
  22.9 6.6 %collective-permute-start.1 = (bf16[16,4096]{1,0:T(8,128)(2,1)S(1)}, bf16[16,4096]{1,0:T(8,128)(2,1)S(1)}, u32[]{:S(2)}, u32[]{:S(2)}) collective-permute-start(bf16[16,4096]{1,0:T(8,128)(2,1)S(1)} %fusion.18), channel_id=1, source_target_pairs={{0,2},{1,3},{2,0},{3,1},{4,6},{5,7},{6,4},{7,5},{8,10},{9,11},{10,... | collective-permute-start | bytes 393224 | tf_op jit(solution)/shard_map/while/body/ppermute | solution.py:130
  29.6 6.9 %collective-permute-start.2 = (bf16[16,4096]{1,0:T(8,128)(2,1)S(1)}, bf16[16,4096]{1,0:T(8,128)(2,1)S(1)}, u32[]{:S(2)}, u32[]{:S(2)}) collective-permute-start(bf16[16,4096]{1,0:T(8,128)(2,1)S(1)} %fusion.19), channel_id=1, source_target_pairs={{0,6},{1,7},{2,4},{3,5},{4,2},{5,3},{6,0},{7,1},{8,14},{9,15},{10,... | collective-permute-start | bytes 393224 | tf_op jit(solution)/shard_map/while/body/ppermute | solution.py:130
  37.0 10.7 %collective-permute-start.3 = (bf16[16,2,4096]{2,1,0:T(2,128)(2,1)S(1)}, bf16[16,2,4096]{2,1,0:T(2,128)(2,1)S(1)}, u32[]{:S(2)}, u32[]{:S(2)}) collective-permute-start(bf16[16,2,4096]{2,1,0:T(2,128)(2,1)S(1)} %all-to-all-done), channel_id=1, source_target_pairs={{0,24},{8,16},{16,8},{24,0},{32,56},{40,48},{48,40},{56,32},{64,88... | collective-permute-start | bytes 786440 | tf_op jit(solution)/shard_map/ppermute | solution.py:134
  41.7 6.0 %collective-permute-start.4 = (bf16[16,4096]{1,0:T(8,128)(2,1)S(1)}, bf16[16,4096]{1,0:T(8,128)(2,1)S(1)}, u32[]{:S(2)}, u32[]{:S(2)}) collective-permute-start(bf16[16,4096]{1,0:T(8,128)(2,1)S(1)} %multiply_convert_fusion.here_ref), channel_id=1, source_target_pairs={{0,8},{8,0},{16,24},{24,16},{32,40},{40,32},{48,56},{56,48},{64,72... | collective-permute-start | bytes 393224 | tf_op jit(solution)/shard_map/ppermute | solution.py:134
  48.8 16.0 %all-to-all-start.1 = ((f32[32,2,32]{2,1,0:T(2,128)}), f32[32,2,32]{2,1,0:T(2,128)S(1)}, u32[]{:S(2)}, u32[]{:S(2)}) async-start(f32[32,2,32]{2,1,0:T(2,128)} %get-tuple-element.43), calls=%async_computation.1 | async-start | bytes 65536 | tf_op jit(solution)/shard_map/all_to_all | solution.py:181
